TPU v7x, 32 devices: a whole 2x2x4 slice. The times are simulated.
32 devices in a mesh: lon: 16 (over z, y, core), lat: 2 (over x).
Axes of the slice: x: 2, y: 2, z: 4, core: 2. Of those that a mesh axis runs over, the one named last changes fastest.
Arguments:
- heat_content: float32 [16, 256, 2048], P(None, 'lat', 'lon'), may hold values from -18 to 18
- eastern_current: float32 [16, 256, 2048], P(None, 'lat', 'lon'), may hold values from -12 to 12
- northern_current: float32 [16, 256, 2048], P(None, 'lat', 'lon'), may hold values from -12 to 12
- mixing_coefficient: float32 [16, 256, 2048], P(None, 'lat', 'lon'), may hold values from 0.1 to 1
- friction_coefficient: float32 [256, 2048], P('lat', 'lon'), may hold values from 0.05 to 0.5
- water_indicator: int32 [256, 2048], P('lat', 'lon'), may hold values from 0 to 1
- flooded_strata: int32 [256, 2048], P('lat', 'lon'), may hold values from 12 to 16
Outputs:
- temp_next: float32 [16, 256, 2048], P(None, 'lat', 'lon')
- u_next: float32 [16, 256, 2048], P(None, 'lat', 'lon')
- v_next: float32 [16, 256, 2048], P(None, 'lat', 'lon')
All inputs are finite; a program needn't handle non-finite values.
Results may differ from a plain program's by a relative error of at most 0.0003.
Values sent between devices are 32-bit elements; how exact they have to be, the bound alone decides.
No kernel may reach another device: no remote copies, remote signals or barrier semaphores. Data moves between devices by JAX's collectives and lax.ppermute only.
A program may use at most 128 MiB of HBM per device.

v0:
```python
import jax
import jax.numpy as jnp
from jax import lax
from jax.sharding import PartitionSpec as P

DT = 0.25
GRAV = 0.1


def extended_2(x, sides, width, wrap):
    for axis, dim in sides:
        peers, length = (lax.axis_size(axis), x.shape[dim])
        up = [(i, (i + 1) % peers) for i in range(peers if wrap else peers - 1)]
        down = [(j, i) for i, j in up]
        last = lax.slice_in_dim(x, length - width, length, axis=dim)
        first = lax.slice_in_dim(x, 0, width, axis=dim)
        before = lax.ppermute(last, axis, up)
        after = lax.ppermute(first, axis, down)
        x = jnp.concatenate([before, x, after], axis=dim)
    return x


def partner(block, axis, stride):
    count = lax.axis_size(axis)
    route = []
    for low in range(count):
        high = low | 1 << stride
        if high != low and high < count:
            route += [(low, high), (high, low)]
    return lax.ppermute(block, axis, route)


def wet_mask(stratum_plane, stratum_number):
    level_index = jnp.arange(stratum_number, dtype=jnp.float32)[:, None, None]
    return (level_index < stratum_plane[None]).astype(jnp.float32)


def neighbours(field):
    return (
        field[:, 1:-1, 1:-1],
        field[:, 1:-1, 2:],
        field[:, 1:-1, :-2],
        field[:, 2:, 1:-1],
        field[:, :-2, 1:-1],
    )


def tracer_step(tracer, u_field, v_field, diffus, wetness):
    t_mid, t_east, t_west, t_north, t_south = neighbours(tracer)
    u_mid, u_east, u_west, u_north, u_south = neighbours(u_field)
    v_mid, v_east, v_west, v_north, v_south = neighbours(v_field)
    k_mid, k_east, k_west, k_north, k_south = neighbours(diffus)
    w_mid, w_east, w_west, w_north, w_south = neighbours(wetness)
    flux_east = (
        w_mid
        * w_east
        * (0.25 * (u_mid + u_east) * (t_mid + t_east) - 0.5 * (k_mid + k_east) * (t_east - t_mid))
    )
    flux_west = (
        w_mid
        * w_west
        * (0.25 * (u_west + u_mid) * (t_west + t_mid) - 0.5 * (k_west + k_mid) * (t_mid - t_west))
    )
    flux_north = (
        w_mid
        * w_north
        * (
            0.25 * (v_mid + v_north) * (t_mid + t_north)
            - 0.5 * (k_mid + k_north) * (t_north - t_mid)
        )
    )
    flux_south = (
        w_mid
        * w_south
        * (
            0.25 * (v_south + v_mid) * (t_south + t_mid)
            - 0.5 * (k_south + k_mid) * (t_mid - t_south)
        )
    )
    flux_up = w_mid[1:] * w_mid[:-1] * 0.5 * (k_mid[1:] + k_mid[:-1]) * (t_mid[1:] - t_mid[:-1])
    zero_level = jnp.zeros_like(t_mid[:1])
    vertical = jnp.concatenate([flux_up, zero_level], 0) - jnp.concatenate([zero_level, flux_up], 0)
    return w_mid * (t_mid + DT * (flux_west - flux_east + flux_south - flux_north + vertical))


def laplace(field, wetness):
    f_mid, f_east, f_west, f_north, f_south = neighbours(field)
    w_mid, w_east, w_west, w_north, w_south = neighbours(wetness)
    return w_mid * (
        w_east * (f_east - f_mid)
        + w_west * (f_west - f_mid)
        + w_north * (f_north - f_mid)
        + w_south * (f_south - f_mid)
    )


def momentum_step(u_field, v_field, pressure, wetness, friction_coefficient, coriolis):
    p_mid, p_east, p_west, p_north, p_south = neighbours(pressure)
    w_mid = wetness[:, 1:-1, 1:-1]
    u_mid = u_field[:, 1:-1, 1:-1]
    v_mid = v_field[:, 1:-1, 1:-1]
    u_new = w_mid * (
        u_mid
        + DT
        * (
            coriolis * v_mid
            - GRAV * 0.5 * (p_east - p_west)
            + friction_coefficient * laplace(u_field, wetness)
        )
    )
    v_new = w_mid * (
        v_mid
        + DT
        * (
            -coriolis * u_mid
            - GRAV * 0.5 * (p_north - p_south)
            + friction_coefficient * laplace(v_field, wetness)
        )
    )
    return (u_new, v_new)


def extend(layered_fields, margin, plane_signs):
    parallel_summed = layered_fields.shape[1]
    lon_wide = extended_2(layered_fields, (("lon", 2),), margin, True)
    both_wide = extended_2(lon_wide, (("lat", 1),), margin, False)
    mirror = both_wide[:, parallel_summed : parallel_summed + margin, :]
    for bit_index in range(lax.axis_size("lon").bit_length() - 1):
        mirror = partner(mirror, "lon", bit_index)
    mirror = mirror[:, ::-1, ::-1]
    mirror = mirror * plane_signs[:, None, None]
    is_top = lax.axis_index("lat") == lax.axis_size("lat") - 1
    north_rows = jnp.where(is_top, mirror, both_wide[:, parallel_summed + margin :, :])
    return jnp.concatenate([both_wide[:, : parallel_summed + margin, :], north_rows], 1)


def on_device(
    heat_content,
    eastern_current,
    northern_current,
    mixing_coefficient,
    friction_coefficient,
    water_indicator,
    flooded_strata,
):
    stratum_number, parallel_summed, stack_summed = heat_content.shape
    stratum_plane = (water_indicator * flooded_strata).astype(jnp.float32)[None]
    layered_fields = jnp.concatenate(
        [heat_content, eastern_current, northern_current, mixing_coefficient, stratum_plane], 0
    )
    plane_signs = jnp.concatenate(
        [
            jnp.ones((stratum_number,), jnp.float32),
            -jnp.ones((2 * stratum_number,), jnp.float32),
            jnp.ones((stratum_number + 1,), jnp.float32),
        ]
    )
    lat_start = (lax.axis_index("lat") * parallel_summed).astype(jnp.float32)
    row_global = jnp.arange(parallel_summed, dtype=jnp.float32) + lat_start
    coriolis = jnp.sin(
        jnp.pi * ((row_global + 0.5) / (parallel_summed * lax.axis_size("lat")) - 0.5)
    )[:, None]
    extended = extend(layered_fields, 1, plane_signs)
    scalar_bordered = extended[:stratum_number]
    u_wide = extended[stratum_number : 2 * stratum_number]
    v_wide = extended[2 * stratum_number : 3 * stratum_number]
    k_wide = extended[3 * stratum_number : 4 * stratum_number]
    wetness = wet_mask(extended[4 * stratum_number], stratum_number)
    temp_next = tracer_step(scalar_bordered, u_wide, v_wide, k_wide, wetness)
    pressure = jnp.cumsum(temp_next, axis=0)
    p_wide = extend(pressure, 1, jnp.ones((stratum_number,), jnp.float32))
    u_next, v_next = momentum_step(u_wide, v_wide, p_wide, wetness, friction_coefficient, coriolis)
    return (temp_next, u_next, v_next)


def solution(mesh):
    return jax.shard_map(
        on_device,
        mesh=mesh,
        in_specs=(
            P(None, "lat", "lon"),
            P(None, "lat", "lon"),
            P(None, "lat", "lon"),
            P(None, "lat", "lon"),
            P("lat", "lon"),
            P("lat", "lon"),
            P("lat", "lon"),
        ),
        out_specs=(P(None, "lat", "lon"), P(None, "lat", "lon"), P(None, "lat", "lon")),
        check_vma=False,
    )
```

profile of v0, /device:TPU:2, one launch (start us, length us, event | category | flops | bytes accessed | tf_op | source)
XLA Modules:
  0.0 110.7 jit_solution(3662313644760221066)
XLA Ops:
  0.7 1.4 %constant_dynamic-update-slice_fusion.3 = f32[65,128,128]{2,1,0:T(8,128)S(1)} fusion(f32[16,128,128]{2,1,0:T(8,128)} %param.7), kind=kLoop, calls=%fused_computation.105 | loop fusion | bytes 2097152
  3.7 4.9 %fusion.60 = (f32[65,128,1]{2,1,0:T(8,128)}, f32[65,128,1]{2,1,0:T(8,128)}) fusion(f32[65,128,128]{2,1,0:T(8,128)S(1)} %bitcast_dynamic-update-slice_fusion), kind=kLoop, calls=%fused_computation.108 | loop fusion | bytes 133120 | tf_op jit(solution)/shard_map/slice | solution.py:15
  8.6 2.9 %copy.10 = f32[65,128,1]{1,2,0:T(1,128)S(1)} copy(f32[65,128,1]{2,1,0:T(8,128)} %get-tuple-element.5) | data formatting | bytes 66560 | tf_op jit(solution)/shard_map/slice | solution.py:15
  11.6 2.9 %copy.11 = f32[65,128,1]{1,2,0:T(1,128)S(1)} copy(f32[65,128,1]{2,1,0:T(8,128)} %get-tuple-element.6) | data formatting | bytes 66560 | tf_op jit(solution)/shard_map/slice | solution.py:16
  14.5 4.5 %collective-permute-start.1 = (f32[65,128,1]{1,2,0:T(1,128)S(1)}, f32[65,128,1]{1,2,0:T(1,128)S(1)}, u32[]{:S(2)}, u32[]{:S(2)}) collective-permute-start(f32[65,128,1]{1,2,0:T(1,128)S(1)} %copy.11), channel_id=1, source_target_pairs={{2,0},{4,2},{6,4},{8,6},{10,8},{12,10},{14,12},{16,14},{18,16},{20... | collective-permute-start | bytes 99848 | tf_op jit(solution)/shard_map/ppermute | solution.py:18
  19.0 2.8 %copy.12 = f32[65,128,1]{2,1,0:T(8,128)} copy(f32[65,128,1]{1,2,0:T(1,128)S(1)} %collective-permute-done) | data formatting | bytes 66560 | tf_op jit(solution)/shard_map/ppermute | solution.py:17
  21.8 2.8 %copy.13 = f32[65,128,1]{2,1,0:T(8,128)} copy(f32[65,128,1]{1,2,0:T(1,128)S(1)} %collective-permute-done.1) | data formatting | bytes 66560 | tf_op jit(solution)/shard_map/ppermute | solution.py:18
  24.6 1.9 %pad_maximum_fusion.30 = (f32[65,1,130]{2,1,0:T(1,128)S(1)}, f32[65,1,130]{2,1,0:T(1,128)S(1)}) fusion(f32[65,128,1]{2,1,0:T(8,128)} %copy.13, f32[65,128,128]{2,1,0:T(8,128)} %copy-done, f32[65,128,1]{2,1,0:T(8,128)} %copy.12), kind=kLoop, calls=%fused_computation.96 | loop fusion | flops 33800 | bytes 4394000 | tf_op jit(solution)/shard_map/slice | solution.py:15
  27.8 4.3 %collective-permute-done.4 = f32[65,1,130]{2,1,0:T(1,128)S(1)} collective-permute-done((f32[65,1,130]{2,1,0:T(1,128)S(1)}, f32[65,1,130]{2,1,0:T(1,128)S(1)}, u32[]{:S(2)}, u32[]{:S(2)}) %collective-permute-start.4) | collective-permute-done | bytes 33832 | tf_op jit(solution)/shard_map/ppermute | solution.py:30
  32.1 4.3 %collective-permute-done.5 = f32[65,1,130]{2,1,0:T(1,128)S(1)} collective-permute-done((f32[65,1,130]{2,1,0:T(1,128)S(1)}, f32[65,1,130]{2,1,0:T(1,128)S(1)}, u32[]{:S(2)}, u32[]{:S(2)}) %collective-permute-start.5) | collective-permute-done | bytes 33832 | tf_op jit(solution)/shard_map/ppermute | solution.py:30
  37.1 2.4 %collective-permute-start.7 = (f32[65,1,130]{2,1,0:T(1,128)S(1)}, f32[65,1,130]{2,1,0:T(1,128)S(1)}, u32[]{:S(2)}, u32[]{:S(2)}) collective-permute-start(f32[65,1,130]{2,1,0:T(1,128)S(1)} %get-tuple-element.4), channel_id=1, source_target_pairs={{1,0},{3,2},{5,4},{7,6},{9,8},{11,10},{13,12},{15,14},{17,16},{19,... | collective-permute-start | bytes 101408 | tf_op jit(solution)/shard_map/ppermute | solution.py:18
  42.7 3.1 %collective-permute-done.2 = f32[65,1,130]{2,1,0:T(1,128)S(1)} collective-permute-done((f32[65,1,130]{2,1,0:T(1,128)S(1)}, f32[65,1,130]{2,1,0:T(1,128)S(1)}, u32[]{:S(2)}, u32[]{:S(2)}) %collective-permute-start.2) | collective-permute-done | bytes 33832 | tf_op jit(solution)/shard_map/ppermute | solution.py:17
  47.0 1.6 %fusion.57 = f32[15,128,128]{2,1,0:T(8,128)} fusion(f32[16,130,130]{2,1,0:T(8,128)S(1)} %fusion, f32[16,128,128]{2,1,0:T(8,128)S(1)} %copy-done.2, f32[16,128,128]{2,1,0:T(8,128)S(1)} %copy-done.4), kind=kLoop, calls=%fused_computation.87 | loop fusion | flops 1474560 | bytes 6881280 | tf_op jit(solution)/shard_map/mul | solution.py:80
  48.5 16.0 %fusion.40 = f32[16,128,128]{2,1,0:T(8,128)} fusion(f32[16,128,128]{2,1,0:T(8,128)} %param.7, f32[16,128,128]{2,1,0:T(8,128)} %param.10, f32[65,1,130]{2,1,0:T(1,128)S(1)} %broadcast_select_fusion, f32[65,128,1]{2,1,0:T(8,128)} %copy.13, f32[65,128,128]{2,1,0:T(8,128)S(1)} %bitcast.8, f32[65,128,1]{2,1,0:T(8,128)} %copy.12, ...), kind=kLoop, calls=%fused_computation.58 | loop fusion | flops 19922944 | bytes 15862800 | tf_op jit(solution)/shard_map/mul | solution.py:83
  65.8 1.7 %fusion.61 = (f32[16,128,1]{2,1,0:T(8,128)}, f32[16,128,1]{2,1,0:T(8,128)}) fusion(f32[16,128,128]{2,1,0:T(8,128)S(1)} %fusion.62), kind=kLoop, calls=%fused_computation.109 | loop fusion | bytes 32768 | tf_op jit(solution)/shard_map/slice | solution.py:16
  67.5 1.6 %copy.16 = f32[16,128,1]{1,0,2:T(8,128)S(1)} copy(f32[16,128,1]{2,1,0:T(8,128)} %get-tuple-element.9) | data formatting | bytes 16384 | tf_op jit(solution)/shard_map/slice | solution.py:16
  69.1 1.6 %copy.18 = f32[16,128,1]{1,0,2:T(8,128)S(1)} copy(f32[16,128,1]{2,1,0:T(8,128)} %get-tuple-element.10) | data formatting | bytes 16384 | tf_op jit(solution)/shard_map/slice | solution.py:15
  71.4 1.3 %copy.17 = f32[16,128,1]{2,1,0:T(8,128)} copy(f32[16,128,1]{1,0,2:T(8,128)S(1)} %collective-permute-done.8) | data formatting | bytes 16384 | tf_op jit(solution)/shard_map/ppermute | solution.py:18
  72.7 3.9 %collective-permute-done.9 = f32[16,128,1]{1,0,2:T(8,128)S(1)} collective-permute-done((f32[16,128,1]{1,0,2:T(8,128)S(1)}, f32[16,128,1]{1,0,2:T(8,128)S(1)}, u32[]{:S(2)}, u32[]{:S(2)}) %collective-permute-start.9) | collective-permute-done | bytes 8224 | tf_op jit(solution)/shard_map/ppermute | solution.py:17
  76.6 1.3 %copy.19 = f32[16,128,1]{2,1,0:T(8,128)} copy(f32[16,128,1]{1,0,2:T(8,128)S(1)} %collective-permute-done.9) | data formatting | bytes 16384 | tf_op jit(solution)/shard_map/ppermute | solution.py:17
  80.3 3.7 %collective-permute-done.11 = f32[16,1,130]{2,1,0:T(1,128)S(1)} collective-permute-done((f32[16,1,130]{2,1,0:T(1,128)S(1)}, f32[16,1,130]{2,1,0:T(1,128)S(1)}, u32[]{:S(2)}, u32[]{:S(2)}) %collective-permute-start.11) | collective-permute-done | bytes 8352 | tf_op jit(solution)/shard_map/ppermute | solution.py:30
  85.4 5.1 %collective-permute-start.14 = (f32[16,1,130]{2,1,0:T(1,128)S(1)}, f32[16,1,130]{2,1,0:T(1,128)S(1)}, u32[]{:S(2)}, u32[]{:S(2)}) collective-permute-start(f32[16,1,130]{2,1,0:T(1,128)S(1)} %get-tuple-element.7), channel_id=1, source_target_pairs={{1,0},{3,2},{5,4},{7,6},{9,8},{11,10},{13,12},{15,14},{17,16},{19,... | collective-permute-start | bytes 24968 | tf_op jit(solution)/shard_map/ppermute | solution.py:18
  90.7 8.7 %fusion.25 = f32[16,128,128]{2,1,0:T(8,128)} fusion(f32[16,128,128]{2,1,0:T(8,128)} %param.8, f32[65,1,130]{2,1,0:T(1,128)S(1)} %collective-permute-done.2, f32[65,128,1]{2,1,0:T(8,128)} %copy.13, f32[65,128,128]{2,1,0:T(8,128)} %copy-done, f32[65,128,1]{2,1,0:T(8,128)} %copy.12, f32[65,1,130]{2,1,0:T(1,128)S(1)} %broadcast_select_fusion, ...), kind=kLoop, calls=%fused_computation.35 | loop fusion | flops 8126464 | bytes 13913616 | tf_op jit(solution)/shard_map/mul | solution.py:102
  101.2 9.4 %fusion.11 = f32[16,128,128]{2,1,0:T(8,128)} fusion(f32[16,128,128]{2,1,0:T(8,128)} %param.9, f32[65,128,128]{2,1,0:T(8,128)} %copy-done, f32[65,128,1]{2,1,0:T(8,128)} %copy.12, f32[65,128,1]{2,1,0:T(8,128)} %copy.13, f32[16,1,130]{2,1,0:T(1,128)} %collective-permute-done.15, f32[16,128,1]{2,1,0:T(8,128)} %copy.17, f32[16,128,128]{2,1,0:T(8,128)S(1)} %fusion.62, ...), kind=kLoop, calls=%fused_computation.13 | loop fusion | flops 9175040 | bytes 13930256 | tf_op jit(solution)/shard_map/mul | solution.py:111
  (62 shorter events, 15.4 us)
Async XLA Ops:
  0.7 3.0 %copy-start.7 = (s32[128,128]{1,0:T(8,128)S(1)}, s32[128,128]{1,0:T(8,128)}, u32[]{:S(2)}) copy-start(s32[128,128]{1,0:T(8,128)} %param.13) | copy-start | bytes 196612
  3.7 4.9 %copy-start = (f32[65,128,128]{2,1,0:T(8,128)}, f32[65,128,128]{2,1,0:T(8,128)S(1)}, u32[]{:S(2)}) copy-start(f32[65,128,128]{2,1,0:T(8,128)S(1)} %bitcast_dynamic-update-slice_fusion) | copy-start | bytes 12779524
  11.5 7.5 %collective-permute-start = (f32[65,128,1]{1,2,0:T(1,128)S(1)}, f32[65,128,1]{1,2,0:T(1,128)S(1)}, u32[]{:S(2)}, u32[]{:S(2)}) collective-permute-start(f32[65,128,1]{1,2,0:T(1,128)S(1)} %copy.10), channel_id=1, source_target_pairs={{0,2},{2,4},{4,6},{6,8},{8,10},{10,12},{12,14},{14,16},{16,18},{18... | collective-permute-start | bytes 99848 | tf_op jit(solution)/shard_map/ppermute | solution.py:17
  14.5 7.3 %collective-permute-start.1 = (f32[65,128,1]{1,2,0:T(1,128)S(1)}, f32[65,128,1]{1,2,0:T(1,128)S(1)}, u32[]{:S(2)}, u32[]{:S(2)}) collective-permute-start(f32[65,128,1]{1,2,0:T(1,128)S(1)} %copy.11), channel_id=1, source_target_pairs={{2,0},{4,2},{6,4},{8,6},{10,8},{12,10},{14,12},{16,14},{18,16},{20... | collective-permute-start | bytes 99848 | tf_op jit(solution)/shard_map/ppermute | solution.py:18
  24.6 17.8 %copy-start.9 = (f32[65]{0:T(128)S(1)}, f32[65]{0:T(128)}, u32[]{:S(2)}) copy-start(f32[65]{0:T(128)} %constant.13.clone.1) | copy-start | bytes 784
  24.6 23.9 %slice-start = ((s8[4259840]{0:T(1024)(128)(4,1)}), s8[65536]{0:T(1024)(128)(4,1)S(1)}, s32[]{:S(2)}) async-start(s8[4259840]{0:T(1024)(128)(4,1)} %bitcast.7), calls=%async_computation | async-start | bytes 131072
  26.5 1.3 %collective-permute-start.3 = (f32[65,1,130]{2,1,0:T(1,128)S(1)}, f32[65,1,130]{2,1,0:T(1,128)S(1)}, u32[]{:S(2)}, u32[]{:S(2)}) collective-permute-start(f32[65,1,130]{2,1,0:T(1,128)S(1)} %get-tuple-element.3), channel_id=1, source_target_pairs={{0,2},{2,0},{4,6},{6,4},{8,10},{10,8},{12,14},{14,12},{16,18},{18,... | collective-permute-start | bytes 101408 | tf_op jit(solution)/shard_map/ppermute | solution.py:30
  27.8 4.3 %collective-permute-start.4 = (f32[65,1,130]{2,1,0:T(1,128)S(1)}, f32[65,1,130]{2,1,0:T(1,128)S(1)}, u32[]{:S(2)}, u32[]{:S(2)}) collective-permute-start(f32[65,1,130]{2,1,0:T(1,128)S(1)} %collective-permute-done.3), channel_id=1, source_target_pairs={{0,4},{4,0},{2,6},{6,2},{8,12},{12,8},{10,14},{14,10},{16,20},{20,... | collective-permute-start | bytes 101408 | tf_op jit(solution)/shard_map/ppermute | solution.py:30
  32.1 4.3 %collective-permute-start.5 = (f32[65,1,130]{2,1,0:T(1,128)S(1)}, f32[65,1,130]{2,1,0:T(1,128)S(1)}, u32[]{:S(2)}, u32[]{:S(2)}) collective-permute-start(f32[65,1,130]{2,1,0:T(1,128)S(1)} %collective-permute-done.4), channel_id=1, source_target_pairs={{0,8},{8,0},{2,10},{10,2},{4,12},{12,4},{6,14},{14,6},{16,24},{24,... | collective-permute-start | bytes 101408 | tf_op jit(solution)/shard_map/ppermute | solution.py:30
  36.4 5.3 %collective-permute-start.6 = (f32[65,1,130]{2,1,0:T(1,128)S(1)}, f32[65,1,130]{2,1,0:T(1,128)S(1)}, u32[]{:S(2)}, u32[]{:S(2)}) collective-permute-start(f32[65,1,130]{2,1,0:T(1,128)S(1)} %collective-permute-done.5), channel_id=1, source_target_pairs={{0,16},{16,0},{2,18},{18,2},{4,20},{20,4},{6,22},{22,6},{8,24},{24... | collective-permute-start | bytes 101408 | tf_op jit(solution)/shard_map/ppermute | solution.py:30
  37.1 5.2 %collective-permute-start.7 = (f32[65,1,130]{2,1,0:T(1,128)S(1)}, f32[65,1,130]{2,1,0:T(1,128)S(1)}, u32[]{:S(2)}, u32[]{:S(2)}) collective-permute-start(f32[65,1,130]{2,1,0:T(1,128)S(1)} %get-tuple-element.4), channel_id=1, source_target_pairs={{1,0},{3,2},{5,4},{7,6},{9,8},{11,10},{13,12},{15,14},{17,16},{19,... | collective-permute-start | bytes 101408 | tf_op jit(solution)/shard_map/ppermute | solution.py:18
  39.6 6.2 %collective-permute-start.2 = (f32[65,1,130]{2,1,0:T(1,128)S(1)}, f32[65,1,130]{2,1,0:T(1,128)S(1)}, u32[]{:S(2)}, u32[]{:S(2)}) collective-permute-start(f32[65,1,130]{2,1,0:T(1,128)S(1)} %get-tuple-element.3), channel_id=1, source_target_pairs={{0,1},{2,3},{4,5},{6,7},{8,9},{10,11},{12,13},{14,15},{16,17},{18,... | collective-permute-start | bytes 101408 | tf_op jit(solution)/shard_map/ppermute | solution.py:17
  42.6 4.3 %copy-start.2 = (f32[16,128,128]{2,1,0:T(8,128)S(1)}, f32[16,128,128]{2,1,0:T(8,128)}, u32[]{:S(2)}) copy-start(f32[16,128,128]{2,1,0:T(8,128)} %param.7) | copy-start | bytes 3145732
  42.6 4.3 %copy-start.4 = (f32[16,128,128]{2,1,0:T(8,128)S(1)}, f32[16,128,128]{2,1,0:T(8,128)}, u32[]{:S(2)}) copy-start(f32[16,128,128]{2,1,0:T(8,128)} %param.10) | copy-start | bytes 3145732
  42.7 5.9 %slice-start.1 = ((s8[4259840]{0:T(1024)(128)(4,1)}), s8[4194304]{0:T(1024)(128)(4,1)S(1)}, s32[]{:S(2)}) async-start(s8[4259840]{0:T(1024)(128)(4,1)} %bitcast.7), calls=%async_computation.1 | async-start | bytes 8388608
  67.5 23.3 %copy-start.5 = (f32[128,128]{1,0:T(8,128)S(1)}, f32[128,128]{1,0:T(8,128)}, u32[]{:S(2)}) copy-start(f32[128,128]{1,0:T(8,128)} %param.11) | copy-start | bytes 196612
  69.1 2.3 %collective-permute-start.8 = (f32[16,128,1]{1,0,2:T(8,128)S(1)}, f32[16,128,1]{1,0,2:T(8,128)S(1)}, u32[]{:S(2)}, u32[]{:S(2)}) collective-permute-start(f32[16,128,1]{1,0,2:T(8,128)S(1)} %copy.16), channel_id=1, source_target_pairs={{2,0},{4,2},{6,4},{8,6},{10,8},{12,10},{14,12},{16,14},{18,16},{20... | collective-permute-start | bytes 24584 | tf_op jit(solution)/shard_map/ppermute | solution.py:18
  70.7 6.0 %collective-permute-start.9 = (f32[16,128,1]{1,0,2:T(8,128)S(1)}, f32[16,128,1]{1,0,2:T(8,128)S(1)}, u32[]{:S(2)}, u32[]{:S(2)}) collective-permute-start(f32[16,128,1]{1,0,2:T(8,128)S(1)} %copy.18), channel_id=1, source_target_pairs={{0,2},{2,4},{4,6},{6,8},{8,10},{10,12},{12,14},{14,16},{16,18},{18... | collective-permute-start | bytes 24584 | tf_op jit(solution)/shard_map/ppermute | solution.py:17
  79.1 1.2 %collective-permute-start.10 = (f32[16,1,130]{2,1,0:T(1,128)S(1)}, f32[16,1,130]{2,1,0:T(1,128)S(1)}, u32[]{:S(2)}, u32[]{:S(2)}) collective-permute-start(f32[16,1,130]{2,1,0:T(1,128)S(1)} %get-tuple-element.8), channel_id=1, source_target_pairs={{0,2},{2,0},{4,6},{6,4},{8,10},{10,8},{12,14},{14,12},{16,18},{18,... | collective-permute-start | bytes 24968 | tf_op jit(solution)/shard_map/ppermute | solution.py:30
  80.3 3.7 %collective-permute-start.11 = (f32[16,1,130]{2,1,0:T(1,128)S(1)}, f32[16,1,130]{2,1,0:T(1,128)S(1)}, u32[]{:S(2)}, u32[]{:S(2)}) collective-permute-start(f32[16,1,130]{2,1,0:T(1,128)S(1)} %collective-permute-done.10), channel_id=1, source_target_pairs={{0,4},{4,0},{2,6},{6,2},{8,12},{12,8},{10,14},{14,10},{16,20},{20,... | collective-permute-start | bytes 24968 | tf_op jit(solution)/shard_map/ppermute | solution.py:30
  84.1 6.5 %collective-permute-start.12 = (f32[16,1,130]{2,1,0:T(1,128)S(1)}, f32[16,1,130]{2,1,0:T(1,128)S(1)}, u32[]{:S(2)}, u32[]{:S(2)}) collective-permute-start(f32[16,1,130]{2,1,0:T(1,128)S(1)} %collective-permute-done.11), channel_id=1, source_target_pairs={{0,8},{8,0},{2,10},{10,2},{4,12},{12,4},{6,14},{14,6},{16,24},{24,... | collective-permute-start | bytes 24968 | tf_op jit(solution)/shard_map/ppermute | solution.py:30
  84.1 17.1 %collective-permute-start.15 = (f32[16,1,130]{2,1,0:T(1,128)S(1)}, f32[16,1,130]{2,1,0:T(1,128)}, u32[]{:S(2)}, u32[]{:S(2)}) collective-permute-start(f32[16,1,130]{2,1,0:T(1,128)S(1)} %get-tuple-element.8), channel_id=1, source_target_pairs={{0,1},{2,3},{4,5},{6,7},{8,9},{10,11},{12,13},{14,15},{16,17},{18,... | collective-permute-start | bytes 24968 | tf_op jit(solution)/shard_map/ppermute | solution.py:17
  85.4 15.6 %collective-permute-start.14 = (f32[16,1,130]{2,1,0:T(1,128)S(1)}, f32[16,1,130]{2,1,0:T(1,128)S(1)}, u32[]{:S(2)}, u32[]{:S(2)}) collective-permute-start(f32[16,1,130]{2,1,0:T(1,128)S(1)} %get-tuple-element.7), channel_id=1, source_target_pairs={{1,0},{3,2},{5,4},{7,6},{9,8},{11,10},{13,12},{15,14},{17,16},{19,... | collective-permute-start | bytes 24968 | tf_op jit(solution)/shard_map/ppermute | solution.py:18
  90.6 8.9 %collective-permute-start.13 = (f32[16,1,130]{2,1,0:T(1,128)S(1)}, f32[16,1,130]{2,1,0:T(1,128)S(1)}, u32[]{:S(2)}, u32[]{:S(2)}) collective-permute-start(f32[16,1,130]{2,1,0:T(1,128)S(1)} %collective-permute-done.12), channel_id=1, source_target_pairs={{0,16},{16,0},{2,18},{18,2},{4,20},{20,4},{6,22},{22,6},{8,24},{24... | collective-permute-start | bytes 24968 | tf_op jit(solution)/shard_map/ppermute | solution.py:30
  (4 other events, 9.3 us)
where the time goes:
time: 112 us; the launch traced here: 111 us
  other arithmetic  41.5 us (37%)
  local copies, waits for them, and re-layouts  29 us (26%)
  waiting for transfers between devices  22.5 us (20%)
  starting transfers between devices  16.5 us (15%)
  between operations  1.16 us (1%)
    mul x1, other arithmetic, tracer_step(): w_mid * (t_mid + DT * (flux_west - flux_east + flux_south - flux_north +...  16 us
    ppermute x8, waiting for transfers between devices, partner(): return lax.ppermute(block, axis, route)  15.5 us
    ppermute x4, starting transfers between devices, extended_2(): after = lax.ppermute(first, axis, down)  12.1 us
    mul x1, other arithmetic, momentum_step(): w_mid * (v_mid + DT * (-coriolis * u_mid - GRAV * 0.5 * (p_north - p_sout...  9.37 us
    slice x3, local copies, waits for them, and re-layouts, extended_2(): last = lax.slice_in_dim(x, length - width, length, axis=dim)  9.37 us
    mul x1, other arithmetic, momentum_step(): w_mid * (u_mid + DT * (coriolis * v_mid - GRAV * 0.5 * (p_east - p_west)...  8.72 us
    ppermute x4, waiting for transfers between devices, extended_2(): before = lax.ppermute(last, axis, up)  7.04 us
    slice x3, local copies, waits for them, and re-layouts, extended_2(): first = lax.slice_in_dim(x, 0, width, axis=dim)  6.18 us
  transfers between devices with their start and end apart: 16, of which 8 were waited for; matrix products, arithmetic and copies ran while one was open for 18% of the time, Pallas kernels for 0%

commit v1 on v0

v1 whole, which is shorter than its diff:
```python
import functools

import jax
import jax.numpy as jnp
from jax import lax
from jax.experimental import pallas as pl
from jax.experimental.pallas import tpu as pltpu
from jax.sharding import PartitionSpec as P

DT = 0.25
GRAV = 0.1
F32, BF16 = jnp.float32, jnp.bfloat16
PAD = 8
RIM = 128
TAIL = 112
CHUNK = 4


def lanes(x, by):
    by %= x.shape[1]
    return x if by == 0 else pltpu.roll(x, by, 1)


def sublanes(x, by):
    by %= x.shape[0]
    return x if by == 0 else pltpu.roll(x, by, 0)


def iota(shape, dim):
    return lax.broadcasted_iota(jnp.int32, shape, dim)


def halves(x):
    high = x.astype(BF16)
    return jnp.concatenate([high, (x - high.astype(F32)).astype(BF16)], 1)


def across(a, b):
    return lax.dot_general(a, b, (((1,), (1,)), ((), ())), preferred_element_type=F32)


def parity(axis):
    return lax.axis_index(axis) % 2 == 0


def pack_kernel(
    levels, t, u, v, kd, water_hbm, strata_hbm, friction_hbm,
    send_a, send_b, depth, drag, drag_ends, tv, uv, vv, kv,
    water, strata, ends, sem, plane_sem,
):
    rows, cols = depth.shape
    pieces, size = levels // CHUNK, CHUNK * rows
    planes = []
    for n, (src, dst) in enumerate(((water_hbm, water), (strata_hbm, strata), (friction_hbm, drag))):
        planes.append(pltpu.make_async_copy(src, dst, plane_sem.at[n]))
        planes[n].start()
    fields = ((t, tv), (kd, kv), (u, uv), (v, vv))
    for part in range(pieces):
        for f, (src, dst) in enumerate(fields):
            at = pl.ds(part * size, size)
            pltpu.make_async_copy(src.at[at], dst.at[at], sem.at[f, part]).start()

    shape = (8, 2 * cols)
    column = iota(shape, 1) & (cols - 1)
    chosen = (column == ((iota(shape, 0) + (cols - 2)) & (cols - 1))) & (iota(shape, 0) < 4)
    take = jnp.where(chosen, 1.0, 0.0).astype(BF16)

    for copy in planes:
        copy.wait()
    d = (water[...] * strata[...]).astype(F32)
    depth[...] = d
    drag[...] = DT * drag[...]
    drag_ends[...] = across(take, halves(drag[...]))
    d = across(take, halves(d))

    @pl.loop(0, pieces)
    def one_piece(part):
        at = pl.ds(pl.multiple_of(part * size, size), size)
        for f, (src, full) in enumerate(fields):
            pltpu.make_async_copy(src.at[at], full.at[at], sem.at[f, part]).wait()
            found = across(take, halves(full[at, :]))
            for n in range(CHUNK):
                to = pl.multiple_of(8 * (f * levels + part * CHUNK + n), 8)
                ends[pl.ds(to, 8), :] = found[:, n * cols : (n + 1) * cols]


    lon_even = parity("lon")
    for q, (f, near) in enumerate(
        ((0, True), (0, False), (1, True), (1, False), (2, True), (2, False), (3, True))
    ):
        east = ends[pl.ds(8 * levels * f + (1 if near else 0), levels, stride=8), :]
        west = ends[pl.ds(8 * levels * f + (2 if near else 3), levels, stride=8), :]
        at = pl.ds(q * levels, levels)
        send_a[at, :] = jnp.where(lon_even, east, west)
        send_b[at, :] = jnp.where(lon_even, west, east)
    tail = (RIM - TAIL, cols)
    sub = iota(tail, 0)

    def tail_of(near, far):
        near, far = (jnp.broadcast_to(d[r : r + 1], tail) for r in (near, far))
        return jnp.where(sub == 0, near, jnp.where(sub == 1, far, 0.0))

    east, west = tail_of(1, 0), tail_of(2, 3)
    send_a[pl.ds(TAIL, RIM - TAIL), :] = jnp.where(lon_even, east, west)
    send_b[pl.ds(TAIL, RIM - TAIL), :] = jnp.where(lon_even, west, east)


def shift_kernel(
    levels, t, u, v, kd, depth, tv, uv, vv, kv,
    tn, un, vn, kn, lat_a, lat_b, te, ke, ue, uw, ve, vw, coriolis, sem, row_sem, depth_sem,
):
    rows, cols = coriolis.shape
    copies = []
    lat_even = parity("lat")
    for side, message in enumerate((lat_a, lat_b)):
        north = lat_even if side == 0 else jnp.logical_not(lat_even)
        near = jnp.where(north, rows - 1, 0)
        far = jnp.where(north, rows - 2, 1)
        for q, (src, row) in enumerate(
            ((t, near), (t, far), (kd, near), (kd, far), (v, near), (v, far), (u, near))
        ):
            at = message.at[pl.ds(q * levels, levels)]
            copies.append(pltpu.make_async_copy(src.at[:, row], at, row_sem.at[side, q]))
        for n, row in enumerate((near, far)):
            at = message.at[pl.ds(TAIL + n, 1)]
            copies.append(pltpu.make_async_copy(depth.at[pl.ds(row, 1)], at, depth_sem.at[side, n]))
    for n, (src, dst) in enumerate(((t, tn), (v, vn), (kd, kn), (u, un))):
        here, north = pl.ds(0, rows - 1), pl.ds(1, rows - 1)
        copies.append(pltpu.make_async_copy(src.at[:, north], dst.at[:, here], sem.at[n]))
    for copy in copies:
        copy.start()

    row = iota((rows, cols), 0) + lax.axis_index("lat") * rows
    total = rows * lax.axis_size("lat")
    coriolis[...] = DT * jnp.sin(jnp.pi * ((row.astype(F32) + 0.5) / total - 0.5))
    shape = (2 * cols, 2 * cols)
    source, target = iota(shape, 0) & (cols - 1), iota(shape, 1)
    want = jnp.where(target < cols, target + 1, target - cols - 1)
    want = jnp.where(target == cols - 1, -1, want)
    both = jnp.where(source == want, 1.0, 0.0).astype(BF16)

    @pl.loop(0, levels)
    def one_level(k):
        at = pl.ds(pl.multiple_of(k * rows, rows), rows)
        for src, east in ((tv, te), (kv, ke)):
            east[at, :] = jnp.dot(halves(src[at, :]), both[:, :cols], preferred_element_type=F32)
        for src, east, west in ((uv, ue, uw), (vv, ve, vw)):
            moved = jnp.dot(halves(src[at, :]), both, preferred_element_type=F32)
            east[at, :] = moved[:, :cols]
            west[at, :] = moved[:, cols:]

    for copy in copies:
        copy.wait()


def corner_kernel(lat_a, lat_b, recv_a, recv_b, out_a, out_b):
    cols = recv_a.shape[1]
    lon_even, lat_even = parity("lon"), parity("lat")
    a, b = recv_a[...], recv_b[...]
    west, east = jnp.where(lon_even, b, a), jnp.where(lon_even, a, b)
    shape = (8, 2 * cols)
    lane, sub = iota(shape, 1) & (cols - 1), iota(shape, 0)
    chosen = ((sub == 0) & (lane == 0)) | ((sub == 1) & (lane == cols - 1))
    take = jnp.where(chosen, 1.0, 0.0).astype(BF16)
    west, east = across(take, halves(west)), across(take, halves(east))
    tail = (RIM - TAIL, cols)
    sub = iota(tail, 0)
    for n, (main, out) in enumerate(((lat_a, out_a), (lat_b, out_b))):
        north = lat_even if n == 0 else jnp.logical_not(lat_even)
        w = jnp.broadcast_to(jnp.where(north, west[1:2], west[0:1]), tail)
        e = jnp.broadcast_to(jnp.where(north, east[1:2], east[0:1]), tail)
        out[pl.ds(0, TAIL), :] = main[pl.ds(0, TAIL), :]
        end = jnp.where(sub == 2, w, jnp.where(sub == 3, e, 0.0))
        out[pl.ds(TAIL, RIM - TAIL), :] = jnp.where(sub < 2, main[pl.ds(TAIL, RIM - TAIL), :], end)


def inner_kernel(
    levels, strip, t, u, v, kd, tn, un, vn, kn, te, ke, ue, uw, ve, vw, depth, drag, coriolis,
    t_out, u_out, v_out,
    fn, gu, gv, back, de, dw, dn, dragn, p, up,
):
    rows, cols = depth.shape
    zero = jnp.zeros((PAD, cols), F32)
    for ref in (fn, gu, back):
        ref[pl.ds(0, PAD), :] = zero

    shape = (strip, cols)
    lane = iota(shape, 1)
    row = iota(shape, 0)
    starts = range(0, rows, strip)
    for r in starts:
        here = pl.ds(r, strip)
        d, f = depth[here, :], drag[here, :]
        de[here, :] = jnp.where(lane < cols - 1, jnp.minimum(d, lanes(d, -1)), 0.0)
        dw[here, :] = jnp.where(lane > 0, jnp.minimum(d, lanes(d, 1)), 0.0)
        if r + strip < rows:
            north = pl.ds(r + 1, strip)
            dn[here, :] = jnp.minimum(d, depth[north, :])
            dragn[here, :] = drag[north, :]
        else:
            dn[here, :] = jnp.where(row < strip - 1, jnp.minimum(d, sublanes(d, -1)), 0.0)
            dragn[here, :] = sublanes(f, -1)

    shape1 = (2 * cols, cols)
    source, target = iota(shape1, 0) & (cols - 1), iota(shape1, 1)
    slope_of = jnp.where(source == target + 1, 1.0, jnp.where(source == target - 1, -1.0, 0.0)).astype(BF16)

    up[...] = jnp.zeros(up.shape, F32)
    p[...] = jnp.zeros(p.shape, F32)

    @pl.loop(0, levels)
    def one_level(k):
        kf = k.astype(F32)
        base = pl.multiple_of(k * rows, rows)
        above = pl.multiple_of(jnp.minimum(k + 1, levels - 1) * rows, rows)
        for r in starts:
            here = pl.ds(base + r, strip)
            plane, padded, below = pl.ds(r, strip), pl.ds(PAD + r, strip), pl.ds(PAD + r - 1, strip)
            d = depth[plane, :]
            t0, u0, v0, k0 = t[here, :], u[here, :], v[here, :], kd[here, :]
            wet, wet_e, wet_n = d > kf, de[plane, :] > kf, dn[plane, :] > kf

            t1, u1, k1 = te[here, :], ue[here, :], ke[here, :]
            flux = 0.0625 * ((u0 + u1) * (t0 + t1)) - 0.125 * ((k0 + k1) * (t1 - t0))
            flux = jnp.where(wet_e, flux, 0.0)
            change = lanes(flux, 1) - flux
            wet_w = dw[plane, :] > kf
            lap_u = jnp.where(wet_e, u1 - u0, 0.0) + jnp.where(wet_w, uw[here, :] - u0, 0.0)
            lap_v = jnp.where(wet_e, ve[here, :] - v0, 0.0) + jnp.where(wet_w, vw[here, :] - v0, 0.0)

            t1, v1, k1 = tn[here, :], vn[here, :], kn[here, :]
            flux = 0.0625 * ((v0 + v1) * (t0 + t1)) - 0.125 * ((k0 + k1) * (t1 - t0))
            flux = jnp.where(wet_n, flux, 0.0)
            lap = jnp.where(wet_n, un[here, :] - u0, 0.0)
            lap2 = jnp.where(wet_n, v1 - v0, 0.0)
            fn[padded, :] = flux
            gu[padded, :] = lap
            gv[plane, :] = lap2
            change = change + (fn[below, :] - flux)
            lap_u = lap_u + (lap - gu[below, :])
            lap_v = lap_v + lap2

            higher = pl.ds(above + r, strip)
            rise = 0.125 * ((kd[higher, :] + k0) * (t[higher, :] - t0))
            rise = jnp.where(d > kf + 1.0, rise, 0.0)
            change = change + (rise - up[plane, :])
            up[plane, :] = rise

            t_next = jnp.where(wet, t0 + change, 0.0)
            t_out[here, :] = t_next
            p[padded, :] = p[padded, :] + t_next
            c, f = coriolis[plane, :], drag[plane, :]
            u_out[here, :] = u0 + (c * v0 + f * lap_u)
            v_out[here, :] = v0 + (f * lap_v - c * u0)
        middle = pl.ds(PAD, rows)
        back[middle, :] = 0.0125 * p[middle, :] - dragn[...] * gv[...]
        slope = jnp.dot(halves(p[middle, :]), slope_of, preferred_element_type=F32)
        for r in starts:
            plane, here = pl.ds(r, strip), pl.ds(base + r, strip)
            wet = depth[plane, :] > kf
            u_next = u_out[here, :] - 0.0125 * slope[r : r + strip]
            v_next = v_out[here, :] + back[pl.ds(PAD + r - 1, strip), :] - 0.0125 * p[pl.ds(PAD + r + 1, strip), :]
            u_out[here, :] = jnp.where(wet, u_next, 0.0)
            v_out[here, :] = jnp.where(wet, v_next, 0.0)


def border_kernel(
    levels, t_in, u_in, v_in,
    send_a, send_b, recv_a, recv_b, lat_a, lat_b, rim_a, rim_b, drag, drag_ends,
    t_out, u_out, v_out, tb, ub, vb, tr, ur, vr0, vr1, sem,
):
    rows, cols = drag.shape
    lon_even, lat_even = parity("lon"), parity("lat")
    is_top = lax.axis_index("lat") == lax.axis_size("lat") - 1

    def sides(even, a, b):
        a, b = a[...], b[...]
        return jnp.where(even, b, a), jnp.where(even, a, b)

    own_w, own_e = sides(lon_even, send_a, send_b)
    west, east = sides(lon_even, recv_a, recv_b)
    own_s, own_n = sides(lat_even, lat_a, lat_b)
    south, north = sides(lat_even, rim_a, rim_b)

    shape = (RIM, 2 * cols)
    unit = jnp.where((iota(shape, 1) & (cols - 1)) == iota(shape, 0), 1.0, 0.0).astype(BF16)
    tails = jnp.concatenate([south[TAIL:], north[TAIL:]], 0)
    ends = across(unit, halves(tails))
    sw, se = ends[:, 2:3], ends[:, 3:4]
    low, high = RIM - TAIL + 2, RIM - TAIL + 3
    nw, ne = ends[:, low : low + 1], ends[:, high : high + 1]
    line = iota((RIM, 1), 0)
    turn = jnp.where((line >= 4 * levels) & (line < 7 * levels), -1.0, 1.0)
    nw, ne = jnp.where(is_top, turn * ne, nw), jnp.where(is_top, turn * nw, ne)
    mirrored = turn * jnp.take_along_axis(north, cols - 1 - iota((RIM, cols), 1), axis=1)
    north = jnp.where(is_top, mirrored, north)

    four, half = (4 * levels, cols), 2 * levels

    def stack(q, blocks):
        return jnp.concatenate([x[q * levels : (q + 1) * levels] for x in blocks], 0)

    def lines(rows_of_one):
        return jnp.concatenate([jnp.broadcast_to(x, (levels, cols)) for x in rows_of_one], 0)

    outside, inside = (west, east, south, north), (own_w, own_e, own_s, own_n)
    t1, t2, k1, k2, n1, n2, s1 = (stack(q, outside) for q in range(7))
    t0, k0, n0, s0 = (stack(q, inside) for q in (0, 2, 4, 6))
    d1, d2 = (lines([x[TAIL + n : TAIL + n + 1] for x in outside]) for n in (0, 1))
    d0, d0b = (lines([x[TAIL + n : TAIL + n + 1] for x in inside]) for n in (0, 1))
    f0 = lines([drag_ends[2:3, :], drag_ends[1:2, :], drag[0:1, :], drag[rows - 1 : rows, :]])
    sub, lane = iota(four, 0), iota(four, 1)
    level_i = sub & (levels - 1)
    level = level_i.astype(F32)
    side = jnp.where((sub & levels) == 0, 1.0, -1.0)
    wet0, wet1 = level < d0, level < d1
    wet01, wet12 = level < jnp.minimum(d0, d1), level < jnp.minimum(d1, d2)

    def face(side, ua, ub, ta, tb, ka, kb):
        return side * (0.0625 * ((ua + ub) * (ta + tb))) - 0.125 * ((ka + kb) * (tb - ta))

    inward = jnp.where(wet01, face(side, n1, n0, t1, t0, k1, k0), 0.0)
    outer = jnp.where(wet12, face(side, n2, n1, t2, t1, k2, k1), 0.0)

    before, after = (sw, se, sw, nw), (nw, ne, se, ne)

    def beyond(x, at):
        lo, hi = (
            jnp.concatenate(
                [jnp.broadcast_to(c[n : n + m], (levels, 1)) for c, (n, m) in zip(cells, at)], 0
            )
            for cells in (before, after)
        )
        lo, hi = jnp.broadcast_to(lo, four), jnp.broadcast_to(hi, four)
        return jnp.where(lane == 0, lo, lanes(x, 1)), jnp.where(lane == cols - 1, hi, lanes(x, -1))

    t_w, t_e = beyond(t1, ((0, levels),) * 4)
    k_w, k_e = beyond(k1, ((2 * levels, levels),) * 4)
    s_w, s_e = beyond(s1, ((6 * levels, levels),) * 2 + ((4 * levels, levels),) * 2)
    d_w, d_e = beyond(d1, ((TAIL, 1),) * 4)
    flux_w = jnp.where(level < jnp.minimum(d_w, d1), face(1.0, s_w, s1, t_w, t1, k_w, k1), 0.0)
    flux_e = jnp.where(level < jnp.minimum(d1, d_e), face(1.0, s1, s_e, t1, t_e, k1, k_e), 0.0)
    rise = 0.125 * ((sublanes(k1, -1) + k1) * (sublanes(t1, -1) - t1))
    rise = jnp.where((level + 1.0 < d1) & (level_i < levels - 1), rise, 0.0)
    change = outer - inward + flux_w - flux_e + rise - sublanes(rise, 1)
    p1, dp0 = jnp.where(wet1, t1 + change, 0.0), inward
    step = 1
    while step < levels:
        p1 = p1 + jnp.where(level_i >= step, sublanes(p1, step), 0.0)
        dp0 = dp0 + jnp.where(level_i >= step, sublanes(dp0, step), 0.0)
        step *= 2
    dn = 0.0125 * (side * p1) + f0 * jnp.where(wet01, n1 - n0, 0.0)
    dn = jnp.where(wet0, dn, 0.0)
    dn2 = jnp.where(level < d0b, 0.0125 * (side * dp0), 0.0)
    slope = jnp.where(lane < cols - 1, lanes(dp0, -1), 0.0) - jnp.where(lane > 0, lanes(dp0, 1), 0.0)
    ds = f0 * jnp.where(wet01, s1 - s0, 0.0) - 0.0125 * slope
    ds = jnp.where(wet0, ds, 0.0)
    tr[...] = inward[half:]
    ur[...] = ds[half:]
    vr0[...] = dn[half:]
    vr1[...] = dn2[half:]

    columns = jnp.concatenate(
        [dn2[levels:half], dn[levels:half], dn[:levels], dn2[:levels],
         inward[levels:half], inward[:levels], ds[levels:half], ds[:levels]], 0,
    ).T
    shape = (2 * cols, 3 * cols)
    group, target = (iota(shape, 0) & (cols - 1)) >> 4, iota(shape, 1)
    want = jnp.full(shape, -1, jnp.int32)
    for g, at in enumerate(
        (2 * cols - 2, 2 * cols - 1, cols, cols + 1, cols - 1, 0, 3 * cols - 1, 2 * cols)
    ):
        want = jnp.where(group == g, at, want)
    place = jnp.where(target == want, 1.0, 0.0).astype(BF16)
    lane = iota((rows, cols), 1) & (levels - 1)

    tail = (8, cols)
    sub = iota(tail, 0)
    fields = ((t_in, t_out, tb), (u_in, u_out, ub), (v_in, v_out, vb))

    def copy_out(n, k):
        at = pl.ds(pl.multiple_of(k * rows, rows), rows)
        return pltpu.make_async_copy(fields[n][2].at[at], fields[n][1].at[at], sem.at[n, k])

    @pl.loop(0, levels)
    def one_level(k):
        base = pl.multiple_of(k * rows, rows)
        moved = jnp.dot(halves(jnp.where(lane == k, columns, 0.0)), place, preferred_element_type=F32)
        for n, (part, _, buf) in enumerate(fields):
            at = pl.ds(base, rows)
            buf[at, :] = part[at, :] + moved[:, n * cols : (n + 1) * cols]

            def row_of(ref, s):
                return jnp.broadcast_to(ref[pl.ds(s * levels + k, 1), :], tail)

            for s, (near, far, begin) in enumerate(((0, 1, 0), (7, 6, rows - 8))):
                add = jnp.where(sub == near, row_of((tr, ur, vr0)[n], s), 0.0)
                if n == 2:
                    add = jnp.where(sub == far, row_of(vr1, s), add)
                at = pl.ds(base + begin, 8)
                buf[at, :] = buf[at, :] + add
            copy_out(n, k).start()

    @pl.loop(0, levels)
    def finish(k):
        for n in range(3):
            copy_out(n, k).wait()


def on_device(t, u, v, kd, friction, water, strata):
    levels, rows, cols = t.shape
    lon_n, lat_n = lax.axis_size("lon"), lax.axis_size("lat")
    vmem = pl.BlockSpec(memory_space=pltpu.VMEM)
    hbm = pl.BlockSpec(memory_space=pltpu.HBM)
    params = pltpu.CompilerParams(vmem_limit_bytes=12 * 1024 * 1024)
    tall = levels * rows
    plane, message, stack = (rows, cols), (RIM, cols), (tall, cols)

    def in_hbm(*arrays):
        return [pltpu.with_memory_space_constraint(x, pltpu.HBM) for x in arrays]

    send_a, send_b, depth, drag, drag_ends, *fields = pl.pallas_call(
        functools.partial(pack_kernel, levels),
        out_shape=[pltpu.VMEM(s, F32) for s in (message, message, plane, plane, (8, cols)) + (stack,) * 4],
        in_specs=[hbm] * 7,
        out_specs=[vmem] * 9,
        scratch_shapes=[pltpu.VMEM(plane, jnp.int32)] * 2
        + [pltpu.VMEM((8 * 4 * levels, cols), F32)]
        + [pltpu.SemaphoreType.DMA((4, levels // CHUNK)), pltpu.SemaphoreType.DMA((3,))],
        compiler_params=params,
        name="pack",
    )(*in_hbm(*[x.reshape(stack) for x in (t, u, v, kd)], water, strata, friction))

    lon_pairs = [(i, i ^ 1) for i in range(lon_n)]
    lon_cross = [(i, (i + 1) % lon_n if i % 2 else (i - 1) % lon_n) for i in range(lon_n)]
    recv_a = lax.ppermute(send_a, "lon", lon_pairs)
    recv_b = lax.ppermute(send_b, "lon", lon_cross)

    *moved, lat_a, lat_b, te, ke, ue, uw, ve, vw, coriolis = pl.pallas_call(
        functools.partial(shift_kernel, levels),
        out_shape=[pltpu.VMEM((levels, rows, 1, cols), F32)] * 4 + [pltpu.VMEM((RIM, 1, cols), F32)] * 2
        + [pltpu.VMEM(stack, F32)] * 6 + [pltpu.VMEM(plane, F32)],
        in_specs=[hbm] * 4 + [vmem] * 5,
        out_specs=[vmem] * 13,
        scratch_shapes=[pltpu.SemaphoreType.DMA(x) for x in ((4,), (2, 7), (2, 2))],
        compiler_params=params,
        name="shift",
    )(*in_hbm(*[x.reshape(levels, rows, 1, cols) for x in (t, u, v, kd)]), depth.reshape(rows, 1, cols), *fields)
    moved = [x.reshape(stack) for x in moved]
    lat_a, lat_b = lat_a.reshape(message), lat_b.reshape(message)

    next_a, next_b = pl.pallas_call(
        corner_kernel,
        out_shape=[pltpu.VMEM(message, F32)] * 2,
        in_specs=[vmem] * 4,
        out_specs=[vmem] * 2,
        compiler_params=params,
        name="corners",
    )(lat_a, lat_b, recv_a, recv_b)
    lat_pairs = [(i, i ^ 1) for i in range(lat_n)]
    cross = []
    for m in range(lon_n):
        for i in range(1, lat_n - 1, 2):
            here, north = m * lat_n + i, m * lat_n + i + 1
            cross += [(here, north), (north, here)]
        cross.append((m * lat_n + lat_n - 1, (lon_n - 1 - m) * lat_n + lat_n - 1))
    rim_a = lax.ppermute(next_a, "lat", lat_pairs)
    rim_b = lax.ppermute(next_b, ("lon", "lat"), cross)

    padded = pltpu.VMEM((rows + 2 * PAD, cols), F32)
    flat = pltpu.VMEM(plane, F32)
    inner = pl.pallas_call(
        functools.partial(inner_kernel, levels, 32),
        out_shape=[pltpu.VMEM(stack, F32)] * 3,
        in_specs=[vmem] * 17,
        out_specs=[vmem] * 3,
        scratch_shapes=[padded, padded, flat, padded, flat, flat, flat, flat, padded, flat],
        compiler_params=params,
        cost_estimate=pl.CostEstimate(flops=100 * tall * cols, bytes_accessed=1 << 20, transcendentals=0),
        name="inner",
    )(*fields, *moved, te, ke, ue, uw, ve, vw, depth, drag, coriolis)

    rim_pair = pltpu.VMEM((2 * levels, cols), F32)
    outs = pl.pallas_call(
        functools.partial(border_kernel, levels),
        out_shape=[jax.ShapeDtypeStruct(stack, F32)] * 3,
        in_specs=[vmem] * 13,
        out_specs=[hbm] * 3,
        scratch_shapes=[pltpu.VMEM(stack, F32)] * 3
        + [rim_pair] * 4
        + [pltpu.SemaphoreType.DMA((3, levels))],
        compiler_params=params,
        name="border",
    )(*inner, send_a, send_b, recv_a, recv_b, lat_a, lat_b, rim_a, rim_b, drag, drag_ends)
    return tuple(x.reshape(levels, rows, cols) for x in outs)


def solution(mesh):
    stack, plane = P(None, "lat", "lon"), P("lat", "lon")
    return jax.shard_map(
        on_device,
        mesh=mesh,
        in_specs=(stack,) * 4 + (plane,) * 3,
        out_specs=(stack,) * 3,
        check_vma=False,
    )
```

time: 112 us -> 29.6 us (0.26)
  other arithmetic: 41.5 us -> 0 us
  local copies, waits for them, and re-layouts: 29 us -> 0 us
  waiting for transfers between devices: 22.5 us -> 0.01 us
  Pallas kernels: 0 us -> 19.5 us
  starting transfers between devices: 16.5 us -> 9.22 us
    mul x4 -> x0, other arithmetic: 35.6 us -> none  [the longest x1 16 us: tracer_step(): w_mid * (t_mid + DT * (flux_west - flux_east + flux_south - flux_north +...]
    ppermute x16 -> x4, waiting for transfers between devices: 22.5 us -> 0.01 us  [the longest x1 0.01 us: on_device(): recv_a = lax.ppermute(send_a, 'lon', lon_pairs)]
    pallas_call x0 -> x5, Pallas kernels: none -> 19.5 us  [the longest x1 5.43 us: on_device(): pl.pallas_call(functools.partial(pack_kernel, levels), out_shape=[pltpu.V...]
    slice x6 -> x0, local copies, waits for them, and re-layouts: 15.6 us -> none  [the longest x3 9.37 us: extended_2(): last = lax.slice_in_dim(x, length - width, length, axis=dim)]
    ppermute x4 -> x0, local copies, waits for them, and re-layouts: 8.28 us -> none  [the longest x2 4.15 us: extended_2(): after = lax.ppermute(first, axis, down)]
    ppermute x16 -> x4, starting transfers between devices: 16.5 us -> 9.22 us  [the longest x1 4.66 us: on_device(): recv_b = lax.ppermute(send_b, 'lon', lon_cross)]
    unnamed x30 -> x0, local copies, waits for them, and re-layouts: 5.16 us -> none
    slice x1 -> x0, other arithmetic: 1.88 us -> none  [extended_2(): last = lax.slice_in_dim(x, length - width, length, axis=dim)]
  transfers between devices with their start and end apart: 16 -> 4, of which waited for: 8 -> 0; matrix products, arithmetic and copies ran while one was open for 18% -> 0% of each run, Pallas kernels for 0% -> 31%
where the time goes in v1:
time: 29.6 us; the launch traced here: 29.4 us
  Pallas kernels  19.5 us (66%)
  starting transfers between devices  9.22 us (31%)
  between operations  0.69 us (2%)
    pallas_call x1, Pallas kernels, on_device(): pl.pallas_call(functools.partial(pack_kernel, levels), out_shape=[pltpu.V...  5.43 us
    pallas_call x1, Pallas kernels, on_device(): pl.pallas_call(functools.partial(inner_kernel, levels, 32), out_shape=[pl...  5.11 us
    pallas_call x1, Pallas kernels, on_device(): pl.pallas_call(functools.partial(border_kernel, levels), out_shape=[jax.S...  4.78 us
    ppermute x1, starting transfers between devices, on_device(): recv_b = lax.ppermute(send_b, 'lon', lon_cross)  4.66 us
    pallas_call x1, Pallas kernels, on_device(): pl.pallas_call(functools.partial(shift_kernel, levels), out_shape=[pltpu....  4.02 us
    ppermute x1, starting transfers between devices, on_device(): rim_b = lax.ppermute(next_b, ('lon', 'lat'), cross)  3.95 us
  transfers between devices with their start and end apart: 4, of which 0 were waited for; matrix products, arithmetic and copies ran while one was open for 0% of the time, Pallas kernels for 31%

profile of v1, /device:TPU:2, one launch (start us, length us, event | category | flops | bytes accessed | tf_op | source)
XLA Modules:
  0.0 29.4 jit_solution(10718278400195860523)
XLA Ops:
  0.6 5.4 %pack.1 = (f32[128,128]{1,0:T(8,128)S(1)}, f32[128,128]{1,0:T(8,128)S(1)}, f32[128,128]{1,0:T(8,128)S(1)}, f32[128,128]{1,0:T(8,128)S(1)}, f32[8,128]{1,0:T(8,12...) custom-call(f32[2048,128]{1,0:T(8,128)} %bitcast.27, ...), custom_call_target="tpu_custom_call" | custom-call | tf_op jit(solution)/shard_map/pack/pallas_call | solution.py:422
  6.1 0.1 collective-permute-start
  6.1 4.7 %collective-permute-start.1 = (f32[128,128]{1,0:T(8,128)S(1)}, f32[128,128]{1,0:T(8,128)S(1)}, u32[]{:S(2)}, u32[]{:S(2)}) collective-permute-start(f32[128,128]{1,0:T(8,128)S(1)} %get-tuple-element.54.send_b), channel_id=1, source_target_pairs={{0,30},{2,4},{4,2},{6,8},{8,6},{10,12},{12,10},{14,16},{16,14},{18... | collective-permute-start | bytes 196616 | tf_op jit(solution)/shard_map/ppermute | solution.py:437
  10.8 4.0 %shift.1 = (f32[16,128,1,128]{3,2,1,0:T(1,128)S(1)}, f32[16,128,1,128]{3,2,1,0:T(1,128)S(1)}, f32[16,128,1,128]{3,2,1,0:T(1,128)S(1)}, f32[16,128,1,128]{3,2,1,0...) custom-call(f32[16,128,1,128]{3,2,1,0:T(1,128)} %bitcast.28, ...), custom_call_target="tpu_custom_call" | custom-call | tf_op jit(solution)/shard_map/shift/pallas_call | solution.py:439
  14.8 0.0 collective-permute-done.recv_a
  14.8 0.0 collective-permute-done.1.recv_b
  14.9 0.2 corners.1
  15.0 0.5 %collective-permute-start.2 = (f32[128,128]{1,0:T(8,128)S(1)}, f32[128,128]{1,0:T(8,128)S(1)}, u32[]{:S(2)}, u32[]{:S(2)}) collective-permute-start(f32[128,128]{1,0:T(8,128)S(1)} %get-tuple-element.57), channel_id=1, source_target_pairs={{0,1},{1,0},{2,3},{3,2},{4,5},{5,4},{6,7},{7,6},{8,9},{9,8},{10,11... | collective-permute-start | bytes 196616 | tf_op jit(solution)/shard_map/ppermute | solution.py:467
  15.6 3.9 %collective-permute-start.3 = (f32[128,128]{1,0:T(8,128)S(1)}, f32[128,128]{1,0:T(8,128)S(1)}, u32[]{:S(2)}, u32[]{:S(2)}) collective-permute-start(f32[128,128]{1,0:T(8,128)S(1)} %get-tuple-element.58), channel_id=1, source_target_pairs={{1,31},{3,29},{5,27},{7,25},{9,23},{11,21},{13,19},{15,17},{17,15}... | collective-permute-start | bytes 196616 | tf_op jit(solution)/shard_map/ppermute | solution.py:468
  19.5 5.1 %inner.1 = (f32[2048,128]{1,0:T(8,128)S(1)}, f32[2048,128]{1,0:T(8,128)S(1)}, f32[2048,128]{1,0:T(8,128)S(1)}) custom-call(f32[2048,128]{1,0:T(8,128)S(1)} %get-tuple-element.33.tv.t, f32[2048,128]{1,0:T(8,128)S(1)} %get-tuple-element.34.uv.u, f32[2048,128]{1,0:T(8,128)S(1)} %get-tuple-element.35.vv.v, f32[2048,128]{1,0:T(8,128)S(1)} %get-tuple-element.36.kv.kd, ...), custom_call_target="tpu_custom_call" | custom-call | flops 26214400 | bytes 1048576 | tf_op jit(solution)/shard_map/inner/pallas_call | solution.py:472
  24.6 0.0 collective-permute-done.2.rim_a
  24.6 0.0 collective-permute-done.3.rim_b
  24.6 4.8 %border.1 = (f32[2048,128]{1,0:T(8,128)}, f32[2048,128]{1,0:T(8,128)}, f32[2048,128]{1,0:T(8,128)}) custom-call(f32[2048,128]{1,0:T(8,128)S(1)} %get-tuple-element.50.t_in, f32[2048,128]{1,0:T(8,128)S(1)} %get-tuple-element.51.u_in, f32[2048,128]{1,0:T(8,128)S(1)} %get-tuple-element.52.v_in, f32[128,128]{1,0:T(8,128)S(1)} %get-tuple-element.53.send_a, ...), custom_call_target="tpu_custom_call" | custom-call | tf_op jit(solution)/shard_map/border/pallas_call | solution.py:484
Async XLA Ops:
  6.1 8.8 %collective-permute-start = (f32[128,128]{1,0:T(8,128)S(1)}, f32[128,128]{1,0:T(8,128)S(1)}, u32[]{:S(2)}, u32[]{:S(2)}) collective-permute-start(f32[128,128]{1,0:T(8,128)S(1)} %get-tuple-element.53.send_a), channel_id=1, source_target_pairs={{0,2},{2,0},{4,6},{6,4},{8,10},{10,8},{12,14},{14,12},{16,18},{18,... | collective-permute-start | bytes 196616 | tf_op jit(solution)/shard_map/ppermute | solution.py:436
  6.1 8.7 %collective-permute-start.1 = (f32[128,128]{1,0:T(8,128)S(1)}, f32[128,128]{1,0:T(8,128)S(1)}, u32[]{:S(2)}, u32[]{:S(2)}) collective-permute-start(f32[128,128]{1,0:T(8,128)S(1)} %get-tuple-element.54.send_b), channel_id=1, source_target_pairs={{0,30},{2,4},{4,2},{6,8},{8,6},{10,12},{12,10},{14,16},{16,14},{18... | collective-permute-start | bytes 196616 | tf_op jit(solution)/shard_map/ppermute | solution.py:437
  15.0 9.6 %collective-permute-start.2 = (f32[128,128]{1,0:T(8,128)S(1)}, f32[128,128]{1,0:T(8,128)S(1)}, u32[]{:S(2)}, u32[]{:S(2)}) collective-permute-start(f32[128,128]{1,0:T(8,128)S(1)} %get-tuple-element.57), channel_id=1, source_target_pairs={{0,1},{1,0},{2,3},{3,2},{4,5},{5,4},{6,7},{7,6},{8,9},{9,8},{10,11... | collective-permute-start | bytes 196616 | tf_op jit(solution)/shard_map/ppermute | solution.py:467
  15.6 9.1 %collective-permute-start.3 = (f32[128,128]{1,0:T(8,128)S(1)}, f32[128,128]{1,0:T(8,128)S(1)}, u32[]{:S(2)}, u32[]{:S(2)}) collective-permute-start(f32[128,128]{1,0:T(8,128)S(1)} %get-tuple-element.58), channel_id=1, source_target_pairs={{1,31},{3,29},{5,27},{7,25},{9,23},{11,21},{13,19},{15,17},{17,15}... | collective-permute-start | bytes 196616 | tf_op jit(solution)/shard_map/ppermute | solution.py:468

commit v2 on v1

--- a/solution.py
+++ b/solution.py
@@ -14,6 +14,7 @@
 RIM = 128
 TAIL = 112
 CHUNK = 4
+STRIP = 32
 
 
 def lanes(x, by):
@@ -46,7 +47,7 @@
 def pack_kernel(
     levels, t, u, v, kd, water_hbm, strata_hbm, friction_hbm,
     send_a, send_b, depth, drag, drag_ends, tv, uv, vv, kv,
-    water, strata, ends, sem, plane_sem,
+    water, strata, gathered, ends, sem, plane_sem,
 ):
     rows, cols = depth.shape
     pieces, size = levels // CHUNK, CHUNK * rows
@@ -60,36 +61,45 @@
             at = pl.ds(part * size, size)
             pltpu.make_async_copy(src.at[at], dst.at[at], sem.at[f, part]).start()
 
-    shape = (8, 2 * cols)
-    column = iota(shape, 1) & (cols - 1)
-    chosen = (column == ((iota(shape, 0) + (cols - 2)) & (cols - 1))) & (iota(shape, 0) < 4)
-    take = jnp.where(chosen, 1.0, 0.0).astype(BF16)
-
+    lane = iota((STRIP, cols), 1)
+    edge = (lane < 2) | (lane >= cols - 2)
+    strips = [pl.ds(r, STRIP) for r in range(0, rows, STRIP)]
     for copy in planes:
         copy.wait()
-    d = (water[...] * strata[...]).astype(F32)
-    depth[...] = d
-    drag[...] = DT * drag[...]
-    drag_ends[...] = across(take, halves(drag[...]))
-    d = across(take, halves(d))
+    for at in strips:
+        d = (water[at, :] * strata[at, :]).astype(F32)
+        depth[at, :] = d
+        drag[at, :] = DT * drag[at, :]
+        gathered[2, at, :] = lanes(d, 2)
+        gathered[3, at, :] = lanes(drag[at, :], 2)
+        gathered[0, at, :] = jnp.zeros((STRIP, cols), F32)
+        gathered[1, at, :] = jnp.zeros((STRIP, cols), F32)
 
     @pl.loop(0, pieces)
     def one_piece(part):
-        at = pl.ds(pl.multiple_of(part * size, size), size)
+        begin = pl.multiple_of(part * size, size)
         for f, (src, full) in enumerate(fields):
-            pltpu.make_async_copy(src.at[at], full.at[at], sem.at[f, part]).wait()
-            found = across(take, halves(full[at, :]))
-            for n in range(CHUNK):
-                to = pl.multiple_of(8 * (f * levels + part * CHUNK + n), 8)
-                ends[pl.ds(to, 8), :] = found[:, n * cols : (n + 1) * cols]
-
+            pltpu.make_async_copy(src.at[pl.ds(begin, size)], full.at[pl.ds(begin, size)], sem.at[f, part]).wait()
+            for r in range(0, rows, STRIP):
+                acc = gathered[f // 2, pl.ds(r, STRIP), :]
+                for n in range(CHUNK):
+                    x = jnp.where(edge, full[pl.ds(begin + n * rows + r, STRIP), :], 0.0)
+                    to = 8 * (part * CHUNK + n) + 4 * (f % 2) + 2
+                    acc = acc + pltpu.roll(x, to & (cols - 1), 1)
+                gathered[f // 2, pl.ds(r, STRIP), :] = acc
+
+    for n in range(2):
+        ends[pl.ds(n * rows, rows), :] = gathered[n, :, :].T
+    d = gathered[2, :, :].T
+    drag_ends[...] = gathered[3, :, :].T[0:8]
 
     lon_even = parity("lon")
     for q, (f, near) in enumerate(
         ((0, True), (0, False), (1, True), (1, False), (2, True), (2, False), (3, True))
     ):
-        east = ends[pl.ds(8 * levels * f + (1 if near else 0), levels, stride=8), :]
-        west = ends[pl.ds(8 * levels * f + (2 if near else 3), levels, stride=8), :]
+        first = (f // 2) * rows + 4 * (f % 2)
+        east = ends[pl.ds(first + (1 if near else 0), levels, stride=8), :]
+        west = ends[pl.ds(first + (2 if near else 3), levels, stride=8), :]
         at = pl.ds(q * levels, levels)
         send_a[at, :] = jnp.where(lon_even, east, west)
         send_b[at, :] = jnp.where(lon_even, west, east)
@@ -133,21 +143,15 @@
     row = iota((rows, cols), 0) + lax.axis_index("lat") * rows
     total = rows * lax.axis_size("lat")
     coriolis[...] = DT * jnp.sin(jnp.pi * ((row.astype(F32) + 0.5) / total - 0.5))
-    shape = (2 * cols, 2 * cols)
-    source, target = iota(shape, 0) & (cols - 1), iota(shape, 1)
-    want = jnp.where(target < cols, target + 1, target - cols - 1)
-    want = jnp.where(target == cols - 1, -1, want)
-    both = jnp.where(source == want, 1.0, 0.0).astype(BF16)
 
     @pl.loop(0, levels)
     def one_level(k):
-        at = pl.ds(pl.multiple_of(k * rows, rows), rows)
-        for src, east in ((tv, te), (kv, ke)):
-            east[at, :] = jnp.dot(halves(src[at, :]), both[:, :cols], preferred_element_type=F32)
-        for src, east, west in ((uv, ue, uw), (vv, ve, vw)):
-            moved = jnp.dot(halves(src[at, :]), both, preferred_element_type=F32)
-            east[at, :] = moved[:, :cols]
-            west[at, :] = moved[:, cols:]
+        for r in range(0, rows, STRIP):
+            at = pl.ds(pl.multiple_of(k * rows, rows) + r, STRIP)
+            for src, east in ((tv, te), (kv, ke), (uv, ue), (vv, ve)):
+                east[at, :] = lanes(src[at, :], -1)
+            for src, west in ((uv, uw), (vv, vw)):
+                west[at, :] = lanes(src[at, :], 1)
 
     for copy in copies:
         copy.wait()
@@ -201,10 +205,6 @@
             dn[here, :] = jnp.where(row < strip - 1, jnp.minimum(d, sublanes(d, -1)), 0.0)
             dragn[here, :] = sublanes(f, -1)
 
-    shape1 = (2 * cols, cols)
-    source, target = iota(shape1, 0) & (cols - 1), iota(shape1, 1)
-    slope_of = jnp.where(source == target + 1, 1.0, jnp.where(source == target - 1, -1.0, 0.0)).astype(BF16)
-
     up[...] = jnp.zeros(up.shape, F32)
     p[...] = jnp.zeros(p.shape, F32)
 
@@ -254,11 +254,12 @@
             v_out[here, :] = v0 + (f * lap_v - c * u0)
         middle = pl.ds(PAD, rows)
         back[middle, :] = 0.0125 * p[middle, :] - dragn[...] * gv[...]
-        slope = jnp.dot(halves(p[middle, :]), slope_of, preferred_element_type=F32)
         for r in starts:
             plane, here = pl.ds(r, strip), pl.ds(base + r, strip)
             wet = depth[plane, :] > kf
-            u_next = u_out[here, :] - 0.0125 * slope[r : r + strip]
+            mid = p[pl.ds(PAD + r, strip), :]
+            slope = jnp.where(lane < cols - 1, lanes(mid, -1), 0.0) - jnp.where(lane > 0, lanes(mid, 1), 0.0)
+            u_next = u_out[here, :] - 0.0125 * slope
             v_next = v_out[here, :] + back[pl.ds(PAD + r - 1, strip), :] - 0.0125 * p[pl.ds(PAD + r + 1, strip), :]
             u_out[here, :] = jnp.where(wet, u_next, 0.0)
             v_out[here, :] = jnp.where(wet, v_next, 0.0)
@@ -266,21 +267,29 @@
 
 def border_kernel(
     levels, t_in, u_in, v_in,
-    send_a, send_b, recv_a, recv_b, lat_a, lat_b, rim_a, rim_b, drag, drag_ends,
-    t_out, u_out, v_out, tb, ub, vb, tr, ur, vr0, vr1, sem,
+    send_a, send_b, recv_a, recv_b, lat_a, lat_b, rim_a, gathered, drag, drag_ends,
+    t_out, u_out, v_out, tb, ub, vb, tr, ur, vr0, vr1, turned, rim_b, sem, rim_sem,
 ):
     rows, cols = drag.shape
     lon_even, lat_even = parity("lon"), parity("lat")
-    is_top = lax.axis_index("lat") == lax.axis_size("lat") - 1
+    lat = lax.axis_index("lat")
+    is_top, is_bottom = lat == lax.axis_size("lat") - 1, lat == 0
 
     def sides(even, a, b):
         a, b = a[...], b[...]
         return jnp.where(even, b, a), jnp.where(even, a, b)
+
+    west_half = lax.axis_index("lon") < lax.axis_size("lon") // 2
+    first_of_pair = jnp.where(is_top | is_bottom, west_half, jnp.logical_not(lat_even))
+    fetch = pltpu.make_async_copy(gathered.at[jnp.where(first_of_pair, 1, 0)], rim_b, rim_sem)
+    fetch.start()
+    fetch.wait()
 
     own_w, own_e = sides(lon_even, send_a, send_b)
     west, east = sides(lon_even, recv_a, recv_b)
     own_s, own_n = sides(lat_even, lat_a, lat_b)
     south, north = sides(lat_even, rim_a, rim_b)
+    south = jnp.where(is_bottom, 0.0, south)
 
     shape = (RIM, 2 * cols)
     unit = jnp.where((iota(shape, 1) & (cols - 1)) == iota(shape, 0), 1.0, 0.0).astype(BF16)
@@ -360,19 +369,15 @@
     vr0[...] = dn[half:]
     vr1[...] = dn2[half:]
 
-    columns = jnp.concatenate(
-        [dn2[levels:half], dn[levels:half], dn[:levels], dn2[:levels],
-         inward[levels:half], inward[:levels], ds[levels:half], ds[:levels]], 0,
-    ).T
-    shape = (2 * cols, 3 * cols)
-    group, target = (iota(shape, 0) & (cols - 1)) >> 4, iota(shape, 1)
-    want = jnp.full(shape, -1, jnp.int32)
-    for g, at in enumerate(
-        (2 * cols - 2, 2 * cols - 1, cols, cols + 1, cols - 1, 0, 3 * cols - 1, 2 * cols)
+    for g, x in enumerate(
+        (dn2[levels:half], dn[levels:half], dn[:levels], dn2[:levels],
+         inward[levels:half], inward[:levels], ds[levels:half], ds[:levels])
     ):
-        want = jnp.where(group == g, at, want)
-    place = jnp.where(target == want, 1.0, 0.0).astype(BF16)
-    lane = iota((rows, cols), 1) & (levels - 1)
+        turned[pl.ds(g, levels, stride=8), :] = x
+    turned[...] = turned[...].T
+    lane = iota((STRIP, cols), 1)
+    one, wide = (lane < 1) | (lane >= cols - 1), (lane < 2) | (lane >= cols - 2)
+    spots = ((one, cols - 1 - 4), (wide, cols - 2), (one, cols - 1 - 6))
 
     tail = (8, cols)
     sub = iota(tail, 0)
@@ -385,10 +390,13 @@
     @pl.loop(0, levels)
     def one_level(k):
         base = pl.multiple_of(k * rows, rows)
-        moved = jnp.dot(halves(jnp.where(lane == k, columns, 0.0)), place, preferred_element_type=F32)
         for n, (part, _, buf) in enumerate(fields):
-            at = pl.ds(base, rows)
-            buf[at, :] = part[at, :] + moved[:, n * cols : (n + 1) * cols]
+            mask, to = spots[n]
+            by = (to - 8 * k) & (cols - 1)
+            for r in range(0, rows, STRIP):
+                at = pl.ds(base + r, STRIP)
+                moved = pltpu.roll(turned[pl.ds(r, STRIP), :], by, 1)
+                buf[at, :] = part[at, :] + jnp.where(mask, moved, 0.0)
 
             def row_of(ref, s):
                 return jnp.broadcast_to(ref[pl.ds(s * levels + k, 1), :], tail)
@@ -425,7 +433,7 @@
         in_specs=[hbm] * 7,
         out_specs=[vmem] * 9,
         scratch_shapes=[pltpu.VMEM(plane, jnp.int32)] * 2
-        + [pltpu.VMEM((8 * 4 * levels, cols), F32)]
+        + [pltpu.VMEM((4, rows, cols), F32), pltpu.VMEM((2 * rows, cols), F32)]
         + [pltpu.SemaphoreType.DMA((4, levels // CHUNK)), pltpu.SemaphoreType.DMA((3,))],
         compiler_params=params,
         name="pack",
@@ -458,14 +466,11 @@
         name="corners",
     )(lat_a, lat_b, recv_a, recv_b)
     lat_pairs = [(i, i ^ 1) for i in range(lat_n)]
-    cross = []
-    for m in range(lon_n):
-        for i in range(1, lat_n - 1, 2):
-            here, north = m * lat_n + i, m * lat_n + i + 1
-            cross += [(here, north), (north, here)]
-        cross.append((m * lat_n + lat_n - 1, (lon_n - 1 - m) * lat_n + lat_n - 1))
+    cross = [[m * lat_n + i, m * lat_n + i + 1] for m in range(lon_n) for i in range(1, lat_n - 1, 2)]
+    for i in (0, lat_n - 1):
+        cross += [[m * lat_n + i, (lon_n - 1 - m) * lat_n + i] for m in range(lon_n // 2)]
+    rim_b = lax.all_gather(next_b, ("lon", "lat"), axis_index_groups=cross)
     rim_a = lax.ppermute(next_a, "lat", lat_pairs)
-    rim_b = lax.ppermute(next_b, ("lon", "lat"), cross)
 
     padded = pltpu.VMEM((rows + 2 * PAD, cols), F32)
     flat = pltpu.VMEM(plane, F32)
@@ -484,14 +489,15 @@
     outs = pl.pallas_call(
         functools.partial(border_kernel, levels),
         out_shape=[jax.ShapeDtypeStruct(stack, F32)] * 3,
-        in_specs=[vmem] * 13,
+        in_specs=[vmem] * 10 + [hbm] + [vmem] * 2,
         out_specs=[hbm] * 3,
         scratch_shapes=[pltpu.VMEM(stack, F32)] * 3
         + [rim_pair] * 4
-        + [pltpu.SemaphoreType.DMA((3, levels))],
+        + [pltpu.VMEM(plane, F32), pltpu.VMEM(message, F32)]
+        + [pltpu.SemaphoreType.DMA((3, levels)), pltpu.SemaphoreType.DMA],
         compiler_params=params,
         name="border",
-    )(*inner, send_a, send_b, recv_a, recv_b, lat_a, lat_b, rim_a, rim_b, drag, drag_ends)
+    )(*inner, send_a, send_b, recv_a, recv_b, lat_a, lat_b, rim_a, *in_hbm(rim_b), drag, drag_ends)
     return tuple(x.reshape(levels, rows, cols) for x in outs)
 
 

time: 29.6 us -> 32.1 us (1.084)
  the two profiles are of different devices: /device:TPU:2 before, /device:TPU:0 now
where the time goes in v2:
time: 32.1 us; the launch traced here: 31.9 us
  Pallas kernels  16.4 us (51%)
  starting transfers between devices  7.68 us (24%)
  blocking collectives  7.17 us (22%)
  between operations  0.67 us (2%)
    all_gather x1, blocking collectives, on_device(): rim_b = lax.all_gather(next_b, ('lon', 'lat'), axis_index_groups=cross)  7.17 us
    ppermute x1, starting transfers between devices, on_device(): recv_b = lax.ppermute(send_b, 'lon', lon_cross)  5.67 us
    pallas_call x1, Pallas kernels, on_device(): pl.pallas_call(functools.partial(pack_kernel, levels), out_shape=[pltpu.V...  4.64 us
    pallas_call x1, Pallas kernels, on_device(): pl.pallas_call(functools.partial(border_kernel, levels), out_shape=[jax.S...  4.36 us
    pallas_call x1, Pallas kernels, on_device(): pl.pallas_call(functools.partial(inner_kernel, levels, 32), out_shape=[pl...  4.04 us
    pallas_call x1, Pallas kernels, on_device(): pl.pallas_call(functools.partial(shift_kernel, levels), out_shape=[pltpu....  3.17 us
    ppermute x1, starting transfers between devices, on_device(): rim_a = lax.ppermute(next_a, 'lat', lat_pairs)  1.49 us
  transfers between devices with their start and end apart: 3, of which 0 were waited for; matrix products, arithmetic and copies ran while one was open for 0% of the time, Pallas kernels for 23%

profile of v2, /device:TPU:0, one launch (start us, length us, event | category | flops | bytes accessed | tf_op | source)
XLA Modules:
  0.0 31.9 jit_solution(7598774059891143928)
XLA Ops:
  0.6 4.6 %pack.1 = (f32[128,128]{1,0:T(8,128)S(1)}, f32[128,128]{1,0:T(8,128)S(1)}, f32[128,128]{1,0:T(8,128)S(1)}, f32[128,128]{1,0:T(8,128)S(1)}, f32[8,128]{1,0:T(8,12...) custom-call(f32[2048,128]{1,0:T(8,128)} %bitcast.28, ...), custom_call_target="tpu_custom_call" | custom-call | tf_op jit(solution)/shard_map/pack/pallas_call | solution.py:430
  5.3 0.5 %collective-permute-start = (f32[128,128]{1,0:T(8,128)S(1)}, f32[128,128]{1,0:T(8,128)S(1)}, u32[]{:S(2)}, u32[]{:S(2)}) collective-permute-start(f32[128,128]{1,0:T(8,128)S(1)} %get-tuple-element.53.send_a), channel_id=1, source_target_pairs={{0,2},{2,0},{4,6},{6,4},{8,10},{10,8},{12,14},{14,12},{16,18},{18,... | collective-permute-start | bytes 196616 | tf_op jit(solution)/shard_map/ppermute | solution.py:444
  5.8 5.7 %collective-permute-start.1 = (f32[128,128]{1,0:T(8,128)S(1)}, f32[128,128]{1,0:T(8,128)S(1)}, u32[]{:S(2)}, u32[]{:S(2)}) collective-permute-start(f32[128,128]{1,0:T(8,128)S(1)} %get-tuple-element.54.send_b), channel_id=1, source_target_pairs={{0,30},{2,4},{4,2},{6,8},{8,6},{10,12},{12,10},{14,16},{16,14},{18... | collective-permute-start | bytes 196616 | tf_op jit(solution)/shard_map/ppermute | solution.py:445
  11.5 3.2 %shift.1 = (f32[16,128,1,128]{3,2,1,0:T(1,128)S(1)}, f32[16,128,1,128]{3,2,1,0:T(1,128)S(1)}, f32[16,128,1,128]{3,2,1,0:T(1,128)S(1)}, f32[16,128,1,128]{3,2,1,0...) custom-call(f32[16,128,1,128]{3,2,1,0:T(1,128)} %bitcast.29, ...), custom_call_target="tpu_custom_call" | custom-call | tf_op jit(solution)/shard_map/shift/pallas_call | solution.py:447
  14.6 0.0 collective-permute-done.recv_a
  14.7 0.0 collective-permute-done.1.recv_b
  14.7 0.2 corners.1
  14.8 1.5 %collective-permute-start.2 = (f32[128,128]{1,0:T(8,128)S(1)}, f32[128,128]{1,0:T(8,128)S(1)}, u32[]{:S(2)}, u32[]{:S(2)}) collective-permute-start(f32[128,128]{1,0:T(8,128)S(1)} %get-tuple-element.57), channel_id=1, source_target_pairs={{0,1},{1,0},{2,3},{3,2},{4,5},{5,4},{6,7},{7,6},{8,9},{9,8},{10,11... | collective-permute-start | bytes 196616 | tf_op jit(solution)/shard_map/ppermute | solution.py:473
  16.3 4.0 %inner.1 = (f32[2048,128]{1,0:T(8,128)S(1)}, f32[2048,128]{1,0:T(8,128)S(1)}, f32[2048,128]{1,0:T(8,128)S(1)}) custom-call(f32[2048,128]{1,0:T(8,128)S(1)} %get-tuple-element.33.tv.t, f32[2048,128]{1,0:T(8,128)S(1)} %get-tuple-element.34.uv.u, f32[2048,128]{1,0:T(8,128)S(1)} %get-tuple-element.35.vv.v, f32[2048,128]{1,0:T(8,128)S(1)} %get-tuple-element.36.kv.kd, ...), custom_call_target="tpu_custom_call" | custom-call | flops 26214400 | bytes 1048576 | tf_op jit(solution)/shard_map/inner/pallas_call | solution.py:477
  20.4 7.2 %all-gather = f32[256,128]{1,0:T(8,128)} all-gather(f32[128,128]{1,0:T(8,128)S(1)} %get-tuple-element.58), channel_id=2, replica_groups={{0,30},{2,28},{4,26},{6,24},{8,22},{10,20},{12,18},{14,16},{1,31},{3,29..., dimensions={0}, use_global_device_ids=true | all-gather | bytes 196608 | tf_op jit(solution)/shard_map/all_gather | solution.py:472
  27.6 0.0 collective-permute-done.2.rim_a
  27.6 4.4 %border.1 = (f32[2048,128]{1,0:T(8,128)}, f32[2048,128]{1,0:T(8,128)}, f32[2048,128]{1,0:T(8,128)}) custom-call(f32[2048,128]{1,0:T(8,128)S(1)} %get-tuple-element.50.t_in, f32[2048,128]{1,0:T(8,128)S(1)} %get-tuple-element.51.u_in, f32[2048,128]{1,0:T(8,128)S(1)} %get-tuple-element.52.v_in, f32[128,128]{1,0:T(8,128)S(1)} %get-tuple-element.53.send_a, ...), custom_call_target="tpu_custom_call" | custom-call | tf_op jit(solution)/shard_map/border/pallas_call | solution.py:489
Async XLA Ops:
  5.3 9.4 %collective-permute-start = (f32[128,128]{1,0:T(8,128)S(1)}, f32[128,128]{1,0:T(8,128)S(1)}, u32[]{:S(2)}, u32[]{:S(2)}) collective-permute-start(f32[128,128]{1,0:T(8,128)S(1)} %get-tuple-element.53.send_a), channel_id=1, source_target_pairs={{0,2},{2,0},{4,6},{6,4},{8,10},{10,8},{12,14},{14,12},{16,18},{18,... | collective-permute-start | bytes 196616 | tf_op jit(solution)/shard_map/ppermute | solution.py:444
  5.8 8.9 %collective-permute-start.1 = (f32[128,128]{1,0:T(8,128)S(1)}, f32[128,128]{1,0:T(8,128)S(1)}, u32[]{:S(2)}, u32[]{:S(2)}) collective-permute-start(f32[128,128]{1,0:T(8,128)S(1)} %get-tuple-element.54.send_b), channel_id=1, source_target_pairs={{0,30},{2,4},{4,2},{6,8},{8,6},{10,12},{12,10},{14,16},{16,14},{18... | collective-permute-start | bytes 196616 | tf_op jit(solution)/shard_map/ppermute | solution.py:445
  14.8 12.7 %collective-permute-start.2 = (f32[128,128]{1,0:T(8,128)S(1)}, f32[128,128]{1,0:T(8,128)S(1)}, u32[]{:S(2)}, u32[]{:S(2)}) collective-permute-start(f32[128,128]{1,0:T(8,128)S(1)} %get-tuple-element.57), channel_id=1, source_target_pairs={{0,1},{1,0},{2,3},{3,2},{4,5},{5,4},{6,7},{7,6},{8,9},{9,8},{10,11... | collective-permute-start | bytes 196616 | tf_op jit(solution)/shard_map/ppermute | solution.py:473

commit v3 on v2

--- a/solution.py
+++ b/solution.py
@@ -9,7 +9,7 @@
 
 DT = 0.25
 GRAV = 0.1
-F32, BF16 = jnp.float32, jnp.bfloat16
+F32 = jnp.float32
 PAD = 8
 RIM = 128
 TAIL = 112
@@ -31,55 +31,69 @@
     return lax.broadcasted_iota(jnp.int32, shape, dim)
 
 
-def halves(x):
-    high = x.astype(BF16)
-    return jnp.concatenate([high, (x - high.astype(F32)).astype(BF16)], 1)
-
-
-def across(a, b):
-    return lax.dot_general(a, b, (((1,), (1,)), ((), ())), preferred_element_type=F32)
-
-
 def parity(axis):
     return lax.axis_index(axis) % 2 == 0
 
 
+def rows_kernel(
+    levels, t, u, v, kd, water, strata, friction, lat_a, lat_b, coriolis, drag,
+    water_rows, strata_rows, sem, plane_sem, drag_sem,
+):
+    rows, cols = coriolis.shape
+    copies, planes = [], []
+    lat_even = parity("lat")
+    for side, message in enumerate((lat_a, lat_b)):
+        north = lat_even if side == 0 else jnp.logical_not(lat_even)
+        near = jnp.where(north, rows - 1, 0)
+        far = jnp.where(north, rows - 2, 1)
+        for n, row in enumerate((near, far)):
+            for m, (src, dst) in enumerate(((water, water_rows), (strata, strata_rows))):
+                at = dst.at[pl.ds(2 * side + n, 1)]
+                planes.append(pltpu.make_async_copy(src.at[pl.ds(row, 1)], at, plane_sem.at[m, side, n]))
+        for q, (src, row) in enumerate(
+            ((t, near), (t, far), (kd, near), (kd, far), (v, near), (v, far), (u, near))
+        ):
+            at = message.at[pl.ds(q * levels, levels)]
+            copies.append(pltpu.make_async_copy(src.at[:, row], at, sem.at[side, q]))
+    whole = pltpu.make_async_copy(friction, drag, drag_sem)
+    for copy in planes + copies + [whole]:
+        copy.start()
+    row = iota((rows, cols), 0) + lax.axis_index("lat") * rows
+    total = rows * lax.axis_size("lat")
+    coriolis[...] = DT * jnp.sin(jnp.pi * ((row.astype(F32) + 0.5) / total - 0.5))
+    for copy in planes:
+        copy.wait()
+    for side, message in enumerate((lat_a, lat_b)):
+        message[pl.ds(TAIL + 2, RIM - TAIL - 2)] = jnp.zeros((RIM - TAIL - 2, 1, cols), F32)
+        for n in range(2):
+            at = pl.ds(2 * side + n, 1)
+            message[pl.ds(TAIL + n, 1)] = (water_rows[at] * strata_rows[at]).astype(F32)
+    whole.wait()
+    drag[...] = DT * drag[...]
+    for copy in copies:
+        copy.wait()
+
+
 def pack_kernel(
-    levels, t, u, v, kd, water_hbm, strata_hbm, friction_hbm,
-    send_a, send_b, depth, drag, drag_ends, tv, uv, vv, kv,
-    water, strata, gathered, ends, sem, plane_sem,
+    levels, t, u, v, kd, water, strata, drag,
+    send_a, send_b, depth, drag_ends, gathered, ends,
 ):
     rows, cols = depth.shape
-    pieces, size = levels // CHUNK, CHUNK * rows
-    planes = []
-    for n, (src, dst) in enumerate(((water_hbm, water), (strata_hbm, strata), (friction_hbm, drag))):
-        planes.append(pltpu.make_async_copy(src, dst, plane_sem.at[n]))
-        planes[n].start()
-    fields = ((t, tv), (kd, kv), (u, uv), (v, vv))
-    for part in range(pieces):
-        for f, (src, dst) in enumerate(fields):
-            at = pl.ds(part * size, size)
-            pltpu.make_async_copy(src.at[at], dst.at[at], sem.at[f, part]).start()
-
     lane = iota((STRIP, cols), 1)
     edge = (lane < 2) | (lane >= cols - 2)
-    strips = [pl.ds(r, STRIP) for r in range(0, rows, STRIP)]
-    for copy in planes:
-        copy.wait()
-    for at in strips:
+    for r in range(0, rows, STRIP):
+        at = pl.ds(r, STRIP)
         d = (water[at, :] * strata[at, :]).astype(F32)
         depth[at, :] = d
-        drag[at, :] = DT * drag[at, :]
         gathered[2, at, :] = lanes(d, 2)
         gathered[3, at, :] = lanes(drag[at, :], 2)
         gathered[0, at, :] = jnp.zeros((STRIP, cols), F32)
         gathered[1, at, :] = jnp.zeros((STRIP, cols), F32)
 
-    @pl.loop(0, pieces)
+    @pl.loop(0, levels // CHUNK)
     def one_piece(part):
-        begin = pl.multiple_of(part * size, size)
-        for f, (src, full) in enumerate(fields):
-            pltpu.make_async_copy(src.at[pl.ds(begin, size)], full.at[pl.ds(begin, size)], sem.at[f, part]).wait()
+        begin = pl.multiple_of(part * CHUNK * rows, rows)
+        for f, full in enumerate((t, kd, u, v)):
             for r in range(0, rows, STRIP):
                 acc = gathered[f // 2, pl.ds(r, STRIP), :]
                 for n in range(CHUNK):
@@ -93,7 +107,7 @@
     d = gathered[2, :, :].T
     drag_ends[...] = gathered[3, :, :].T[0:8]
 
-    lon_even = parity("lon")
+    lon_even, lat_even = parity("lon"), parity("lat")
     for q, (f, near) in enumerate(
         ((0, True), (0, False), (1, True), (1, False), (2, True), (2, False), (3, True))
     ):
@@ -103,6 +117,7 @@
         at = pl.ds(q * levels, levels)
         send_a[at, :] = jnp.where(lon_even, east, west)
         send_b[at, :] = jnp.where(lon_even, west, east)
+
     tail = (RIM - TAIL, cols)
     sub = iota(tail, 0)
 
@@ -115,71 +130,29 @@
     send_b[pl.ds(TAIL, RIM - TAIL), :] = jnp.where(lon_even, west, east)
 
 
-def shift_kernel(
-    levels, t, u, v, kd, depth, tv, uv, vv, kv,
-    tn, un, vn, kn, lat_a, lat_b, te, ke, ue, uw, ve, vw, coriolis, sem, row_sem, depth_sem,
-):
-    rows, cols = coriolis.shape
-    copies = []
-    lat_even = parity("lat")
-    for side, message in enumerate((lat_a, lat_b)):
-        north = lat_even if side == 0 else jnp.logical_not(lat_even)
-        near = jnp.where(north, rows - 1, 0)
-        far = jnp.where(north, rows - 2, 1)
-        for q, (src, row) in enumerate(
-            ((t, near), (t, far), (kd, near), (kd, far), (v, near), (v, far), (u, near))
-        ):
-            at = message.at[pl.ds(q * levels, levels)]
-            copies.append(pltpu.make_async_copy(src.at[:, row], at, row_sem.at[side, q]))
-        for n, row in enumerate((near, far)):
-            at = message.at[pl.ds(TAIL + n, 1)]
-            copies.append(pltpu.make_async_copy(depth.at[pl.ds(row, 1)], at, depth_sem.at[side, n]))
-    for n, (src, dst) in enumerate(((t, tn), (v, vn), (kd, kn), (u, un))):
-        here, north = pl.ds(0, rows - 1), pl.ds(1, rows - 1)
-        copies.append(pltpu.make_async_copy(src.at[:, north], dst.at[:, here], sem.at[n]))
-    for copy in copies:
-        copy.start()
-
-    row = iota((rows, cols), 0) + lax.axis_index("lat") * rows
-    total = rows * lax.axis_size("lat")
-    coriolis[...] = DT * jnp.sin(jnp.pi * ((row.astype(F32) + 0.5) / total - 0.5))
-
-    @pl.loop(0, levels)
-    def one_level(k):
-        for r in range(0, rows, STRIP):
-            at = pl.ds(pl.multiple_of(k * rows, rows) + r, STRIP)
-            for src, east in ((tv, te), (kv, ke), (uv, ue), (vv, ve)):
-                east[at, :] = lanes(src[at, :], -1)
-            for src, west in ((uv, uw), (vv, vw)):
-                west[at, :] = lanes(src[at, :], 1)
-
-    for copy in copies:
-        copy.wait()
-
-
-def corner_kernel(lat_a, lat_b, recv_a, recv_b, out_a, out_b):
-    cols = recv_a.shape[1]
+def corner_kernel(levels, send_a, send_b, rim_a, rim_b, out_a, out_b):
+    cols = send_a.shape[1]
     lon_even, lat_even = parity("lon"), parity("lat")
-    a, b = recv_a[...], recv_b[...]
-    west, east = jnp.where(lon_even, b, a), jnp.where(lon_even, a, b)
-    shape = (8, 2 * cols)
-    lane, sub = iota(shape, 1) & (cols - 1), iota(shape, 0)
-    chosen = ((sub == 0) & (lane == 0)) | ((sub == 1) & (lane == cols - 1))
-    take = jnp.where(chosen, 1.0, 0.0).astype(BF16)
-    west, east = across(take, halves(west)), across(take, halves(east))
+    a, b = rim_a[...], rim_b[...]
+    south, north = jnp.where(lat_even, b, a).T, jnp.where(lat_even, a, b).T
+    is_top = lax.axis_index("lat") == lax.axis_size("lat") - 1
+    line = iota((1, cols), 1)
+    turn = jnp.where((line >= 4 * levels) & (line < 7 * levels), -1.0, 1.0)
+    first, last = north[0:1], north[cols - 1 : cols]
+    first, last = jnp.where(is_top, turn * last, first), jnp.where(is_top, turn * first, last)
     tail = (RIM - TAIL, cols)
     sub = iota(tail, 0)
-    for n, (main, out) in enumerate(((lat_a, out_a), (lat_b, out_b))):
-        north = lat_even if n == 0 else jnp.logical_not(lat_even)
-        w = jnp.broadcast_to(jnp.where(north, west[1:2], west[0:1]), tail)
-        e = jnp.broadcast_to(jnp.where(north, east[1:2], east[0:1]), tail)
+    for n, (main, out) in enumerate(((send_a, out_a), (send_b, out_b))):
+        east = lon_even if n == 0 else jnp.logical_not(lon_even)
+        s = jnp.broadcast_to(jnp.where(east, south[cols - 1 : cols], south[0:1]), tail)
+        q = jnp.broadcast_to(jnp.where(east, last, first), tail)
         out[pl.ds(0, TAIL), :] = main[pl.ds(0, TAIL), :]
-        end = jnp.where(sub == 2, w, jnp.where(sub == 3, e, 0.0))
-        out[pl.ds(TAIL, RIM - TAIL), :] = jnp.where(sub < 2, main[pl.ds(TAIL, RIM - TAIL), :], end)
+        depths = main[pl.ds(TAIL, RIM - TAIL), :]
+        out[pl.ds(TAIL, RIM - TAIL), :] = jnp.where(sub == 2, s, jnp.where(sub == 3, q, depths))
 
 
 def inner_kernel(
-    levels, strip, t, u, v, kd, tn, un, vn, kn, te, ke, ue, uw, ve, vw, depth, drag, coriolis,
+    levels, strip, t, u, v, kd, depth, drag, coriolis,
     t_out, u_out, v_out,
     fn, gu, gv, back, de, dw, dn, dragn, p, up,
 ):
@@ -216,22 +189,26 @@
         for r in starts:
             here = pl.ds(base + r, strip)
             plane, padded, below = pl.ds(r, strip), pl.ds(PAD + r, strip), pl.ds(PAD + r - 1, strip)
+
+            def north_of(ref, mid):
+                return ref[pl.ds(base + r + 1, strip), :] if r + strip < rows else sublanes(mid, -1)
+
             d = depth[plane, :]
             t0, u0, v0, k0 = t[here, :], u[here, :], v[here, :], kd[here, :]
             wet, wet_e, wet_n = d > kf, de[plane, :] > kf, dn[plane, :] > kf
 
-            t1, u1, k1 = te[here, :], ue[here, :], ke[here, :]
+            t1, u1, k1 = lanes(t0, -1), lanes(u0, -1), lanes(k0, -1)
             flux = 0.0625 * ((u0 + u1) * (t0 + t1)) - 0.125 * ((k0 + k1) * (t1 - t0))
             flux = jnp.where(wet_e, flux, 0.0)
             change = lanes(flux, 1) - flux
             wet_w = dw[plane, :] > kf
-            lap_u = jnp.where(wet_e, u1 - u0, 0.0) + jnp.where(wet_w, uw[here, :] - u0, 0.0)
-            lap_v = jnp.where(wet_e, ve[here, :] - v0, 0.0) + jnp.where(wet_w, vw[here, :] - v0, 0.0)
-
-            t1, v1, k1 = tn[here, :], vn[here, :], kn[here, :]
+            lap_u = jnp.where(wet_e, u1 - u0, 0.0) + jnp.where(wet_w, lanes(u0, 1) - u0, 0.0)
+            lap_v = jnp.where(wet_e, lanes(v0, -1) - v0, 0.0) + jnp.where(wet_w, lanes(v0, 1) - v0, 0.0)
+
+            t1, v1, k1 = north_of(t, t0), north_of(v, v0), north_of(kd, k0)
             flux = 0.0625 * ((v0 + v1) * (t0 + t1)) - 0.125 * ((k0 + k1) * (t1 - t0))
             flux = jnp.where(wet_n, flux, 0.0)
-            lap = jnp.where(wet_n, un[here, :] - u0, 0.0)
+            lap = jnp.where(wet_n, north_of(u, u0) - u0, 0.0)
             lap2 = jnp.where(wet_n, v1 - v0, 0.0)
             fn[padded, :] = flux
             gu[padded, :] = lap
@@ -267,40 +244,27 @@
 
 def border_kernel(
     levels, t_in, u_in, v_in,
-    send_a, send_b, recv_a, recv_b, lat_a, lat_b, rim_a, gathered, drag, drag_ends,
-    t_out, u_out, v_out, tb, ub, vb, tr, ur, vr0, vr1, turned, rim_b, sem, rim_sem,
+    send_a, send_b, recv_a, recv_b, lat_a, lat_b, rim_a, rim_b, drag, drag_ends,
+    t_out, u_out, v_out, tb, ub, vb, tr, ur, vr0, vr1, turned, sem,
 ):
     rows, cols = drag.shape
     lon_even, lat_even = parity("lon"), parity("lat")
-    lat = lax.axis_index("lat")
-    is_top, is_bottom = lat == lax.axis_size("lat") - 1, lat == 0
+    is_top = lax.axis_index("lat") == lax.axis_size("lat") - 1
 
     def sides(even, a, b):
         a, b = a[...], b[...]
         return jnp.where(even, b, a), jnp.where(even, a, b)
-
-    west_half = lax.axis_index("lon") < lax.axis_size("lon") // 2
-    first_of_pair = jnp.where(is_top | is_bottom, west_half, jnp.logical_not(lat_even))
-    fetch = pltpu.make_async_copy(gathered.at[jnp.where(first_of_pair, 1, 0)], rim_b, rim_sem)
-    fetch.start()
-    fetch.wait()
 
     own_w, own_e = sides(lon_even, send_a, send_b)
     west, east = sides(lon_even, recv_a, recv_b)
     own_s, own_n = sides(lat_even, lat_a, lat_b)
     south, north = sides(lat_even, rim_a, rim_b)
-    south = jnp.where(is_bottom, 0.0, south)
-
-    shape = (RIM, 2 * cols)
-    unit = jnp.where((iota(shape, 1) & (cols - 1)) == iota(shape, 0), 1.0, 0.0).astype(BF16)
-    tails = jnp.concatenate([south[TAIL:], north[TAIL:]], 0)
-    ends = across(unit, halves(tails))
-    sw, se = ends[:, 2:3], ends[:, 3:4]
-    low, high = RIM - TAIL + 2, RIM - TAIL + 3
-    nw, ne = ends[:, low : low + 1], ends[:, high : high + 1]
+
+    low, high = TAIL + 2, TAIL + 3
+    sw, nw = (west.T[:, n : n + 1] for n in (low, high))
+    se, ne = (east.T[:, n : n + 1] for n in (low, high))
     line = iota((RIM, 1), 0)
     turn = jnp.where((line >= 4 * levels) & (line < 7 * levels), -1.0, 1.0)
-    nw, ne = jnp.where(is_top, turn * ne, nw), jnp.where(is_top, turn * nw, ne)
     mirrored = turn * jnp.take_along_axis(north, cols - 1 - iota((RIM, cols), 1), axis=1)
     north = jnp.where(is_top, mirrored, north)
 
@@ -345,7 +309,7 @@
 
     t_w, t_e = beyond(t1, ((0, levels),) * 4)
     k_w, k_e = beyond(k1, ((2 * levels, levels),) * 4)
-    s_w, s_e = beyond(s1, ((6 * levels, levels),) * 2 + ((4 * levels, levels),) * 2)
+    s_w, s_e = beyond(s1, ((4 * levels, levels),) * 2 + ((6 * levels, levels),) * 2)
     d_w, d_e = beyond(d1, ((TAIL, 1),) * 4)
     flux_w = jnp.where(level < jnp.minimum(d_w, d1), face(1.0, s_w, s1, t_w, t1, k_w, k1), 0.0)
     flux_e = jnp.where(level < jnp.minimum(d1, d_e), face(1.0, s1, s_e, t1, t_e, k1, k_e), 0.0)
@@ -427,77 +391,79 @@
     def in_hbm(*arrays):
         return [pltpu.with_memory_space_constraint(x, pltpu.HBM) for x in arrays]
 
-    send_a, send_b, depth, drag, drag_ends, *fields = pl.pallas_call(
+    lat_a, lat_b, coriolis, drag = pl.pallas_call(
+        functools.partial(rows_kernel, levels),
+        out_shape=[pltpu.VMEM((RIM, 1, cols), F32)] * 2 + [pltpu.VMEM(plane, F32)] * 2,
+        in_specs=[hbm] * 7,
+        out_specs=[vmem] * 4,
+        scratch_shapes=[pltpu.VMEM((4, 1, cols), jnp.int32)] * 2
+        + [pltpu.SemaphoreType.DMA((2, 7)), pltpu.SemaphoreType.DMA((2, 2, 2)), pltpu.SemaphoreType.DMA],
+        compiler_params=params,
+        name="rows",
+    )(
+        *in_hbm(*[x.reshape(levels, rows, 1, cols) for x in (t, u, v, kd)]),
+        *in_hbm(*[x.reshape(rows, 1, cols) for x in (water, strata)], friction),
+    )
+    lat_a, lat_b = lat_a.reshape(message), lat_b.reshape(message)
+    lat_pairs = [(i, i ^ 1) for i in range(lat_n)]
+    cross = []
+    for m in range(lon_n):
+        for i in range(1, lat_n - 1, 2):
+            here, north = m * lat_n + i, m * lat_n + i + 1
+            cross += [(here, north), (north, here)]
+        cross.append((m * lat_n + lat_n - 1, (lon_n - 1 - m) * lat_n + lat_n - 1))
+    rim_b = lax.ppermute(lat_b, ("lon", "lat"), cross)
+    rim_a = lax.ppermute(lat_a, "lat", lat_pairs)
+
+    fields = [x.reshape(stack) for x in (t, u, v, kd)]
+    send_a, send_b, depth, drag_ends = pl.pallas_call(
         functools.partial(pack_kernel, levels),
-        out_shape=[pltpu.VMEM(s, F32) for s in (message, message, plane, plane, (8, cols)) + (stack,) * 4],
-        in_specs=[hbm] * 7,
-        out_specs=[vmem] * 9,
-        scratch_shapes=[pltpu.VMEM(plane, jnp.int32)] * 2
-        + [pltpu.VMEM((4, rows, cols), F32), pltpu.VMEM((2 * rows, cols), F32)]
-        + [pltpu.SemaphoreType.DMA((4, levels // CHUNK)), pltpu.SemaphoreType.DMA((3,))],
+        out_shape=[pltpu.VMEM(s, F32) for s in (message, message, plane, (8, cols))],
+        in_specs=[vmem] * 7,
+        out_specs=[vmem] * 4,
+        scratch_shapes=[pltpu.VMEM((4, rows, cols), F32), pltpu.VMEM((2 * rows, cols), F32)],
         compiler_params=params,
         name="pack",
-    )(*in_hbm(*[x.reshape(stack) for x in (t, u, v, kd)], water, strata, friction))
-
-    lon_pairs = [(i, i ^ 1) for i in range(lon_n)]
-    lon_cross = [(i, (i + 1) % lon_n if i % 2 else (i - 1) % lon_n) for i in range(lon_n)]
-    recv_a = lax.ppermute(send_a, "lon", lon_pairs)
-    recv_b = lax.ppermute(send_b, "lon", lon_cross)
-
-    *moved, lat_a, lat_b, te, ke, ue, uw, ve, vw, coriolis = pl.pallas_call(
-        functools.partial(shift_kernel, levels),
-        out_shape=[pltpu.VMEM((levels, rows, 1, cols), F32)] * 4 + [pltpu.VMEM((RIM, 1, cols), F32)] * 2
-        + [pltpu.VMEM(stack, F32)] * 6 + [pltpu.VMEM(plane, F32)],
-        in_specs=[hbm] * 4 + [vmem] * 5,
-        out_specs=[vmem] * 13,
-        scratch_shapes=[pltpu.SemaphoreType.DMA(x) for x in ((4,), (2, 7), (2, 2))],
-        compiler_params=params,
-        name="shift",
-    )(*in_hbm(*[x.reshape(levels, rows, 1, cols) for x in (t, u, v, kd)]), depth.reshape(rows, 1, cols), *fields)
-    moved = [x.reshape(stack) for x in moved]
-    lat_a, lat_b = lat_a.reshape(message), lat_b.reshape(message)
-
-    next_a, next_b = pl.pallas_call(
-        corner_kernel,
+    )(*fields, water, strata, drag)
+    send_a, send_b = pl.pallas_call(
+        functools.partial(corner_kernel, levels),
         out_shape=[pltpu.VMEM(message, F32)] * 2,
         in_specs=[vmem] * 4,
         out_specs=[vmem] * 2,
         compiler_params=params,
         name="corners",
-    )(lat_a, lat_b, recv_a, recv_b)
-    lat_pairs = [(i, i ^ 1) for i in range(lat_n)]
-    cross = [[m * lat_n + i, m * lat_n + i + 1] for m in range(lon_n) for i in range(1, lat_n - 1, 2)]
-    for i in (0, lat_n - 1):
-        cross += [[m * lat_n + i, (lon_n - 1 - m) * lat_n + i] for m in range(lon_n // 2)]
-    rim_b = lax.all_gather(next_b, ("lon", "lat"), axis_index_groups=cross)
-    rim_a = lax.ppermute(next_a, "lat", lat_pairs)
+    )(send_a, send_b, rim_a, rim_b)
+    lon_pairs = [(i, i ^ 1) for i in range(lon_n)]
+    lon_cross = [(i, (i + 1) % lon_n if i % 2 else (i - 1) % lon_n) for i in range(lon_n)]
+    recv_b = lax.ppermute(send_b, "lon", lon_cross)
+    recv_a = lax.ppermute(send_a, "lon", lon_pairs)
 
     padded = pltpu.VMEM((rows + 2 * PAD, cols), F32)
     flat = pltpu.VMEM(plane, F32)
     inner = pl.pallas_call(
         functools.partial(inner_kernel, levels, 32),
         out_shape=[pltpu.VMEM(stack, F32)] * 3,
-        in_specs=[vmem] * 17,
+        in_specs=[vmem] * 7,
         out_specs=[vmem] * 3,
         scratch_shapes=[padded, padded, flat, padded, flat, flat, flat, flat, padded, flat],
         compiler_params=params,
         cost_estimate=pl.CostEstimate(flops=100 * tall * cols, bytes_accessed=1 << 20, transcendentals=0),
         name="inner",
-    )(*fields, *moved, te, ke, ue, uw, ve, vw, depth, drag, coriolis)
+    )(*fields, depth, drag, coriolis)
 
     rim_pair = pltpu.VMEM((2 * levels, cols), F32)
     outs = pl.pallas_call(
         functools.partial(border_kernel, levels),
         out_shape=[jax.ShapeDtypeStruct(stack, F32)] * 3,
-        in_specs=[vmem] * 10 + [hbm] + [vmem] * 2,
+        in_specs=[vmem] * 13,
         out_specs=[hbm] * 3,
         scratch_shapes=[pltpu.VMEM(stack, F32)] * 3
         + [rim_pair] * 4
-        + [pltpu.VMEM(plane, F32), pltpu.VMEM(message, F32)]
-        + [pltpu.SemaphoreType.DMA((3, levels)), pltpu.SemaphoreType.DMA],
+        + [pltpu.VMEM(plane, F32)]
+        + [pltpu.SemaphoreType.DMA((3, levels))],
         compiler_params=params,
         name="border",
-    )(*inner, send_a, send_b, recv_a, recv_b, lat_a, lat_b, rim_a, *in_hbm(rim_b), drag, drag_ends)
+    )(*inner, send_a, send_b, recv_a, recv_b, lat_a, lat_b, rim_a, rim_b, drag, drag_ends)
     return tuple(x.reshape(levels, rows, cols) for x in outs)
 
 

time: 32.1 us -> 24.8 us (0.77)
  the two profiles are of different devices: /device:TPU:0 before, /device:TPU:2 now
where the time goes in v3:
time: 24.8 us; the launch traced here: 24.7 us
  starting transfers between devices  11.8 us (48%)
  Pallas kernels  11.5 us (46%)
  between operations  0.8 us (3%)
  waiting for transfers between devices  0.61 us (2%)
    ppermute x1, starting transfers between devices, on_device(): rim_b = lax.ppermute(lat_b, ('lon', 'lat'), cross)  6.13 us
    pallas_call x1, Pallas kernels, on_device(): pl.pallas_call(functools.partial(inner_kernel, levels, 32), out_shape=[pl...  4.98 us
    ppermute x1, starting transfers between devices, on_device(): recv_b = lax.ppermute(send_b, 'lon', lon_cross)  4.87 us
    pallas_call x1, Pallas kernels, on_device(): pl.pallas_call(functools.partial(border_kernel, levels), out_shape=[jax.S...  3.48 us
    pallas_call x1, Pallas kernels, on_device(): pl.pallas_call(functools.partial(pack_kernel, levels), out_shape=[pltpu.V...  1.56 us
    pallas_call x1, Pallas kernels, on_device(): pl.pallas_call(functools.partial(rows_kernel, levels), out_shape=[pltpu.V...  1.35 us
    ppermute x1, starting transfers between devices, on_device(): recv_a = lax.ppermute(send_a, 'lon', lon_pairs)  0.71 us
    ppermute x1, waiting for transfers between devices, on_device(): rim_b = lax.ppermute(lat_b, ('lon', 'lat'), cross)  0.6 us
  transfers between devices with their start and end apart: 4, of which 1 were waited for; matrix products, arithmetic and copies ran while one was open for 0% of the time, Pallas kernels for 26%

profile of v3, /device:TPU:2, one launch (start us, length us, event | category | flops | bytes accessed | tf_op | source)
XLA Modules:
  0.0 24.7 jit_solution(17493149181490501119)
XLA Ops:
  0.6 0.0 copy-start
  0.6 0.0 copy-start.1
  0.7 0.0 copy-start.2
  0.7 0.0 copy-start.3
  0.7 0.0 copy-start.4
  0.7 0.0 copy-start.5
  0.7 1.3 %rows.1 = (f32[128,1,128]{2,1,0:T(1,128)S(1)}, f32[128,1,128]{2,1,0:T(1,128)S(1)}, f32[128,128]{1,0:T(8,128)S(1)}, f32[128,128]{1,0:T(8,128)S(1)}) custom-call(f32[16,128,1,128]{3,2,1,0:T(1,128)} %bitcast.15, f32[16,128,1,128]{3,2,1,0:T(1,128)} %bitcast.18, f32[16,128,1,128]{3,2,1,0:T(1,128)} %bitcast.21, f32[16,128,1,128]{3,2,1,0:T(1,128)} %bitcast.24, ...), custom_call_target="tpu_custom_call" | custom-call | tf_op jit(solution)/shard_map/rows/pallas_call | solution.py:394
  2.0 0.1 collective-permute-start
  2.1 6.1 %collective-permute-start.1 = (f32[128,128]{1,0:T(8,128)S(1)}, f32[128,128]{1,0:T(8,128)S(1)}, u32[]{:S(2)}, u32[]{:S(2)}) collective-permute-start(f32[128,128]{1,0:T(8,128)S(1)} %bitcast.31), channel_id=1, source_target_pairs={{1,31},{3,29},{5,27},{7,25},{9,23},{11,21},{13,19},{15,17},{17,15}... | collective-permute-start | bytes 196616 | tf_op jit(solution)/shard_map/ppermute | solution.py:415
  8.3 0.0 copy-done
  8.3 0.0 copy-done.1
  8.3 0.0 copy-done.2
  8.3 0.0 copy-done.3
  8.3 0.0 copy-done.4
  8.3 1.6 %pack.1 = (f32[128,128]{1,0:T(8,128)S(1)}, f32[128,128]{1,0:T(8,128)S(1)}, f32[128,128]{1,0:T(8,128)S(1)}, f32[8,128]{1,0:T(8,128)S(1)}) custom-call(f32[2048,128]{1,0:T(8,128)S(1)} %bitcast.16, f32[2048,128]{1,0:T(8,128)S(1)} %bitcast.19, f32[2048,128]{1,0:T(8,128)S(1)} %bitcast.22, f32[2048,128]{1,0:T(8,128)S(1)} %bitcast.25, s32[128,128]{1,0:T(8,128)S(1)} %copy-done.4, ...), custom_call_target="tpu_custom_call" | custom-call | tf_op jit(solution)/shard_map/pack/pallas_call | solution.py:419
  9.9 0.0 collective-permute-done.rim_a
  9.9 0.6 %collective-permute-done.1.rim_b = f32[128,128]{1,0:T(8,128)S(1)} collective-permute-done((f32[128,128]{1,0:T(8,128)S(1)}, f32[128,128]{1,0:T(8,128)S(1)}, u32[]{:S(2)}, u32[]{:S(2)}) %collective-permute-start.1) | collective-permute-done | bytes 65568 | tf_op jit(solution)/shard_map/ppermute | solution.py:415
  10.5 0.1 corners.1
  10.6 0.7 %collective-permute-start.2 = (f32[128,128]{1,0:T(8,128)S(1)}, f32[128,128]{1,0:T(8,128)S(1)}, u32[]{:S(2)}, u32[]{:S(2)}) collective-permute-start(f32[128,128]{1,0:T(8,128)S(1)} %get-tuple-element.29.send_a), channel_id=1, source_target_pairs={{0,2},{2,0},{4,6},{6,4},{8,10},{10,8},{12,14},{14,12},{16,18},{18,... | collective-permute-start | bytes 196616 | tf_op jit(solution)/shard_map/ppermute | solution.py:439
  11.3 4.9 %collective-permute-start.3 = (f32[128,128]{1,0:T(8,128)S(1)}, f32[128,128]{1,0:T(8,128)S(1)}, u32[]{:S(2)}, u32[]{:S(2)}) collective-permute-start(f32[128,128]{1,0:T(8,128)S(1)} %get-tuple-element.30.send_b), channel_id=1, source_target_pairs={{0,30},{2,4},{4,2},{6,8},{8,6},{10,12},{12,10},{14,16},{16,14},{18... | collective-permute-start | bytes 196616 | tf_op jit(solution)/shard_map/ppermute | solution.py:438
  16.2 5.0 %inner.1 = (f32[2048,128]{1,0:T(8,128)S(1)}, f32[2048,128]{1,0:T(8,128)S(1)}, f32[2048,128]{1,0:T(8,128)S(1)}) custom-call(f32[2048,128]{1,0:T(8,128)S(1)} %bitcast.17, f32[2048,128]{1,0:T(8,128)S(1)} %bitcast.20, f32[2048,128]{1,0:T(8,128)S(1)} %bitcast.23, f32[2048,128]{1,0:T(8,128)S(1)} %bitcast.26, f32[128,128]{1,0:T(8,128)S(1)} %get-tuple-element.20.depth, ...), custom_call_target="tpu_custom_call" | custom-call | flops 26214400 | bytes 1048576 | tf_op jit(solution)/shard_map/inner/pallas_call | solution.py:443
  21.2 0.0 collective-permute-done.2.recv_a
  21.2 0.0 collective-permute-done.3.recv_b
  21.2 3.5 %border.1 = (f32[2048,128]{1,0:T(8,128)}, f32[2048,128]{1,0:T(8,128)}, f32[2048,128]{1,0:T(8,128)}) custom-call(f32[2048,128]{1,0:T(8,128)S(1)} %get-tuple-element.22.t_in, f32[2048,128]{1,0:T(8,128)S(1)} %get-tuple-element.23.u_in, f32[2048,128]{1,0:T(8,128)S(1)} %get-tuple-element.24.v_in, f32[128,128]{1,0:T(8,128)S(1)} %get-tuple-element.29.send_a, ...), custom_call_target="tpu_custom_call" | custom-call | tf_op jit(solution)/shard_map/border/pallas_call | solution.py:455
  (1 shorter events, 0.0 us)
Async XLA Ops:
  0.6 7.6 %copy-start = (f32[16,128,128]{2,1,0:T(8,128)S(1)}, f32[16,128,128]{2,1,0:T(8,128)}, u32[]{:S(2)}) copy-start(f32[16,128,128]{2,1,0:T(8,128)} %param.7) | copy-start | bytes 3145732
  0.6 7.6 %copy-start.1 = (f32[16,128,128]{2,1,0:T(8,128)S(1)}, f32[16,128,128]{2,1,0:T(8,128)}, u32[]{:S(2)}) copy-start(f32[16,128,128]{2,1,0:T(8,128)} %param.8) | copy-start | bytes 3145732
  0.7 7.6 %copy-start.2 = (f32[16,128,128]{2,1,0:T(8,128)S(1)}, f32[16,128,128]{2,1,0:T(8,128)}, u32[]{:S(2)}) copy-start(f32[16,128,128]{2,1,0:T(8,128)} %param.9) | copy-start | bytes 3145732
  0.7 7.6 %copy-start.3 = (f32[16,128,128]{2,1,0:T(8,128)S(1)}, f32[16,128,128]{2,1,0:T(8,128)}, u32[]{:S(2)}) copy-start(f32[16,128,128]{2,1,0:T(8,128)} %param.10) | copy-start | bytes 3145732
  0.7 7.6 %copy-start.4 = (s32[128,128]{1,0:T(8,128)S(1)}, s32[128,128]{1,0:T(8,128)}, u32[]{:S(2)}) copy-start(s32[128,128]{1,0:T(8,128)} %water.1) | copy-start | bytes 196612
  0.7 7.6 %copy-start.5 = (s32[128,128]{1,0:T(8,128)S(1)}, s32[128,128]{1,0:T(8,128)}, u32[]{:S(2)}) copy-start(s32[128,128]{1,0:T(8,128)} %strata.1) | copy-start | bytes 196612
  2.0 7.9 %collective-permute-start = (f32[128,128]{1,0:T(8,128)S(1)}, f32[128,128]{1,0:T(8,128)S(1)}, u32[]{:S(2)}, u32[]{:S(2)}) collective-permute-start(f32[128,128]{1,0:T(8,128)S(1)} %bitcast.29), channel_id=1, source_target_pairs={{0,1},{1,0},{2,3},{3,2},{4,5},{5,4},{6,7},{7,6},{8,9},{9,8},{10,11... | collective-permute-start | bytes 196616 | tf_op jit(solution)/shard_map/ppermute | solution.py:416
  2.1 8.4 %collective-permute-start.1 = (f32[128,128]{1,0:T(8,128)S(1)}, f32[128,128]{1,0:T(8,128)S(1)}, u32[]{:S(2)}, u32[]{:S(2)}) collective-permute-start(f32[128,128]{1,0:T(8,128)S(1)} %bitcast.31), channel_id=1, source_target_pairs={{1,31},{3,29},{5,27},{7,25},{9,23},{11,21},{13,19},{15,17},{17,15}... | collective-permute-start | bytes 196616 | tf_op jit(solution)/shard_map/ppermute | solution.py:415
  10.6 10.6 %collective-permute-start.2 = (f32[128,128]{1,0:T(8,128)S(1)}, f32[128,128]{1,0:T(8,128)S(1)}, u32[]{:S(2)}, u32[]{:S(2)}) collective-permute-start(f32[128,128]{1,0:T(8,128)S(1)} %get-tuple-element.29.send_a), channel_id=1, source_target_pairs={{0,2},{2,0},{4,6},{6,4},{8,10},{10,8},{12,14},{14,12},{16,18},{18,... | collective-permute-start | bytes 196616 | tf_op jit(solution)/shard_map/ppermute | solution.py:439
  11.3 9.9 %collective-permute-start.3 = (f32[128,128]{1,0:T(8,128)S(1)}, f32[128,128]{1,0:T(8,128)S(1)}, u32[]{:S(2)}, u32[]{:S(2)}) collective-permute-start(f32[128,128]{1,0:T(8,128)S(1)} %get-tuple-element.30.send_b), channel_id=1, source_target_pairs={{0,30},{2,4},{4,2},{6,8},{8,6},{10,12},{12,10},{14,16},{16,14},{18... | collective-permute-start | bytes 196616 | tf_op jit(solution)/shard_map/ppermute | solution.py:438

commit v4 on v3

--- a/solution.py
+++ b/solution.py
@@ -130,10 +130,11 @@
     send_b[pl.ds(TAIL, RIM - TAIL), :] = jnp.where(lon_even, west, east)
 
 
-def corner_kernel(levels, send_a, send_b, rim_a, rim_b, out_a, out_b):
+def corner_kernel(levels, send_a, send_b, rim_b, rim_a, when, out_a, out_b):
     cols = send_a.shape[1]
     lon_even, lat_even = parity("lon"), parity("lat")
     a, b = rim_a[...], rim_b[...]
+    b = jnp.where(lax.axis_index("lat") == 0, 0.0, b)
     south, north = jnp.where(lat_even, b, a).T, jnp.where(lat_even, a, b).T
     is_top = lax.axis_index("lat") == lax.axis_size("lat") - 1
     line = iota((1, cols), 1)
@@ -152,14 +153,15 @@
 
 
 def inner_kernel(
-    levels, strip, t, u, v, kd, depth, drag, coriolis,
-    t_out, u_out, v_out,
-    fn, gu, gv, back, de, dw, dn, dragn, p, up,
+    levels, first, last, strip, t, u, v, kd, depth, drag, coriolis, p_in, up_in,
+    t_out, u_out, v_out, p, up,
+    fn, gu, gv, back, fn2, gu2, gv2, back2, p2, de, dw, dn, dragn,
 ):
     rows, cols = depth.shape
     zero = jnp.zeros((PAD, cols), F32)
-    for ref in (fn, gu, back):
+    for ref in (fn, gu, back, fn2, gu2, back2, p2):
         ref[pl.ds(0, PAD), :] = zero
+    p2[pl.ds(PAD + rows, PAD), :] = zero
 
     shape = (strip, cols)
     lane = iota(shape, 1)
@@ -178,16 +180,16 @@
             dn[here, :] = jnp.where(row < strip - 1, jnp.minimum(d, sublanes(d, -1)), 0.0)
             dragn[here, :] = sublanes(f, -1)
 
-    up[...] = jnp.zeros(up.shape, F32)
-    p[...] = jnp.zeros(p.shape, F32)
-
-    @pl.loop(0, levels)
-    def one_level(k):
+    up[...] = jnp.zeros(up.shape, F32) if p_in is None else up_in[...]
+    p[...] = jnp.zeros(p.shape, F32) if p_in is None else p_in[...]
+
+    def one_level(k, before, p, fn, gu, gv, back):
         kf = k.astype(F32)
         base = pl.multiple_of(k * rows, rows)
         above = pl.multiple_of(jnp.minimum(k + 1, levels - 1) * rows, rows)
+        begin = pl.multiple_of((k - first) * rows, rows)
         for r in starts:
-            here = pl.ds(base + r, strip)
+            here, out = pl.ds(base + r, strip), pl.ds(begin + r, strip)
             plane, padded, below = pl.ds(r, strip), pl.ds(PAD + r, strip), pl.ds(PAD + r - 1, strip)
 
             def north_of(ref, mid):
@@ -224,28 +226,47 @@
             up[plane, :] = rise
 
             t_next = jnp.where(wet, t0 + change, 0.0)
-            t_out[here, :] = t_next
-            p[padded, :] = p[padded, :] + t_next
+            t_out[out, :] = t_next
+            p[padded, :] = before[padded, :] + t_next
             c, f = coriolis[plane, :], drag[plane, :]
-            u_out[here, :] = u0 + (c * v0 + f * lap_u)
-            v_out[here, :] = v0 + (f * lap_v - c * u0)
-        middle = pl.ds(PAD, rows)
-        back[middle, :] = 0.0125 * p[middle, :] - dragn[...] * gv[...]
-        for r in starts:
-            plane, here = pl.ds(r, strip), pl.ds(base + r, strip)
-            wet = depth[plane, :] > kf
-            mid = p[pl.ds(PAD + r, strip), :]
-            slope = jnp.where(lane < cols - 1, lanes(mid, -1), 0.0) - jnp.where(lane > 0, lanes(mid, 1), 0.0)
-            u_next = u_out[here, :] - 0.0125 * slope
-            v_next = v_out[here, :] + back[pl.ds(PAD + r - 1, strip), :] - 0.0125 * p[pl.ds(PAD + r + 1, strip), :]
-            u_out[here, :] = jnp.where(wet, u_next, 0.0)
-            v_out[here, :] = jnp.where(wet, v_next, 0.0)
+            u_out[out, :] = u0 + (c * v0 + f * lap_u)
+            v_out[out, :] = v0 + (f * lap_v - c * u0)
+
+        def finish():
+            middle = pl.ds(PAD, rows)
+            back[middle, :] = 0.0125 * p[middle, :] - dragn[...] * gv[...]
+            for r in starts:
+                plane, out = pl.ds(r, strip), pl.ds(begin + r, strip)
+                wet = depth[plane, :] > kf
+                mid = p[pl.ds(PAD + r, strip), :]
+                slope = jnp.where(lane < cols - 1, lanes(mid, -1), 0.0) - jnp.where(lane > 0, lanes(mid, 1), 0.0)
+                u_next = u_out[out, :] - 0.0125 * slope
+                v_next = v_out[out, :] + back[pl.ds(PAD + r - 1, strip), :] - 0.0125 * p[pl.ds(PAD + r + 1, strip), :]
+                u_out[out, :] = jnp.where(wet, u_next, 0.0)
+                v_out[out, :] = jnp.where(wet, v_next, 0.0)
+
+        return finish
+
+    @pl.loop(first, last, step=2)
+    def two_levels(k):
+        finish = one_level(k, p, p2, fn, gu, gv, back)
+        finish2 = one_level(k + 1, p2, p, fn2, gu2, gv2, back2)
+        finish()
+        finish2()
+
+
+def low_kernel(levels, half, strip, *refs):
+    inner_kernel(levels, 0, half, strip, *refs[:7], None, None, *refs[7:])
+
+
+def high_kernel(levels, half, strip, *refs):
+    inner_kernel(levels, half, levels, strip, *refs[:9], *refs[10:])
 
 
 def border_kernel(
-    levels, t_in, u_in, v_in,
+    levels, t_low, u_low, v_low, t_high, u_high, v_high,
     send_a, send_b, recv_a, recv_b, lat_a, lat_b, rim_a, rim_b, drag, drag_ends,
-    t_out, u_out, v_out, tb, ub, vb, tr, ur, vr0, vr1, turned, sem,
+    t_out, u_out, v_out, tb, ub, vb, tr, ur, vr0, vr1, turned, turned_t, sem,
 ):
     rows, cols = drag.shape
     lon_even, lat_even = parity("lon"), parity("lat")
@@ -259,6 +280,7 @@
     west, east = sides(lon_even, recv_a, recv_b)
     own_s, own_n = sides(lat_even, lat_a, lat_b)
     south, north = sides(lat_even, rim_a, rim_b)
+    south = jnp.where(lax.axis_index("lat") == 0, 0.0, south)
 
     low, high = TAIL + 2, TAIL + 3
     sw, nw = (west.T[:, n : n + 1] for n in (low, high))
@@ -294,6 +316,54 @@
 
     inward = jnp.where(wet01, face(side, n1, n0, t1, t0, k1, k0), 0.0)
     outer = jnp.where(wet12, face(side, n2, n1, t2, t1, k2, k1), 0.0)
+
+    def turn_columns(ref, lines_of):
+        for g, x in enumerate(lines_of):
+            ref[pl.ds(g, levels, stride=8), :] = x
+        ref[...] = ref[...].T
+
+    tail = (8, cols)
+    sub8, lane8 = iota(tail, 0), iota((STRIP, cols), 1)
+    one, wide = (lane8 < 1) | (lane8 >= cols - 1), (lane8 < 2) | (lane8 >= cols - 2)
+    spots = ((one, cols - 1), (wide, cols - 2), (one, cols - 1 - 4))
+    bufs, outs = (tb, ub, vb), (t_out, u_out, v_out)
+
+    def copy_out(n, k):
+        at = pl.ds(pl.multiple_of(k * rows, rows), rows)
+        return pltpu.make_async_copy(bufs[n].at[at], outs[n].at[at], sem.at[n, k])
+
+    def one_level(k, n, part, inside):
+        base, buf = pl.multiple_of(k * rows, rows), bufs[n]
+        mask, to = spots[n]
+        by = (to - 8 * k) & (cols - 1)
+        for r in range(0, rows, STRIP):
+            moved = pltpu.roll((turned_t if n == 0 else turned)[pl.ds(r, STRIP), :], by, 1)
+            old = part[pl.ds(pl.multiple_of(inside * rows, rows) + r, STRIP), :]
+            buf[pl.ds(base + r, STRIP), :] = old + jnp.where(mask, moved, 0.0)
+
+        def row_of(ref, s):
+            return jnp.broadcast_to(ref[pl.ds(s * levels + k, 1), :], tail)
+
+        for s, (near, far, begin) in enumerate(((0, 1, 0), (7, 6, rows - 8))):
+            add = jnp.where(sub8 == near, row_of((tr, ur, vr0)[n], s), 0.0)
+            if n == 2:
+                add = jnp.where(sub8 == far, row_of(vr1, s), add)
+            at = pl.ds(base + begin, 8)
+            buf[at, :] = buf[at, :] + add
+        copy_out(n, k).start()
+
+    def all_levels(*which):
+        for begin, parts in ((0, (t_low, u_low, v_low)), (levels // 2, (t_high, u_high, v_high))):
+
+            @pl.loop(0, levels // 2, step=CHUNK)
+            def some_of_them(k):
+                for i in range(CHUNK):
+                    for n in which:
+                        one_level(begin + k + i, n, parts[n], k + i)
+
+    tr[...] = inward[half:]
+    turn_columns(turned_t, (inward[levels:half], inward[:levels]))
+    all_levels(0)
 
     before, after = (sw, se, sw, nw), (nw, ne, se, ne)
 
@@ -328,50 +398,14 @@
     slope = jnp.where(lane < cols - 1, lanes(dp0, -1), 0.0) - jnp.where(lane > 0, lanes(dp0, 1), 0.0)
     ds = f0 * jnp.where(wet01, s1 - s0, 0.0) - 0.0125 * slope
     ds = jnp.where(wet0, ds, 0.0)
-    tr[...] = inward[half:]
     ur[...] = ds[half:]
     vr0[...] = dn[half:]
     vr1[...] = dn2[half:]
 
-    for g, x in enumerate(
-        (dn2[levels:half], dn[levels:half], dn[:levels], dn2[:levels],
-         inward[levels:half], inward[:levels], ds[levels:half], ds[:levels])
-    ):
-        turned[pl.ds(g, levels, stride=8), :] = x
-    turned[...] = turned[...].T
-    lane = iota((STRIP, cols), 1)
-    one, wide = (lane < 1) | (lane >= cols - 1), (lane < 2) | (lane >= cols - 2)
-    spots = ((one, cols - 1 - 4), (wide, cols - 2), (one, cols - 1 - 6))
-
-    tail = (8, cols)
-    sub = iota(tail, 0)
-    fields = ((t_in, t_out, tb), (u_in, u_out, ub), (v_in, v_out, vb))
-
-    def copy_out(n, k):
-        at = pl.ds(pl.multiple_of(k * rows, rows), rows)
-        return pltpu.make_async_copy(fields[n][2].at[at], fields[n][1].at[at], sem.at[n, k])
-
-    @pl.loop(0, levels)
-    def one_level(k):
-        base = pl.multiple_of(k * rows, rows)
-        for n, (part, _, buf) in enumerate(fields):
-            mask, to = spots[n]
-            by = (to - 8 * k) & (cols - 1)
-            for r in range(0, rows, STRIP):
-                at = pl.ds(base + r, STRIP)
-                moved = pltpu.roll(turned[pl.ds(r, STRIP), :], by, 1)
-                buf[at, :] = part[at, :] + jnp.where(mask, moved, 0.0)
-
-            def row_of(ref, s):
-                return jnp.broadcast_to(ref[pl.ds(s * levels + k, 1), :], tail)
-
-            for s, (near, far, begin) in enumerate(((0, 1, 0), (7, 6, rows - 8))):
-                add = jnp.where(sub == near, row_of((tr, ur, vr0)[n], s), 0.0)
-                if n == 2:
-                    add = jnp.where(sub == far, row_of(vr1, s), add)
-                at = pl.ds(base + begin, 8)
-                buf[at, :] = buf[at, :] + add
-            copy_out(n, k).start()
+    turn_columns(
+        turned, (dn2[levels:half], dn[levels:half], dn[:levels], dn2[:levels], ds[levels:half], ds[:levels])
+    )
+    all_levels(1, 2)
 
     @pl.loop(0, levels)
     def finish(k):
@@ -412,8 +446,9 @@
             here, north = m * lat_n + i, m * lat_n + i + 1
             cross += [(here, north), (north, here)]
         cross.append((m * lat_n + lat_n - 1, (lon_n - 1 - m) * lat_n + lat_n - 1))
+        cross.append((m * lat_n, m * lat_n))
+    rim_a = lax.ppermute(lat_a, "lat", lat_pairs)
     rim_b = lax.ppermute(lat_b, ("lon", "lat"), cross)
-    rim_a = lax.ppermute(lat_a, "lat", lat_pairs)
 
     fields = [x.reshape(stack) for x in (t, u, v, kd)]
     send_a, send_b, depth, drag_ends = pl.pallas_call(
@@ -425,45 +460,58 @@
         compiler_params=params,
         name="pack",
     )(*fields, water, strata, drag)
+    half = levels // 2
+    padded, flat = pltpu.VMEM((rows + 2 * PAD, cols), F32), pltpu.VMEM(plane, F32)
+    part = pltpu.VMEM((half * rows, cols), F32)
+    work = [padded, padded, flat, padded] * 2 + [padded] + [flat] * 4
+    cost = pl.CostEstimate(flops=50 * tall * cols, bytes_accessed=1 << 20, transcendentals=0)
+    *first, p_mid, up_mid = pl.pallas_call(
+        functools.partial(low_kernel, levels, half, STRIP),
+        out_shape=[part] * 3 + [padded, flat],
+        in_specs=[vmem] * 7,
+        out_specs=[vmem] * 5,
+        scratch_shapes=work,
+        compiler_params=params,
+        cost_estimate=cost,
+        name="inner_low",
+    )(*fields, depth, drag, coriolis)
     send_a, send_b = pl.pallas_call(
         functools.partial(corner_kernel, levels),
         out_shape=[pltpu.VMEM(message, F32)] * 2,
-        in_specs=[vmem] * 4,
+        in_specs=[vmem] * 5,
         out_specs=[vmem] * 2,
         compiler_params=params,
         name="corners",
-    )(send_a, send_b, rim_a, rim_b)
+    )(send_a, send_b, rim_b, rim_a, up_mid)
     lon_pairs = [(i, i ^ 1) for i in range(lon_n)]
     lon_cross = [(i, (i + 1) % lon_n if i % 2 else (i - 1) % lon_n) for i in range(lon_n)]
     recv_b = lax.ppermute(send_b, "lon", lon_cross)
     recv_a = lax.ppermute(send_a, "lon", lon_pairs)
 
-    padded = pltpu.VMEM((rows + 2 * PAD, cols), F32)
-    flat = pltpu.VMEM(plane, F32)
-    inner = pl.pallas_call(
-        functools.partial(inner_kernel, levels, 32),
-        out_shape=[pltpu.VMEM(stack, F32)] * 3,
-        in_specs=[vmem] * 7,
+    second = pl.pallas_call(
+        functools.partial(high_kernel, levels, half, STRIP),
+        out_shape=[part] * 3,
+        in_specs=[vmem] * 10,
         out_specs=[vmem] * 3,
-        scratch_shapes=[padded, padded, flat, padded, flat, flat, flat, flat, padded, flat],
+        scratch_shapes=[padded, flat] + work,
         compiler_params=params,
-        cost_estimate=pl.CostEstimate(flops=100 * tall * cols, bytes_accessed=1 << 20, transcendentals=0),
-        name="inner",
-    )(*fields, depth, drag, coriolis)
+        cost_estimate=cost,
+        name="inner_high",
+    )(*fields, depth, drag, coriolis, p_mid, up_mid, send_a)
 
     rim_pair = pltpu.VMEM((2 * levels, cols), F32)
     outs = pl.pallas_call(
         functools.partial(border_kernel, levels),
         out_shape=[jax.ShapeDtypeStruct(stack, F32)] * 3,
-        in_specs=[vmem] * 13,
+        in_specs=[vmem] * 16,
         out_specs=[hbm] * 3,
         scratch_shapes=[pltpu.VMEM(stack, F32)] * 3
         + [rim_pair] * 4
-        + [pltpu.VMEM(plane, F32)]
+        + [pltpu.VMEM(plane, F32)] * 2
         + [pltpu.SemaphoreType.DMA((3, levels))],
         compiler_params=params,
         name="border",
-    )(*inner, send_a, send_b, recv_a, recv_b, lat_a, lat_b, rim_a, rim_b, drag, drag_ends)
+    )(*first, *second, send_a, send_b, recv_a, recv_b, lat_a, lat_b, rim_a, rim_b, drag, drag_ends)
     return tuple(x.reshape(levels, rows, cols) for x in outs)
 
 

time: 24.8 us -> 22.8 us (0.919)
  starting transfers between devices: 11.8 us -> 8.52 us
  Pallas kernels: 11.5 us -> 12.3 us
  waiting for transfers between devices: 0.61 us -> 1.01 us
    ppermute x1, starting transfers between devices: 4.87 us -> 2.31 us  [on_device(): recv_b = lax.ppermute(send_b, 'lon', lon_cross)]
    pallas_call x1 -> x2, Pallas kernels: 4.98 us -> 6.29 us  [the longest x1 3.17 us: on_device(): pl.pallas_call(functools.partial(low_kernel, levels, half, STRIP), out_sh...]
    ppermute x1, waiting for transfers between devices: 0.01 us -> 1.01 us  [on_device(): recv_b = lax.ppermute(send_b, 'lon', lon_cross)]
    ppermute x1, starting transfers between devices: 0.71 us -> 0.01 us  [on_device(): recv_a = lax.ppermute(send_a, 'lon', lon_pairs)]
    ppermute x1, waiting for transfers between devices: 0.6 us -> 0.01 us  [on_device(): rim_b = lax.ppermute(lat_b, ('lon', 'lat'), cross)]
    pallas_call x1, Pallas kernels: 3.48 us -> 2.99 us  [on_device(): pl.pallas_call(functools.partial(border_kernel, levels), out_shape=[jax.S...]
  transfers between devices with their start and end apart: 4 -> 4, of which waited for: 1 -> 1; matrix products, arithmetic and copies ran while one was open for 0% -> 0% of each run, Pallas kernels for 26% -> 35%
where the time goes in v4:
time: 22.8 us; the launch traced here: 22.7 us
  Pallas kernels  12.3 us (54%)
  starting transfers between devices  8.52 us (37%)
  waiting for transfers between devices  1.01 us (4%)
  between operations  0.8 us (4%)
    ppermute x1, starting transfers between devices, on_device(): rim_b = lax.ppermute(lat_b, ('lon', 'lat'), cross)  6.13 us
    pallas_call x1, Pallas kernels, on_device(): pl.pallas_call(functools.partial(low_kernel, levels, half, STRIP), out_sh...  3.17 us
    pallas_call x1, Pallas kernels, on_device(): pl.pallas_call(functools.partial(high_kernel, levels, half, STRIP), out_s...  3.12 us
    pallas_call x1, Pallas kernels, on_device(): pl.pallas_call(functools.partial(border_kernel, levels), out_shape=[jax.S...  2.99 us
    ppermute x1, starting transfers between devices, on_device(): recv_b = lax.ppermute(send_b, 'lon', lon_cross)  2.31 us
    pallas_call x1, Pallas kernels, on_device(): pl.pallas_call(functools.partial(pack_kernel, levels), out_shape=[pltpu.V...  1.58 us
    pallas_call x1, Pallas kernels, on_device(): pl.pallas_call(functools.partial(rows_kernel, levels), out_shape=[pltpu.V...  1.35 us
    ppermute x1, waiting for transfers between devices, on_device(): recv_b = lax.ppermute(send_b, 'lon', lon_cross)  1.01 us
  transfers between devices with their start and end apart: 4, of which 1 were waited for; matrix products, arithmetic and copies ran while one was open for 0% of the time, Pallas kernels for 35%

profile of v4, /device:TPU:2, one launch (start us, length us, event | category | flops | bytes accessed | tf_op | source)
XLA Modules:
  0.0 22.7 jit_solution(6807941132314155702)
XLA Ops:
  0.6 0.0 copy-start
  0.6 0.0 copy-start.1
  0.7 0.0 copy-start.2
  0.7 0.0 copy-start.3
  0.7 0.0 copy-start.4
  0.7 0.0 copy-start.5
  0.7 1.3 %rows.1 = (f32[128,1,128]{2,1,0:T(1,128)S(1)}, f32[128,1,128]{2,1,0:T(1,128)S(1)}, f32[128,128]{1,0:T(8,128)S(1)}, f32[128,128]{1,0:T(8,128)S(1)}) custom-call(f32[16,128,1,128]{3,2,1,0:T(1,128)} %bitcast.15, f32[16,128,1,128]{3,2,1,0:T(1,128)} %bitcast.19, f32[16,128,1,128]{3,2,1,0:T(1,128)} %bitcast.23, f32[16,128,1,128]{3,2,1,0:T(1,128)} %bitcast.27, ...), custom_call_target="tpu_custom_call" | custom-call | tf_op jit(solution)/shard_map/rows/pallas_call | solution.py:428
  2.0 0.1 collective-permute-start.1
  2.1 6.1 %collective-permute-start = (f32[128,128]{1,0:T(8,128)S(1)}, f32[128,128]{1,0:T(8,128)S(1)}, u32[]{:S(2)}, u32[]{:S(2)}) collective-permute-start(f32[128,128]{1,0:T(8,128)S(1)} %bitcast.35), channel_id=1, source_target_pairs={{1,31},{0,0},{3,29},{2,2},{5,27},{4,4},{7,25},{6,6},{9,23},{8,8},{... | collective-permute-start | bytes 196616 | tf_op jit(solution)/shard_map/ppermute | solution.py:451
  8.3 0.0 copy-done
  8.3 0.0 copy-done.1
  8.3 0.0 copy-done.2
  8.3 0.0 copy-done.3
  8.3 1.6 %pack.1 = (f32[128,128]{1,0:T(8,128)S(1)}, f32[128,128]{1,0:T(8,128)S(1)}, f32[128,128]{1,0:T(8,128)S(1)}, f32[8,128]{1,0:T(8,128)S(1)}) custom-call(f32[2048,128]{1,0:T(8,128)S(1)} %bitcast.16, f32[2048,128]{1,0:T(8,128)S(1)} %bitcast.20, f32[2048,128]{1,0:T(8,128)S(1)} %bitcast.24, f32[2048,128]{1,0:T(8,128)S(1)} %bitcast.28, s32[128,128]{1,0:T(8,128)S(1)} %copy-done.4, ...), custom_call_target="tpu_custom_call" | custom-call | tf_op jit(solution)/shard_map/pack/pallas_call | solution.py:454
  9.9 3.2 %inner_low.1 = (f32[1024,128]{1,0:T(8,128)S(1)}, f32[1024,128]{1,0:T(8,128)S(1)}, f32[1024,128]{1,0:T(8,128)S(1)}, f32[144,128]{1,0:T(8,128)S(1)}, f32[128,128]{1,0:T(8,128)S(1)}) custom-call(f32[2048,128]{1,0:T(8,128)S(1)} %bitcast.17, f32[2048,128]{1,0:T(8,128)S(1)} %bitcast.21, f32[2048,128]{1,0:T(8,128)S(1)} %bitcast.25, f32[2048,128]{1,0:T(8,128)S(1)} %bitcast.29, ...), custom_call_target="tpu_custom_call" | custom-call | flops 13107200 | bytes 1048576 | tf_op jit(solution)/shard_map/inner_low/pallas_call | solution.py:468
  13.1 0.0 collective-permute-done.1.rim_a
  13.1 0.0 collective-permute-done.rim_b
  13.1 0.1 corners.1
  13.2 2.3 %collective-permute-start.3 = (f32[128,128]{1,0:T(8,128)S(1)}, f32[128,128]{1,0:T(8,128)S(1)}, u32[]{:S(2)}, u32[]{:S(2)}) collective-permute-start(f32[128,128]{1,0:T(8,128)S(1)} %get-tuple-element.40.send_b), channel_id=1, source_target_pairs={{0,30},{2,4},{4,2},{6,8},{8,6},{10,12},{12,10},{14,16},{16,14},{18... | collective-permute-start | bytes 196616 | tf_op jit(solution)/shard_map/ppermute | solution.py:488
  15.5 0.0 collective-permute-start.2
  15.5 3.1 %inner_high.1 = (f32[1024,128]{1,0:T(8,128)S(1)}, f32[1024,128]{1,0:T(8,128)S(1)}, f32[1024,128]{1,0:T(8,128)S(1)}) custom-call(f32[2048,128]{1,0:T(8,128)S(1)} %bitcast.18, f32[2048,128]{1,0:T(8,128)S(1)} %bitcast.22, f32[2048,128]{1,0:T(8,128)S(1)} %bitcast.26, f32[2048,128]{1,0:T(8,128)S(1)} %bitcast.30, f32[128,128]{1,0:T(8,128)S(1)} %get-tuple-element.25.refs_4_, ...), custom_call_target="tpu_custom_call" | custom-call | flops 13107200 | bytes 1048576 | tf_op jit(solution)/shard_map/inner_high/pallas_call | solution.py:491
  18.7 1.0 %collective-permute-done.3.recv_b = f32[128,128]{1,0:T(8,128)S(1)} collective-permute-done((f32[128,128]{1,0:T(8,128)S(1)}, f32[128,128]{1,0:T(8,128)S(1)}, u32[]{:S(2)}, u32[]{:S(2)}) %collective-permute-start.3) | collective-permute-done | bytes 65568 | tf_op jit(solution)/shard_map/ppermute | solution.py:488
  19.7 0.0 collective-permute-done.2.recv_a
  19.7 3.0 %border.1 = (f32[2048,128]{1,0:T(8,128)}, f32[2048,128]{1,0:T(8,128)}, f32[2048,128]{1,0:T(8,128)}) custom-call(f32[1024,128]{1,0:T(8,128)S(1)} %get-tuple-element.27.t_low, f32[1024,128]{1,0:T(8,128)S(1)} %get-tuple-element.28.u_low, f32[1024,128]{1,0:T(8,128)S(1)} %get-tuple-element.29.v_low, f32[1024,128]{1,0:T(8,128)S(1)} %get-tuple-element.37.t_high, ...), custom_call_target="tpu_custom_call" | custom-call | tf_op jit(solution)/shard_map/border/pallas_call | solution.py:503
  (2 shorter events, 0.0 us)
Async XLA Ops:
  0.6 7.6 %copy-start = (f32[16,128,128]{2,1,0:T(8,128)S(1)}, f32[16,128,128]{2,1,0:T(8,128)}, u32[]{:S(2)}) copy-start(f32[16,128,128]{2,1,0:T(8,128)} %param.7) | copy-start | bytes 3145732
  0.6 7.6 %copy-start.1 = (f32[16,128,128]{2,1,0:T(8,128)S(1)}, f32[16,128,128]{2,1,0:T(8,128)}, u32[]{:S(2)}) copy-start(f32[16,128,128]{2,1,0:T(8,128)} %param.8) | copy-start | bytes 3145732
  0.7 7.6 %copy-start.2 = (f32[16,128,128]{2,1,0:T(8,128)S(1)}, f32[16,128,128]{2,1,0:T(8,128)}, u32[]{:S(2)}) copy-start(f32[16,128,128]{2,1,0:T(8,128)} %param.9) | copy-start | bytes 3145732
  0.7 7.6 %copy-start.3 = (f32[16,128,128]{2,1,0:T(8,128)S(1)}, f32[16,128,128]{2,1,0:T(8,128)}, u32[]{:S(2)}) copy-start(f32[16,128,128]{2,1,0:T(8,128)} %param.10) | copy-start | bytes 3145732
  0.7 7.6 %copy-start.4 = (s32[128,128]{1,0:T(8,128)S(1)}, s32[128,128]{1,0:T(8,128)}, u32[]{:S(2)}) copy-start(s32[128,128]{1,0:T(8,128)} %water.1) | copy-start | bytes 196612
  0.7 7.6 %copy-start.5 = (s32[128,128]{1,0:T(8,128)S(1)}, s32[128,128]{1,0:T(8,128)}, u32[]{:S(2)}) copy-start(s32[128,128]{1,0:T(8,128)} %strata.1) | copy-start | bytes 196612
  2.0 11.0 %collective-permute-start.1 = (f32[128,128]{1,0:T(8,128)S(1)}, f32[128,128]{1,0:T(8,128)S(1)}, u32[]{:S(2)}, u32[]{:S(2)}) collective-permute-start(f32[128,128]{1,0:T(8,128)S(1)} %bitcast.33), channel_id=1, source_target_pairs={{0,1},{1,0},{2,3},{3,2},{4,5},{5,4},{6,7},{7,6},{8,9},{9,8},{10,11... | collective-permute-start | bytes 196616 | tf_op jit(solution)/shard_map/ppermute | solution.py:450
  2.1 11.0 %collective-permute-start = (f32[128,128]{1,0:T(8,128)S(1)}, f32[128,128]{1,0:T(8,128)S(1)}, u32[]{:S(2)}, u32[]{:S(2)}) collective-permute-start(f32[128,128]{1,0:T(8,128)S(1)} %bitcast.35), channel_id=1, source_target_pairs={{1,31},{0,0},{3,29},{2,2},{5,27},{4,4},{7,25},{6,6},{9,23},{8,8},{... | collective-permute-start | bytes 196616 | tf_op jit(solution)/shard_map/ppermute | solution.py:451
  13.2 6.5 %collective-permute-start.3 = (f32[128,128]{1,0:T(8,128)S(1)}, f32[128,128]{1,0:T(8,128)S(1)}, u32[]{:S(2)}, u32[]{:S(2)}) collective-permute-start(f32[128,128]{1,0:T(8,128)S(1)} %get-tuple-element.40.send_b), channel_id=1, source_target_pairs={{0,30},{2,4},{4,2},{6,8},{8,6},{10,12},{12,10},{14,16},{16,14},{18... | collective-permute-start | bytes 196616 | tf_op jit(solution)/shard_map/ppermute | solution.py:488
  15.5 4.1 %collective-permute-start.2 = (f32[128,128]{1,0:T(8,128)S(1)}, f32[128,128]{1,0:T(8,128)S(1)}, u32[]{:S(2)}, u32[]{:S(2)}) collective-permute-start(f32[128,128]{1,0:T(8,128)S(1)} %get-tuple-element.36.refs_9_.send_a), channel_id=1, source_target_pairs={{0,2},{2,0},{4,6},{6,4},{8,10},{10,8},{12,14},{14,12},{16,18},{18,... | collective-permute-start | bytes 196616 | tf_op jit(solution)/shard_map/ppermute | solution.py:489

commit v5 on v4

--- a/solution.py
+++ b/solution.py
@@ -155,13 +155,12 @@
 def inner_kernel(
     levels, first, last, strip, t, u, v, kd, depth, drag, coriolis, p_in, up_in,
     t_out, u_out, v_out, p, up,
-    fn, gu, gv, back, fn2, gu2, gv2, back2, p2, de, dw, dn, dragn,
+    fn, gu, gv, back, de, dw, dn, dragn,
 ):
     rows, cols = depth.shape
     zero = jnp.zeros((PAD, cols), F32)
-    for ref in (fn, gu, back, fn2, gu2, back2, p2):
+    for ref in (fn, gu, back):
         ref[pl.ds(0, PAD), :] = zero
-    p2[pl.ds(PAD + rows, PAD), :] = zero
 
     shape = (strip, cols)
     lane = iota(shape, 1)
@@ -183,7 +182,7 @@
     up[...] = jnp.zeros(up.shape, F32) if p_in is None else up_in[...]
     p[...] = jnp.zeros(p.shape, F32) if p_in is None else p_in[...]
 
-    def one_level(k, before, p, fn, gu, gv, back):
+    def one_level(k):
         kf = k.astype(F32)
         base = pl.multiple_of(k * rows, rows)
         above = pl.multiple_of(jnp.minimum(k + 1, levels - 1) * rows, rows)
@@ -227,32 +226,26 @@
 
             t_next = jnp.where(wet, t0 + change, 0.0)
             t_out[out, :] = t_next
-            p[padded, :] = before[padded, :] + t_next
+            p[padded, :] = p[padded, :] + t_next
             c, f = coriolis[plane, :], drag[plane, :]
             u_out[out, :] = u0 + (c * v0 + f * lap_u)
             v_out[out, :] = v0 + (f * lap_v - c * u0)
 
-        def finish():
-            middle = pl.ds(PAD, rows)
-            back[middle, :] = 0.0125 * p[middle, :] - dragn[...] * gv[...]
-            for r in starts:
-                plane, out = pl.ds(r, strip), pl.ds(begin + r, strip)
-                wet = depth[plane, :] > kf
-                mid = p[pl.ds(PAD + r, strip), :]
-                slope = jnp.where(lane < cols - 1, lanes(mid, -1), 0.0) - jnp.where(lane > 0, lanes(mid, 1), 0.0)
-                u_next = u_out[out, :] - 0.0125 * slope
-                v_next = v_out[out, :] + back[pl.ds(PAD + r - 1, strip), :] - 0.0125 * p[pl.ds(PAD + r + 1, strip), :]
-                u_out[out, :] = jnp.where(wet, u_next, 0.0)
-                v_out[out, :] = jnp.where(wet, v_next, 0.0)
-
-        return finish
-
-    @pl.loop(first, last, step=2)
-    def two_levels(k):
-        finish = one_level(k, p, p2, fn, gu, gv, back)
-        finish2 = one_level(k + 1, p2, p, fn2, gu2, gv2, back2)
-        finish()
-        finish2()
+        middle = pl.ds(PAD, rows)
+        back[middle, :] = 0.0125 * p[middle, :] - dragn[...] * gv[...]
+        for r in starts:
+            plane, out = pl.ds(r, strip), pl.ds(begin + r, strip)
+            wet = depth[plane, :] > kf
+            mid = p[pl.ds(PAD + r, strip), :]
+            slope = jnp.where(lane < cols - 1, lanes(mid, -1), 0.0) - jnp.where(lane > 0, lanes(mid, 1), 0.0)
+            u_next = u_out[out, :] - 0.0125 * slope
+            v_next = v_out[out, :] + back[pl.ds(PAD + r - 1, strip), :] - 0.0125 * p[pl.ds(PAD + r + 1, strip), :]
+            u_out[out, :] = jnp.where(wet, u_next, 0.0)
+            v_out[out, :] = jnp.where(wet, v_next, 0.0)
+
+    @pl.loop(first, last)
+    def each_level(k):
+        one_level(k)
 
 
 def low_kernel(levels, half, strip, *refs):
@@ -446,7 +439,7 @@
             here, north = m * lat_n + i, m * lat_n + i + 1
             cross += [(here, north), (north, here)]
         cross.append((m * lat_n + lat_n - 1, (lon_n - 1 - m) * lat_n + lat_n - 1))
-        cross.append((m * lat_n, m * lat_n))
+        cross.append((m * lat_n, (m ^ 1) * lat_n))
     rim_a = lax.ppermute(lat_a, "lat", lat_pairs)
     rim_b = lax.ppermute(lat_b, ("lon", "lat"), cross)
 
@@ -463,7 +456,7 @@
     half = levels // 2
     padded, flat = pltpu.VMEM((rows + 2 * PAD, cols), F32), pltpu.VMEM(plane, F32)
     part = pltpu.VMEM((half * rows, cols), F32)
-    work = [padded, padded, flat, padded] * 2 + [padded] + [flat] * 4
+    work = [padded, padded, flat, padded] + [flat] * 4
     cost = pl.CostEstimate(flops=50 * tall * cols, bytes_accessed=1 << 20, transcendentals=0)
     *first, p_mid, up_mid = pl.pallas_call(
         functools.partial(low_kernel, levels, half, STRIP),

time: 22.8 us -> 20.4 us (0.89)
  starting transfers between devices: 8.52 us -> 7.18 us
  Pallas kernels: 12.3 us -> 11.4 us
    ppermute x1, starting transfers between devices: 6.13 us -> 4.24 us  [on_device(): rim_b = lax.ppermute(lat_b, ('lon', 'lat'), cross)]
    ppermute x1, starting transfers between devices: 2.31 us -> 2.86 us  [on_device(): recv_b = lax.ppermute(send_b, 'lon', lon_cross)]
    pallas_call x1, Pallas kernels: 3.17 us -> 2.66 us  [on_device(): pl.pallas_call(functools.partial(low_kernel, levels, half, STRIP), out_sh...]
    pallas_call x1, Pallas kernels: 3.12 us -> 2.68 us  [on_device(): pl.pallas_call(functools.partial(high_kernel, levels, half, STRIP), out_s...]
  transfers between devices with their start and end apart: 4 -> 4, of which waited for: 1 -> 1; matrix products, arithmetic and copies ran while one was open for 0% -> 0% of each run, Pallas kernels for 35% -> 34%
where the time goes in v5:
time: 20.4 us; the launch traced here: 20.2 us
  Pallas kernels  11.4 us (56%)
  starting transfers between devices  7.18 us (35%)
  waiting for transfers between devices  0.91 us (4%)
  between operations  0.76 us (4%)
    ppermute x1, starting transfers between devices, on_device(): rim_b = lax.ppermute(lat_b, ('lon', 'lat'), cross)  4.24 us
    pallas_call x1, Pallas kernels, on_device(): pl.pallas_call(functools.partial(border_kernel, levels), out_shape=[jax.S...  2.99 us
    ppermute x1, starting transfers between devices, on_device(): recv_b = lax.ppermute(send_b, 'lon', lon_cross)  2.86 us
    pallas_call x1, Pallas kernels, on_device(): pl.pallas_call(functools.partial(high_kernel, levels, half, STRIP), out_s...  2.68 us
    pallas_call x1, Pallas kernels, on_device(): pl.pallas_call(functools.partial(low_kernel, levels, half, STRIP), out_sh...  2.66 us
    pallas_call x1, Pallas kernels, on_device(): pl.pallas_call(functools.partial(pack_kernel, levels), out_shape=[pltpu.V...  1.58 us
    pallas_call x1, Pallas kernels, on_device(): pl.pallas_call(functools.partial(rows_kernel, levels), out_shape=[pltpu.V...  1.35 us
    ppermute x1, waiting for transfers between devices, on_device(): recv_b = lax.ppermute(send_b, 'lon', lon_cross)  0.9 us
  transfers between devices with their start and end apart: 4, of which 1 were waited for; matrix products, arithmetic and copies ran while one was open for 0% of the time, Pallas kernels for 34%

profile of v5, /device:TPU:2, one launch (start us, length us, event | category | flops | bytes accessed | tf_op | source)
XLA Modules:
  0.0 20.2 jit_solution(3680453419341431603)
XLA Ops:
  0.6 0.0 copy-start
  0.6 0.0 copy-start.1
  0.7 0.0 copy-start.2
  0.7 0.0 copy-start.3
  0.7 0.0 copy-start.4
  0.7 0.0 copy-start.5
  0.7 1.3 %rows.1 = (f32[128,1,128]{2,1,0:T(1,128)S(1)}, f32[128,1,128]{2,1,0:T(1,128)S(1)}, f32[128,128]{1,0:T(8,128)S(1)}, f32[128,128]{1,0:T(8,128)S(1)}) custom-call(f32[16,128,1,128]{3,2,1,0:T(1,128)} %bitcast.15, f32[16,128,1,128]{3,2,1,0:T(1,128)} %bitcast.19, f32[16,128,1,128]{3,2,1,0:T(1,128)} %bitcast.23, f32[16,128,1,128]{3,2,1,0:T(1,128)} %bitcast.27, ...), custom_call_target="tpu_custom_call" | custom-call | tf_op jit(solution)/shard_map/rows/pallas_call | solution.py:421
  2.0 0.1 collective-permute-start.1
  2.1 4.2 %collective-permute-start = (f32[128,128]{1,0:T(8,128)S(1)}, f32[128,128]{1,0:T(8,128)S(1)}, u32[]{:S(2)}, u32[]{:S(2)}) collective-permute-start(f32[128,128]{1,0:T(8,128)S(1)} %bitcast.35), channel_id=1, source_target_pairs={{1,31},{0,2},{3,29},{2,0},{5,27},{4,6},{7,25},{6,4},{9,23},{8,10},... | collective-permute-start | bytes 196616 | tf_op jit(solution)/shard_map/ppermute | solution.py:444
  6.4 0.0 copy-done
  6.4 0.0 copy-done.1
  6.4 0.0 copy-done.2
  6.4 0.0 copy-done.3
  6.4 1.6 %pack.1 = (f32[128,128]{1,0:T(8,128)S(1)}, f32[128,128]{1,0:T(8,128)S(1)}, f32[128,128]{1,0:T(8,128)S(1)}, f32[8,128]{1,0:T(8,128)S(1)}) custom-call(f32[2048,128]{1,0:T(8,128)S(1)} %bitcast.16, f32[2048,128]{1,0:T(8,128)S(1)} %bitcast.20, f32[2048,128]{1,0:T(8,128)S(1)} %bitcast.24, f32[2048,128]{1,0:T(8,128)S(1)} %bitcast.28, s32[128,128]{1,0:T(8,128)S(1)} %copy-done.4, ...), custom_call_target="tpu_custom_call" | custom-call | tf_op jit(solution)/shard_map/pack/pallas_call | solution.py:447
  8.0 2.7 %inner_low.1 = (f32[1024,128]{1,0:T(8,128)S(1)}, f32[1024,128]{1,0:T(8,128)S(1)}, f32[1024,128]{1,0:T(8,128)S(1)}, f32[144,128]{1,0:T(8,128)S(1)}, f32[128,128]{1,0:T(8,128)S(1)}) custom-call(f32[2048,128]{1,0:T(8,128)S(1)} %bitcast.17, f32[2048,128]{1,0:T(8,128)S(1)} %bitcast.21, f32[2048,128]{1,0:T(8,128)S(1)} %bitcast.25, f32[2048,128]{1,0:T(8,128)S(1)} %bitcast.29, ...), custom_call_target="tpu_custom_call" | custom-call | flops 13107200 | bytes 1048576 | tf_op jit(solution)/shard_map/inner_low/pallas_call | solution.py:461
  10.7 0.0 collective-permute-done.1.rim_a
  10.7 0.0 collective-permute-done.rim_b
  10.7 0.1 corners.1
  10.8 2.9 %collective-permute-start.3 = (f32[128,128]{1,0:T(8,128)S(1)}, f32[128,128]{1,0:T(8,128)S(1)}, u32[]{:S(2)}, u32[]{:S(2)}) collective-permute-start(f32[128,128]{1,0:T(8,128)S(1)} %get-tuple-element.40.send_b), channel_id=1, source_target_pairs={{0,30},{2,4},{4,2},{6,8},{8,6},{10,12},{12,10},{14,16},{16,14},{18... | collective-permute-start | bytes 196616 | tf_op jit(solution)/shard_map/ppermute | solution.py:481
  13.6 0.0 collective-permute-start.2
  13.7 2.7 %inner_high.1 = (f32[1024,128]{1,0:T(8,128)S(1)}, f32[1024,128]{1,0:T(8,128)S(1)}, f32[1024,128]{1,0:T(8,128)S(1)}) custom-call(f32[2048,128]{1,0:T(8,128)S(1)} %bitcast.18, f32[2048,128]{1,0:T(8,128)S(1)} %bitcast.22, f32[2048,128]{1,0:T(8,128)S(1)} %bitcast.26, f32[2048,128]{1,0:T(8,128)S(1)} %bitcast.30, f32[128,128]{1,0:T(8,128)S(1)} %get-tuple-element.25.refs_4_, ...), custom_call_target="tpu_custom_call" | custom-call | flops 13107200 | bytes 1048576 | tf_op jit(solution)/shard_map/inner_high/pallas_call | solution.py:484
  16.3 0.9 %collective-permute-done.3.recv_b = f32[128,128]{1,0:T(8,128)S(1)} collective-permute-done((f32[128,128]{1,0:T(8,128)S(1)}, f32[128,128]{1,0:T(8,128)S(1)}, u32[]{:S(2)}, u32[]{:S(2)}) %collective-permute-start.3) | collective-permute-done | bytes 65568 | tf_op jit(solution)/shard_map/ppermute | solution.py:481
  17.2 0.0 collective-permute-done.2.recv_a
  17.2 3.0 %border.1 = (f32[2048,128]{1,0:T(8,128)}, f32[2048,128]{1,0:T(8,128)}, f32[2048,128]{1,0:T(8,128)}) custom-call(f32[1024,128]{1,0:T(8,128)S(1)} %get-tuple-element.27.t_low, f32[1024,128]{1,0:T(8,128)S(1)} %get-tuple-element.28.u_low, f32[1024,128]{1,0:T(8,128)S(1)} %get-tuple-element.29.v_low, f32[1024,128]{1,0:T(8,128)S(1)} %get-tuple-element.37.t_high, ...), custom_call_target="tpu_custom_call" | custom-call | tf_op jit(solution)/shard_map/border/pallas_call | solution.py:496
  (2 shorter events, 0.0 us)
Async XLA Ops:
  0.6 5.7 %copy-start = (f32[16,128,128]{2,1,0:T(8,128)S(1)}, f32[16,128,128]{2,1,0:T(8,128)}, u32[]{:S(2)}) copy-start(f32[16,128,128]{2,1,0:T(8,128)} %param.7) | copy-start | bytes 3145732
  0.6 5.7 %copy-start.1 = (f32[16,128,128]{2,1,0:T(8,128)S(1)}, f32[16,128,128]{2,1,0:T(8,128)}, u32[]{:S(2)}) copy-start(f32[16,128,128]{2,1,0:T(8,128)} %param.8) | copy-start | bytes 3145732
  0.7 5.7 %copy-start.2 = (f32[16,128,128]{2,1,0:T(8,128)S(1)}, f32[16,128,128]{2,1,0:T(8,128)}, u32[]{:S(2)}) copy-start(f32[16,128,128]{2,1,0:T(8,128)} %param.9) | copy-start | bytes 3145732
  0.7 5.7 %copy-start.3 = (f32[16,128,128]{2,1,0:T(8,128)S(1)}, f32[16,128,128]{2,1,0:T(8,128)}, u32[]{:S(2)}) copy-start(f32[16,128,128]{2,1,0:T(8,128)} %param.10) | copy-start | bytes 3145732
  0.7 5.7 %copy-start.4 = (s32[128,128]{1,0:T(8,128)S(1)}, s32[128,128]{1,0:T(8,128)}, u32[]{:S(2)}) copy-start(s32[128,128]{1,0:T(8,128)} %water.1) | copy-start | bytes 196612
  0.7 5.7 %copy-start.5 = (s32[128,128]{1,0:T(8,128)S(1)}, s32[128,128]{1,0:T(8,128)}, u32[]{:S(2)}) copy-start(s32[128,128]{1,0:T(8,128)} %strata.1) | copy-start | bytes 196612
  2.0 8.6 %collective-permute-start.1 = (f32[128,128]{1,0:T(8,128)S(1)}, f32[128,128]{1,0:T(8,128)S(1)}, u32[]{:S(2)}, u32[]{:S(2)}) collective-permute-start(f32[128,128]{1,0:T(8,128)S(1)} %bitcast.33), channel_id=1, source_target_pairs={{0,1},{1,0},{2,3},{3,2},{4,5},{5,4},{6,7},{7,6},{8,9},{9,8},{10,11... | collective-permute-start | bytes 196616 | tf_op jit(solution)/shard_map/ppermute | solution.py:443
  2.1 8.5 %collective-permute-start = (f32[128,128]{1,0:T(8,128)S(1)}, f32[128,128]{1,0:T(8,128)S(1)}, u32[]{:S(2)}, u32[]{:S(2)}) collective-permute-start(f32[128,128]{1,0:T(8,128)S(1)} %bitcast.35), channel_id=1, source_target_pairs={{1,31},{0,2},{3,29},{2,0},{5,27},{4,6},{7,25},{6,4},{9,23},{8,10},... | collective-permute-start | bytes 196616 | tf_op jit(solution)/shard_map/ppermute | solution.py:444
  10.8 6.5 %collective-permute-start.3 = (f32[128,128]{1,0:T(8,128)S(1)}, f32[128,128]{1,0:T(8,128)S(1)}, u32[]{:S(2)}, u32[]{:S(2)}) collective-permute-start(f32[128,128]{1,0:T(8,128)S(1)} %get-tuple-element.40.send_b), channel_id=1, source_target_pairs={{0,30},{2,4},{4,2},{6,8},{8,6},{10,12},{12,10},{14,16},{16,14},{18... | collective-permute-start | bytes 196616 | tf_op jit(solution)/shard_map/ppermute | solution.py:481
  13.6 3.6 %collective-permute-start.2 = (f32[128,128]{1,0:T(8,128)S(1)}, f32[128,128]{1,0:T(8,128)S(1)}, u32[]{:S(2)}, u32[]{:S(2)}) collective-permute-start(f32[128,128]{1,0:T(8,128)S(1)} %get-tuple-element.36.refs_9_.send_a), channel_id=1, source_target_pairs={{0,2},{2,0},{4,6},{6,4},{8,10},{10,8},{12,14},{14,12},{16,18},{18,... | collective-permute-start | bytes 196616 | tf_op jit(solution)/shard_map/ppermute | solution.py:482

commit v6 on v4

--- a/solution.py
+++ b/solution.py
@@ -155,12 +155,14 @@
 def inner_kernel(
     levels, first, last, strip, t, u, v, kd, depth, drag, coriolis, p_in, up_in,
     t_out, u_out, v_out, p, up,
-    fn, gu, gv, back, fn2, gu2, gv2, back2, p2, de, dw, dn, dragn,
+    p2, de, dw, dn, dragn, *work,
 ):
     rows, cols = depth.shape
     zero = jnp.zeros((PAD, cols), F32)
-    for ref in (fn, gu, back, fn2, gu2, back2, p2):
-        ref[pl.ds(0, PAD), :] = zero
+    sets = work[:6], work[6:]
+    for fn, gu, _, back, _, _ in sets:
+        for ref in (fn, gu, back):
+            ref[pl.ds(0, PAD), :] = zero
     p2[pl.ds(PAD + rows, PAD), :] = zero
 
     shape = (strip, cols)
@@ -183,7 +185,7 @@
     up[...] = jnp.zeros(up.shape, F32) if p_in is None else up_in[...]
     p[...] = jnp.zeros(p.shape, F32) if p_in is None else p_in[...]
 
-    def one_level(k, before, p, fn, gu, gv, back):
+    def one_level(k, before, p, fn, gu, gv, back, us, vs):
         kf = k.astype(F32)
         base = pl.multiple_of(k * rows, rows)
         above = pl.multiple_of(jnp.minimum(k + 1, levels - 1) * rows, rows)
@@ -193,7 +195,9 @@
             plane, padded, below = pl.ds(r, strip), pl.ds(PAD + r, strip), pl.ds(PAD + r - 1, strip)
 
             def north_of(ref, mid):
-                return ref[pl.ds(base + r + 1, strip), :] if r + strip < rows else sublanes(mid, -1)
+                if r + strip == rows:
+                    return sublanes(mid, -1)
+                return ref[pl.ds(base + r, strip + 8), :][1 : strip + 1]
 
             d = depth[plane, :]
             t0, u0, v0, k0 = t[here, :], u[here, :], v[here, :], kd[here, :]
@@ -229,8 +233,8 @@
             t_out[out, :] = t_next
             p[padded, :] = before[padded, :] + t_next
             c, f = coriolis[plane, :], drag[plane, :]
-            u_out[out, :] = u0 + (c * v0 + f * lap_u)
-            v_out[out, :] = v0 + (f * lap_v - c * u0)
+            us[plane, :] = u0 + (c * v0 + f * lap_u)
+            vs[plane, :] = v0 + (f * lap_v - c * u0)
 
         def finish():
             middle = pl.ds(PAD, rows)
@@ -240,8 +244,8 @@
                 wet = depth[plane, :] > kf
                 mid = p[pl.ds(PAD + r, strip), :]
                 slope = jnp.where(lane < cols - 1, lanes(mid, -1), 0.0) - jnp.where(lane > 0, lanes(mid, 1), 0.0)
-                u_next = u_out[out, :] - 0.0125 * slope
-                v_next = v_out[out, :] + back[pl.ds(PAD + r - 1, strip), :] - 0.0125 * p[pl.ds(PAD + r + 1, strip), :]
+                u_next = us[plane, :] - 0.0125 * slope
+                v_next = vs[plane, :] + back[pl.ds(PAD + r - 1, strip), :] - 0.0125 * p[pl.ds(PAD + r + 1, strip), :]
                 u_out[out, :] = jnp.where(wet, u_next, 0.0)
                 v_out[out, :] = jnp.where(wet, v_next, 0.0)
 
@@ -249,8 +253,8 @@
 
     @pl.loop(first, last, step=2)
     def two_levels(k):
-        finish = one_level(k, p, p2, fn, gu, gv, back)
-        finish2 = one_level(k + 1, p2, p, fn2, gu2, gv2, back2)
+        finish = one_level(k, p, p2, *sets[0])
+        finish2 = one_level(k + 1, p2, p, *sets[1])
         finish()
         finish2()
 
@@ -446,7 +450,7 @@
             here, north = m * lat_n + i, m * lat_n + i + 1
             cross += [(here, north), (north, here)]
         cross.append((m * lat_n + lat_n - 1, (lon_n - 1 - m) * lat_n + lat_n - 1))
-        cross.append((m * lat_n, m * lat_n))
+        cross.append((m * lat_n, (m ^ 1) * lat_n))
     rim_a = lax.ppermute(lat_a, "lat", lat_pairs)
     rim_b = lax.ppermute(lat_b, ("lon", "lat"), cross)
 
@@ -463,7 +467,7 @@
     half = levels // 2
     padded, flat = pltpu.VMEM((rows + 2 * PAD, cols), F32), pltpu.VMEM(plane, F32)
     part = pltpu.VMEM((half * rows, cols), F32)
-    work = [padded, padded, flat, padded] * 2 + [padded] + [flat] * 4
+    work = [padded] + [flat] * 4 + [padded, padded, flat, padded, flat, flat] * 2
     cost = pl.CostEstimate(flops=50 * tall * cols, bytes_accessed=1 << 20, transcendentals=0)
     *first, p_mid, up_mid = pl.pallas_call(
         functools.partial(low_kernel, levels, half, STRIP),

time: 22.8 us -> 21 us (0.921)
  starting transfers between devices: 8.52 us -> 6.74 us
    ppermute x1, starting transfers between devices: 6.13 us -> 4.24 us  [on_device(): rim_b = lax.ppermute(lat_b, ('lon', 'lat'), cross)]
  transfers between devices with their start and end apart: 4 -> 4, of which waited for: 1 -> 1; matrix products, arithmetic and copies ran while one was open for 0% -> 0% of each run, Pallas kernels for 35% -> 38%
where the time goes in v6:
time: 21 us; the launch traced here: 20.7 us
  Pallas kernels  12.2 us (58%)
  starting transfers between devices  6.74 us (32%)
  waiting for transfers between devices  0.89 us (4%)
  between operations  0.77 us (4%)
    ppermute x1, starting transfers between devices, on_device(): rim_b = lax.ppermute(lat_b, ('lon', 'lat'), cross)  4.24 us
    pallas_call x1, Pallas kernels, on_device(): pl.pallas_call(functools.partial(high_kernel, levels, half, STRIP), out_s...  3.12 us
    pallas_call x1, Pallas kernels, on_device(): pl.pallas_call(functools.partial(low_kernel, levels, half, STRIP), out_sh...  3.09 us
    pallas_call x1, Pallas kernels, on_device(): pl.pallas_call(functools.partial(border_kernel, levels), out_shape=[jax.S...  2.99 us
    ppermute x1, starting transfers between devices, on_device(): recv_b = lax.ppermute(send_b, 'lon', lon_cross)  2.43 us
    pallas_call x1, Pallas kernels, on_device(): pl.pallas_call(functools.partial(pack_kernel, levels), out_shape=[pltpu.V...  1.58 us
    pallas_call x1, Pallas kernels, on_device(): pl.pallas_call(functools.partial(rows_kernel, levels), out_shape=[pltpu.V...  1.35 us
    ppermute x1, waiting for transfers between devices, on_device(): recv_b = lax.ppermute(send_b, 'lon', lon_cross)  0.89 us
  transfers between devices with their start and end apart: 4, of which 1 were waited for; matrix products, arithmetic and copies ran while one was open for 0% of the time, Pallas kernels for 38%

profile of v6, /device:TPU:2, one launch (start us, length us, event | category | flops | bytes accessed | tf_op | source)
XLA Modules:
  0.0 20.7 jit_solution(4455358779523656332)
XLA Ops:
  0.6 0.0 copy-start
  0.6 0.0 copy-start.1
  0.7 0.0 copy-start.2
  0.7 0.0 copy-start.3
  0.7 0.0 copy-start.4
  0.7 0.0 copy-start.5
  0.7 1.3 %rows.1 = (f32[128,1,128]{2,1,0:T(1,128)S(1)}, f32[128,1,128]{2,1,0:T(1,128)S(1)}, f32[128,128]{1,0:T(8,128)S(1)}, f32[128,128]{1,0:T(8,128)S(1)}) custom-call(f32[16,128,1,128]{3,2,1,0:T(1,128)} %bitcast.15, f32[16,128,1,128]{3,2,1,0:T(1,128)} %bitcast.19, f32[16,128,1,128]{3,2,1,0:T(1,128)} %bitcast.23, f32[16,128,1,128]{3,2,1,0:T(1,128)} %bitcast.27, ...), custom_call_target="tpu_custom_call" | custom-call | tf_op jit(solution)/shard_map/rows/pallas_call | solution.py:432
  2.0 0.1 collective-permute-start.1
  2.1 4.2 %collective-permute-start = (f32[128,128]{1,0:T(8,128)S(1)}, f32[128,128]{1,0:T(8,128)S(1)}, u32[]{:S(2)}, u32[]{:S(2)}) collective-permute-start(f32[128,128]{1,0:T(8,128)S(1)} %bitcast.35), channel_id=1, source_target_pairs={{1,31},{0,2},{3,29},{2,0},{5,27},{4,6},{7,25},{6,4},{9,23},{8,10},... | collective-permute-start | bytes 196616 | tf_op jit(solution)/shard_map/ppermute | solution.py:455
  6.4 0.0 copy-done
  6.4 0.0 copy-done.1
  6.4 0.0 copy-done.2
  6.4 0.0 copy-done.3
  6.4 1.6 %pack.1 = (f32[128,128]{1,0:T(8,128)S(1)}, f32[128,128]{1,0:T(8,128)S(1)}, f32[128,128]{1,0:T(8,128)S(1)}, f32[8,128]{1,0:T(8,128)S(1)}) custom-call(f32[2048,128]{1,0:T(8,128)S(1)} %bitcast.16, f32[2048,128]{1,0:T(8,128)S(1)} %bitcast.20, f32[2048,128]{1,0:T(8,128)S(1)} %bitcast.24, f32[2048,128]{1,0:T(8,128)S(1)} %bitcast.28, s32[128,128]{1,0:T(8,128)S(1)} %copy-done.4, ...), custom_call_target="tpu_custom_call" | custom-call | tf_op jit(solution)/shard_map/pack/pallas_call | solution.py:458
  8.0 3.1 %inner_low.1 = (f32[1024,128]{1,0:T(8,128)S(1)}, f32[1024,128]{1,0:T(8,128)S(1)}, f32[1024,128]{1,0:T(8,128)S(1)}, f32[144,128]{1,0:T(8,128)S(1)}, f32[128,128]{1,0:T(8,128)S(1)}) custom-call(f32[2048,128]{1,0:T(8,128)S(1)} %bitcast.17, f32[2048,128]{1,0:T(8,128)S(1)} %bitcast.21, f32[2048,128]{1,0:T(8,128)S(1)} %bitcast.25, f32[2048,128]{1,0:T(8,128)S(1)} %bitcast.29, ...), custom_call_target="tpu_custom_call" | custom-call | flops 13107200 | bytes 1048576 | tf_op jit(solution)/shard_map/inner_low/pallas_call | solution.py:472
  11.1 0.0 collective-permute-done.1.rim_a
  11.1 0.0 collective-permute-done.rim_b
  11.1 0.1 corners.1
  11.2 2.4 %collective-permute-start.3 = (f32[128,128]{1,0:T(8,128)S(1)}, f32[128,128]{1,0:T(8,128)S(1)}, u32[]{:S(2)}, u32[]{:S(2)}) collective-permute-start(f32[128,128]{1,0:T(8,128)S(1)} %get-tuple-element.40.send_b), channel_id=1, source_target_pairs={{0,30},{2,4},{4,2},{6,8},{8,6},{10,12},{12,10},{14,16},{16,14},{18... | collective-permute-start | bytes 196616 | tf_op jit(solution)/shard_map/ppermute | solution.py:492
  13.6 0.0 collective-permute-start.2
  13.7 3.1 %inner_high.1 = (f32[1024,128]{1,0:T(8,128)S(1)}, f32[1024,128]{1,0:T(8,128)S(1)}, f32[1024,128]{1,0:T(8,128)S(1)}) custom-call(f32[2048,128]{1,0:T(8,128)S(1)} %bitcast.18, f32[2048,128]{1,0:T(8,128)S(1)} %bitcast.22, f32[2048,128]{1,0:T(8,128)S(1)} %bitcast.26, f32[2048,128]{1,0:T(8,128)S(1)} %bitcast.30, f32[128,128]{1,0:T(8,128)S(1)} %get-tuple-element.25.refs_4_, ...), custom_call_target="tpu_custom_call" | custom-call | flops 13107200 | bytes 1048576 | tf_op jit(solution)/shard_map/inner_high/pallas_call | solution.py:495
  16.8 0.9 %collective-permute-done.3.recv_b = f32[128,128]{1,0:T(8,128)S(1)} collective-permute-done((f32[128,128]{1,0:T(8,128)S(1)}, f32[128,128]{1,0:T(8,128)S(1)}, u32[]{:S(2)}, u32[]{:S(2)}) %collective-permute-start.3) | collective-permute-done | bytes 65568 | tf_op jit(solution)/shard_map/ppermute | solution.py:492
  17.7 0.0 collective-permute-done.2.recv_a
  17.7 3.0 %border.1 = (f32[2048,128]{1,0:T(8,128)}, f32[2048,128]{1,0:T(8,128)}, f32[2048,128]{1,0:T(8,128)}) custom-call(f32[1024,128]{1,0:T(8,128)S(1)} %get-tuple-element.27.t_low, f32[1024,128]{1,0:T(8,128)S(1)} %get-tuple-element.28.u_low, f32[1024,128]{1,0:T(8,128)S(1)} %get-tuple-element.29.v_low, f32[1024,128]{1,0:T(8,128)S(1)} %get-tuple-element.37.t_high, ...), custom_call_target="tpu_custom_call" | custom-call | tf_op jit(solution)/shard_map/border/pallas_call | solution.py:507
  (2 shorter events, 0.0 us)
Async XLA Ops:
  0.6 5.7 %copy-start = (f32[16,128,128]{2,1,0:T(8,128)S(1)}, f32[16,128,128]{2,1,0:T(8,128)}, u32[]{:S(2)}) copy-start(f32[16,128,128]{2,1,0:T(8,128)} %param.7) | copy-start | bytes 3145732
  0.6 5.7 %copy-start.1 = (f32[16,128,128]{2,1,0:T(8,128)S(1)}, f32[16,128,128]{2,1,0:T(8,128)}, u32[]{:S(2)}) copy-start(f32[16,128,128]{2,1,0:T(8,128)} %param.8) | copy-start | bytes 3145732
  0.7 5.7 %copy-start.2 = (f32[16,128,128]{2,1,0:T(8,128)S(1)}, f32[16,128,128]{2,1,0:T(8,128)}, u32[]{:S(2)}) copy-start(f32[16,128,128]{2,1,0:T(8,128)} %param.9) | copy-start | bytes 3145732
  0.7 5.7 %copy-start.3 = (f32[16,128,128]{2,1,0:T(8,128)S(1)}, f32[16,128,128]{2,1,0:T(8,128)}, u32[]{:S(2)}) copy-start(f32[16,128,128]{2,1,0:T(8,128)} %param.10) | copy-start | bytes 3145732
  0.7 5.7 %copy-start.4 = (s32[128,128]{1,0:T(8,128)S(1)}, s32[128,128]{1,0:T(8,128)}, u32[]{:S(2)}) copy-start(s32[128,128]{1,0:T(8,128)} %water.1) | copy-start | bytes 196612
  0.7 5.7 %copy-start.5 = (s32[128,128]{1,0:T(8,128)S(1)}, s32[128,128]{1,0:T(8,128)}, u32[]{:S(2)}) copy-start(s32[128,128]{1,0:T(8,128)} %strata.1) | copy-start | bytes 196612
  2.0 9.0 %collective-permute-start.1 = (f32[128,128]{1,0:T(8,128)S(1)}, f32[128,128]{1,0:T(8,128)S(1)}, u32[]{:S(2)}, u32[]{:S(2)}) collective-permute-start(f32[128,128]{1,0:T(8,128)S(1)} %bitcast.33), channel_id=1, source_target_pairs={{0,1},{1,0},{2,3},{3,2},{4,5},{5,4},{6,7},{7,6},{8,9},{9,8},{10,11... | collective-permute-start | bytes 196616 | tf_op jit(solution)/shard_map/ppermute | solution.py:454
  2.1 9.0 %collective-permute-start = (f32[128,128]{1,0:T(8,128)S(1)}, f32[128,128]{1,0:T(8,128)S(1)}, u32[]{:S(2)}, u32[]{:S(2)}) collective-permute-start(f32[128,128]{1,0:T(8,128)S(1)} %bitcast.35), channel_id=1, source_target_pairs={{1,31},{0,2},{3,29},{2,0},{5,27},{4,6},{7,25},{6,4},{9,23},{8,10},... | collective-permute-start | bytes 196616 | tf_op jit(solution)/shard_map/ppermute | solution.py:455
  11.2 6.5 %collective-permute-start.3 = (f32[128,128]{1,0:T(8,128)S(1)}, f32[128,128]{1,0:T(8,128)S(1)}, u32[]{:S(2)}, u32[]{:S(2)}) collective-permute-start(f32[128,128]{1,0:T(8,128)S(1)} %get-tuple-element.40.send_b), channel_id=1, source_target_pairs={{0,30},{2,4},{4,2},{6,8},{8,6},{10,12},{12,10},{14,16},{16,14},{18... | collective-permute-start | bytes 196616 | tf_op jit(solution)/shard_map/ppermute | solution.py:492
  13.6 4.0 %collective-permute-start.2 = (f32[128,128]{1,0:T(8,128)S(1)}, f32[128,128]{1,0:T(8,128)S(1)}, u32[]{:S(2)}, u32[]{:S(2)}) collective-permute-start(f32[128,128]{1,0:T(8,128)S(1)} %get-tuple-element.36.refs_9_.send_a), channel_id=1, source_target_pairs={{0,2},{2,0},{4,6},{6,4},{8,10},{10,8},{12,14},{14,12},{16,18},{18,... | collective-permute-start | bytes 196616 | tf_op jit(solution)/shard_map/ppermute | solution.py:493

commit v7 on v5

--- a/solution.py
+++ b/solution.py
@@ -11,9 +11,9 @@
 GRAV = 0.1
 F32 = jnp.float32
 PAD = 8
-RIM = 128
-TAIL = 112
-CHUNK = 4
+RIM = 88
+TAIL = 80
+CHUNK = 8
 STRIP = 32
 
 
@@ -35,9 +35,18 @@
     return lax.axis_index(axis) % 2 == 0
 
 
+def face(side, ua, ub, ta, tb, ka, kb):
+    return side * (0.0625 * ((ua + ub) * (ta + tb))) - 0.125 * ((ka + kb) * (tb - ta))
+
+
+def square(x):
+    rows, cols = x.shape
+    return jnp.concatenate([x, jnp.zeros((cols - rows, cols), F32)], 0)
+
+
 def rows_kernel(
     levels, t, u, v, kd, water, strata, friction, lat_a, lat_b, coriolis, drag,
-    water_rows, strata_rows, sem, plane_sem, drag_sem,
+    far_rows, water_rows, strata_rows, sem, plane_sem, drag_sem,
 ):
     rows, cols = coriolis.shape
     copies, planes = [], []
@@ -50,17 +59,18 @@
             for m, (src, dst) in enumerate(((water, water_rows), (strata, strata_rows))):
                 at = dst.at[pl.ds(2 * side + n, 1)]
                 planes.append(pltpu.make_async_copy(src.at[pl.ds(row, 1)], at, plane_sem.at[m, side, n]))
-        for q, (src, row) in enumerate(
-            ((t, near), (t, far), (kd, near), (kd, far), (v, near), (v, far), (u, near))
-        ):
+        for q, src in enumerate((t, kd, v, u)):
             at = message.at[pl.ds(q * levels, levels)]
-            copies.append(pltpu.make_async_copy(src.at[:, row], at, sem.at[side, q]))
+            copies.append(pltpu.make_async_copy(src.at[:, near], at, sem.at[side, q]))
+        for q, src in enumerate((t, kd, v)):
+            copies.append(pltpu.make_async_copy(src.at[:, far], far_rows.at[side, q], sem.at[side, 4 + q]))
     whole = pltpu.make_async_copy(friction, drag, drag_sem)
     for copy in planes + copies + [whole]:
         copy.start()
-    row = iota((rows, cols), 0) + lax.axis_index("lat") * rows
+    row = iota((8, rows), 1) + lax.axis_index("lat") * rows
     total = rows * lax.axis_size("lat")
-    coriolis[...] = DT * jnp.sin(jnp.pi * ((row.astype(F32) + 0.5) / total - 0.5))
+    line = DT * jnp.sin(jnp.pi * ((row.astype(F32) + 0.5) / total - 0.5))
+    coriolis[...] = jnp.broadcast_to(line[0:1], (cols, rows)).T
     for copy in planes:
         copy.wait()
     for side, message in enumerate((lat_a, lat_b)):
@@ -72,6 +82,14 @@
     drag[...] = DT * drag[...]
     for copy in copies:
         copy.wait()
+    level = iota((levels, 1, cols), 0).astype(F32)
+    for side, message in enumerate((lat_a, lat_b)):
+        north = lat_even if side == 0 else jnp.logical_not(lat_even)
+        t1, k1, v1 = (message[pl.ds(q * levels, levels)] for q in range(3))
+        t2, k2, v2 = (far_rows[side, q] for q in range(3))
+        wet = level < jnp.minimum(message[pl.ds(TAIL, 1)], message[pl.ds(TAIL + 1, 1)])
+        flux = face(jnp.where(north, 1.0, -1.0), v2, v1, t2, t1, k2, k1)
+        message[pl.ds(4 * levels, levels)] = jnp.where(wet, flux, 0.0)
 
 
 def pack_kernel(
@@ -108,16 +126,20 @@
     drag_ends[...] = gathered[3, :, :].T[0:8]
 
     lon_even, lat_even = parity("lon"), parity("lat")
-    for q, (f, near) in enumerate(
-        ((0, True), (0, False), (1, True), (1, False), (2, True), (2, False), (3, True))
-    ):
-        first = (f // 2) * rows + 4 * (f % 2)
-        east = ends[pl.ds(first + (1 if near else 0), levels, stride=8), :]
-        west = ends[pl.ds(first + (2 if near else 3), levels, stride=8), :]
+
+    def line_of(f, c):
+        return ends[pl.ds((f // 2) * rows + 4 * (f % 2) + c, levels, stride=8), :]
+
+    def side_of(side, near, far):
+        t1, k1, u1, v1 = (line_of(f, near) for f in range(4))
+        t2, k2, u2 = (line_of(f, far) for f in range(3))
+        wet = iota((levels, cols), 0).astype(F32) < jnp.minimum(d[near : near + 1], d[far : far + 1])
+        return t1, k1, u1, v1, jnp.where(wet, face(side, u2, u1, t2, t1, k2, k1), 0.0)
+
+    for q, (east, west) in enumerate(zip(side_of(1.0, 1, 0), side_of(-1.0, 2, 3))):
         at = pl.ds(q * levels, levels)
         send_a[at, :] = jnp.where(lon_even, east, west)
         send_b[at, :] = jnp.where(lon_even, west, east)
-
     tail = (RIM - TAIL, cols)
     sub = iota(tail, 0)
 
@@ -135,10 +157,10 @@
     lon_even, lat_even = parity("lon"), parity("lat")
     a, b = rim_a[...], rim_b[...]
     b = jnp.where(lax.axis_index("lat") == 0, 0.0, b)
-    south, north = jnp.where(lat_even, b, a).T, jnp.where(lat_even, a, b).T
+    south, north = square(jnp.where(lat_even, b, a)).T, square(jnp.where(lat_even, a, b)).T
     is_top = lax.axis_index("lat") == lax.axis_size("lat") - 1
     line = iota((1, cols), 1)
-    turn = jnp.where((line >= 4 * levels) & (line < 7 * levels), -1.0, 1.0)
+    turn = jnp.where((line >= 2 * levels) & (line < 4 * levels), -1.0, 1.0)
     first, last = north[0:1], north[cols - 1 : cols]
     first, last = jnp.where(is_top, turn * last, first), jnp.where(is_top, turn * first, last)
     tail = (RIM - TAIL, cols)
@@ -276,10 +298,11 @@
     south = jnp.where(lax.axis_index("lat") == 0, 0.0, south)
 
     low, high = TAIL + 2, TAIL + 3
-    sw, nw = (west.T[:, n : n + 1] for n in (low, high))
-    se, ne = (east.T[:, n : n + 1] for n in (low, high))
+    ends_w, ends_e = square(west).T, square(east).T
+    sw, nw = (ends_w[:, n : n + 1] for n in (low, high))
+    se, ne = (ends_e[:, n : n + 1] for n in (low, high))
     line = iota((RIM, 1), 0)
-    turn = jnp.where((line >= 4 * levels) & (line < 7 * levels), -1.0, 1.0)
+    turn = jnp.where((line >= 2 * levels) & (line < 4 * levels), -1.0, 1.0)
     mirrored = turn * jnp.take_along_axis(north, cols - 1 - iota((RIM, cols), 1), axis=1)
     north = jnp.where(is_top, mirrored, north)
 
@@ -292,9 +315,9 @@
         return jnp.concatenate([jnp.broadcast_to(x, (levels, cols)) for x in rows_of_one], 0)
 
     outside, inside = (west, east, south, north), (own_w, own_e, own_s, own_n)
-    t1, t2, k1, k2, n1, n2, s1 = (stack(q, outside) for q in range(7))
-    t0, k0, n0, s0 = (stack(q, inside) for q in (0, 2, 4, 6))
-    d1, d2 = (lines([x[TAIL + n : TAIL + n + 1] for x in outside]) for n in (0, 1))
+    t1, k1, n1, s1, outer = (stack(q, outside) for q in range(5))
+    t0, k0, n0, s0 = (stack(q, inside) for q in range(4))
+    d1 = lines([x[TAIL : TAIL + 1] for x in outside])
     d0, d0b = (lines([x[TAIL + n : TAIL + n + 1] for x in inside]) for n in (0, 1))
     f0 = lines([drag_ends[2:3, :], drag_ends[1:2, :], drag[0:1, :], drag[rows - 1 : rows, :]])
     sub, lane = iota(four, 0), iota(four, 1)
@@ -302,13 +325,9 @@
     level = level_i.astype(F32)
     side = jnp.where((sub & levels) == 0, 1.0, -1.0)
     wet0, wet1 = level < d0, level < d1
-    wet01, wet12 = level < jnp.minimum(d0, d1), level < jnp.minimum(d1, d2)
-
-    def face(side, ua, ub, ta, tb, ka, kb):
-        return side * (0.0625 * ((ua + ub) * (ta + tb))) - 0.125 * ((ka + kb) * (tb - ta))
+    wet01 = level < jnp.minimum(d0, d1)
 
     inward = jnp.where(wet01, face(side, n1, n0, t1, t0, k1, k0), 0.0)
-    outer = jnp.where(wet12, face(side, n2, n1, t2, t1, k2, k1), 0.0)
 
     def turn_columns(ref, lines_of):
         for g, x in enumerate(lines_of):
@@ -371,8 +390,8 @@
         return jnp.where(lane == 0, lo, lanes(x, 1)), jnp.where(lane == cols - 1, hi, lanes(x, -1))
 
     t_w, t_e = beyond(t1, ((0, levels),) * 4)
-    k_w, k_e = beyond(k1, ((2 * levels, levels),) * 4)
-    s_w, s_e = beyond(s1, ((4 * levels, levels),) * 2 + ((6 * levels, levels),) * 2)
+    k_w, k_e = beyond(k1, ((levels, levels),) * 4)
+    s_w, s_e = beyond(s1, ((2 * levels, levels),) * 2 + ((3 * levels, levels),) * 2)
     d_w, d_e = beyond(d1, ((TAIL, 1),) * 4)
     flux_w = jnp.where(level < jnp.minimum(d_w, d1), face(1.0, s_w, s1, t_w, t1, k_w, k1), 0.0)
     flux_e = jnp.where(level < jnp.minimum(d1, d_e), face(1.0, s1, s_e, t1, t_e, k1, k_e), 0.0)
@@ -423,7 +442,8 @@
         out_shape=[pltpu.VMEM((RIM, 1, cols), F32)] * 2 + [pltpu.VMEM(plane, F32)] * 2,
         in_specs=[hbm] * 7,
         out_specs=[vmem] * 4,
-        scratch_shapes=[pltpu.VMEM((4, 1, cols), jnp.int32)] * 2
+        scratch_shapes=[pltpu.VMEM((2, 3, levels, 1, cols), F32)]
+        + [pltpu.VMEM((4, 1, cols), jnp.int32)] * 2
         + [pltpu.SemaphoreType.DMA((2, 7)), pltpu.SemaphoreType.DMA((2, 2, 2)), pltpu.SemaphoreType.DMA],
         compiler_params=params,
         name="rows",

time: 20.4 us -> 20 us (0.980)
  starting transfers between devices: 7.18 us -> 6.78 us
    ppermute x1, starting transfers between devices: 2.86 us -> 2.47 us  [on_device(): recv_b = lax.ppermute(send_b, 'lon', lon_cross)]
    pallas_call x1, Pallas kernels: 2.99 us -> 2.77 us  [on_device(): pl.pallas_call(functools.partial(border_kernel, levels), out_shape=[jax.S...]
  transfers between devices with their start and end apart: 4 -> 4, of which waited for: 1 -> 1; matrix products, arithmetic and copies ran while one was open for 0% -> 0% of each run, Pallas kernels for 34% -> 35%
where the time goes in v7:
time: 20 us; the launch traced here: 19.8 us
  Pallas kernels  11.2 us (56%)
  starting transfers between devices  6.78 us (34%)
  waiting for transfers between devices  1.08 us (5%)
  between operations  0.76 us (4%)
    ppermute x1, starting transfers between devices, on_device(): rim_b = lax.ppermute(lat_b, ('lon', 'lat'), cross)  4.24 us
    pallas_call x1, Pallas kernels, on_device(): pl.pallas_call(functools.partial(border_kernel, levels), out_shape=[jax.S...  2.77 us
    pallas_call x1, Pallas kernels, on_device(): pl.pallas_call(functools.partial(low_kernel, levels, half, STRIP), out_sh...  2.75 us
    pallas_call x1, Pallas kernels, on_device(): pl.pallas_call(functools.partial(high_kernel, levels, half, STRIP), out_s...  2.68 us
    ppermute x1, starting transfers between devices, on_device(): recv_b = lax.ppermute(send_b, 'lon', lon_cross)  2.47 us
    pallas_call x1, Pallas kernels, on_device(): pl.pallas_call(functools.partial(pack_kernel, levels), out_shape=[pltpu.V...  1.45 us
    pallas_call x1, Pallas kernels, on_device(): pl.pallas_call(functools.partial(rows_kernel, levels), out_shape=[pltpu.V...  1.41 us
    ppermute x1, waiting for transfers between devices, on_device(): recv_b = lax.ppermute(send_b, 'lon', lon_cross)  1.07 us
  transfers between devices with their start and end apart: 4, of which 1 were waited for; matrix products, arithmetic and copies ran while one was open for 0% of the time, Pallas kernels for 35%

profile of v7, /device:TPU:2, one launch (start us, length us, event | category | flops | bytes accessed | tf_op | source)
XLA Modules:
  0.0 19.8 jit_solution(14423097340957581490)
XLA Ops:
  0.6 0.0 copy-start
  0.6 0.0 copy-start.1
  0.7 0.0 copy-start.2
  0.7 0.0 copy-start.3
  0.7 0.0 copy-start.4
  0.7 0.0 copy-start.5
  0.7 1.4 %rows.1 = (f32[88,1,128]{2,1,0:T(1,128)S(1)}, f32[88,1,128]{2,1,0:T(1,128)S(1)}, f32[128,128]{1,0:T(8,128)S(1)}, f32[128,128]{1,0:T(8,128)S(1)}) custom-call(f32[16,128,1,128]{3,2,1,0:T(1,128)} %bitcast.15, f32[16,128,1,128]{3,2,1,0:T(1,128)} %bitcast.19, f32[16,128,1,128]{3,2,1,0:T(1,128)} %bitcast.23, f32[16,128,1,128]{3,2,1,0:T(1,128)} %bitcast.27, ...), custom_call_target="tpu_custom_call" | custom-call | tf_op jit(solution)/shard_map/rows/pallas_call | solution.py:440
  2.1 0.1 collective-permute-start.1
  2.2 4.2 %collective-permute-start = (f32[88,128]{1,0:T(8,128)S(1)}, f32[88,128]{1,0:T(8,128)S(1)}, u32[]{:S(2)}, u32[]{:S(2)}) collective-permute-start(f32[88,128]{1,0:T(8,128)S(1)} %bitcast.35), channel_id=1, source_target_pairs={{1,31},{0,2},{3,29},{2,0},{5,27},{4,6},{7,25},{6,4},{9,23},{8,10},... | collective-permute-start | bytes 135176 | tf_op jit(solution)/shard_map/ppermute | solution.py:464
  6.4 0.0 copy-done
  6.4 0.0 copy-done.1
  6.4 0.0 copy-done.2
  6.4 0.0 copy-done.3
  6.5 1.4 %pack.1 = (f32[88,128]{1,0:T(8,128)S(1)}, f32[88,128]{1,0:T(8,128)S(1)}, f32[128,128]{1,0:T(8,128)S(1)}, f32[8,128]{1,0:T(8,128)S(1)}) custom-call(f32[2048,128]{1,0:T(8,128)S(1)} %bitcast.16, f32[2048,128]{1,0:T(8,128)S(1)} %bitcast.20, f32[2048,128]{1,0:T(8,128)S(1)} %bitcast.24, f32[2048,128]{1,0:T(8,128)S(1)} %bitcast.28, s32[128,128]{1,0:T(8,128)S(1)} %copy-done.4, ...), custom_call_target="tpu_custom_call" | custom-call | tf_op jit(solution)/shard_map/pack/pallas_call | solution.py:467
  7.9 2.8 %inner_low.1 = (f32[1024,128]{1,0:T(8,128)S(1)}, f32[1024,128]{1,0:T(8,128)S(1)}, f32[1024,128]{1,0:T(8,128)S(1)}, f32[144,128]{1,0:T(8,128)S(1)}, f32[128,128]{1,0:T(8,128)S(1)}) custom-call(f32[2048,128]{1,0:T(8,128)S(1)} %bitcast.17, f32[2048,128]{1,0:T(8,128)S(1)} %bitcast.21, f32[2048,128]{1,0:T(8,128)S(1)} %bitcast.25, f32[2048,128]{1,0:T(8,128)S(1)} %bitcast.29, ...), custom_call_target="tpu_custom_call" | custom-call | flops 13107200 | bytes 1048576 | tf_op jit(solution)/shard_map/inner_low/pallas_call | solution.py:481
  10.7 0.0 collective-permute-done.1.rim_a
  10.7 0.0 collective-permute-done.rim_b
  10.7 0.1 corners.1
  10.8 2.5 %collective-permute-start.3 = (f32[88,128]{1,0:T(8,128)S(1)}, f32[88,128]{1,0:T(8,128)S(1)}, u32[]{:S(2)}, u32[]{:S(2)}) collective-permute-start(f32[88,128]{1,0:T(8,128)S(1)} %get-tuple-element.40.send_b), channel_id=1, source_target_pairs={{0,30},{2,4},{4,2},{6,8},{8,6},{10,12},{12,10},{14,16},{16,14},{18... | collective-permute-start | bytes 135176 | tf_op jit(solution)/shard_map/ppermute | solution.py:501
  13.3 0.0 collective-permute-start.2
  13.3 2.7 %inner_high.1 = (f32[1024,128]{1,0:T(8,128)S(1)}, f32[1024,128]{1,0:T(8,128)S(1)}, f32[1024,128]{1,0:T(8,128)S(1)}) custom-call(f32[2048,128]{1,0:T(8,128)S(1)} %bitcast.18, f32[2048,128]{1,0:T(8,128)S(1)} %bitcast.22, f32[2048,128]{1,0:T(8,128)S(1)} %bitcast.26, f32[2048,128]{1,0:T(8,128)S(1)} %bitcast.30, f32[128,128]{1,0:T(8,128)S(1)} %get-tuple-element.25.refs_4_, ...), custom_call_target="tpu_custom_call" | custom-call | flops 13107200 | bytes 1048576 | tf_op jit(solution)/shard_map/inner_high/pallas_call | solution.py:504
  16.0 1.1 %collective-permute-done.3.recv_b = f32[88,128]{1,0:T(8,128)S(1)} collective-permute-done((f32[88,128]{1,0:T(8,128)S(1)}, f32[88,128]{1,0:T(8,128)S(1)}, u32[]{:S(2)}, u32[]{:S(2)}) %collective-permute-start.3) | collective-permute-done | bytes 45088 | tf_op jit(solution)/shard_map/ppermute | solution.py:501
  17.0 0.0 collective-permute-done.2.recv_a
  17.0 2.8 %border.1 = (f32[2048,128]{1,0:T(8,128)}, f32[2048,128]{1,0:T(8,128)}, f32[2048,128]{1,0:T(8,128)}) custom-call(f32[1024,128]{1,0:T(8,128)S(1)} %get-tuple-element.27.t_low, f32[1024,128]{1,0:T(8,128)S(1)} %get-tuple-element.28.u_low, f32[1024,128]{1,0:T(8,128)S(1)} %get-tuple-element.29.v_low, f32[1024,128]{1,0:T(8,128)S(1)} %get-tuple-element.37.t_high, ...), custom_call_target="tpu_custom_call" | custom-call | tf_op jit(solution)/shard_map/border/pallas_call | solution.py:516
  (2 shorter events, 0.0 us)
Async XLA Ops:
  0.6 5.8 %copy-start = (f32[16,128,128]{2,1,0:T(8,128)S(1)}, f32[16,128,128]{2,1,0:T(8,128)}, u32[]{:S(2)}) copy-start(f32[16,128,128]{2,1,0:T(8,128)} %param.7) | copy-start | bytes 3145732
  0.6 5.8 %copy-start.1 = (f32[16,128,128]{2,1,0:T(8,128)S(1)}, f32[16,128,128]{2,1,0:T(8,128)}, u32[]{:S(2)}) copy-start(f32[16,128,128]{2,1,0:T(8,128)} %param.8) | copy-start | bytes 3145732
  0.7 5.8 %copy-start.2 = (f32[16,128,128]{2,1,0:T(8,128)S(1)}, f32[16,128,128]{2,1,0:T(8,128)}, u32[]{:S(2)}) copy-start(f32[16,128,128]{2,1,0:T(8,128)} %param.9) | copy-start | bytes 3145732
  0.7 5.8 %copy-start.3 = (f32[16,128,128]{2,1,0:T(8,128)S(1)}, f32[16,128,128]{2,1,0:T(8,128)}, u32[]{:S(2)}) copy-start(f32[16,128,128]{2,1,0:T(8,128)} %param.10) | copy-start | bytes 3145732
  0.7 5.8 %copy-start.4 = (s32[128,128]{1,0:T(8,128)S(1)}, s32[128,128]{1,0:T(8,128)}, u32[]{:S(2)}) copy-start(s32[128,128]{1,0:T(8,128)} %water.1) | copy-start | bytes 196612
  0.7 5.8 %copy-start.5 = (s32[128,128]{1,0:T(8,128)S(1)}, s32[128,128]{1,0:T(8,128)}, u32[]{:S(2)}) copy-start(s32[128,128]{1,0:T(8,128)} %strata.1) | copy-start | bytes 196612
  2.1 8.6 %collective-permute-start.1 = (f32[88,128]{1,0:T(8,128)S(1)}, f32[88,128]{1,0:T(8,128)S(1)}, u32[]{:S(2)}, u32[]{:S(2)}) collective-permute-start(f32[88,128]{1,0:T(8,128)S(1)} %bitcast.33), channel_id=1, source_target_pairs={{0,1},{1,0},{2,3},{3,2},{4,5},{5,4},{6,7},{7,6},{8,9},{9,8},{10,11... | collective-permute-start | bytes 135176 | tf_op jit(solution)/shard_map/ppermute | solution.py:463
  2.2 8.5 %collective-permute-start = (f32[88,128]{1,0:T(8,128)S(1)}, f32[88,128]{1,0:T(8,128)S(1)}, u32[]{:S(2)}, u32[]{:S(2)}) collective-permute-start(f32[88,128]{1,0:T(8,128)S(1)} %bitcast.35), channel_id=1, source_target_pairs={{1,31},{0,2},{3,29},{2,0},{5,27},{4,6},{7,25},{6,4},{9,23},{8,10},... | collective-permute-start | bytes 135176 | tf_op jit(solution)/shard_map/ppermute | solution.py:464
  10.8 6.2 %collective-permute-start.3 = (f32[88,128]{1,0:T(8,128)S(1)}, f32[88,128]{1,0:T(8,128)S(1)}, u32[]{:S(2)}, u32[]{:S(2)}) collective-permute-start(f32[88,128]{1,0:T(8,128)S(1)} %get-tuple-element.40.send_b), channel_id=1, source_target_pairs={{0,30},{2,4},{4,2},{6,8},{8,6},{10,12},{12,10},{14,16},{16,14},{18... | collective-permute-start | bytes 135176 | tf_op jit(solution)/shard_map/ppermute | solution.py:501
  13.3 3.8 %collective-permute-start.2 = (f32[88,128]{1,0:T(8,128)S(1)}, f32[88,128]{1,0:T(8,128)S(1)}, u32[]{:S(2)}, u32[]{:S(2)}) collective-permute-start(f32[88,128]{1,0:T(8,128)S(1)} %get-tuple-element.36.refs_9_.send_a), channel_id=1, source_target_pairs={{0,2},{2,0},{4,6},{6,4},{8,10},{10,8},{12,14},{14,12},{16,18},{18,... | collective-permute-start | bytes 135176 | tf_op jit(solution)/shard_map/ppermute | solution.py:502

commit v8 on v7

--- a/solution.py
+++ b/solution.py
@@ -208,9 +208,8 @@
         kf = k.astype(F32)
         base = pl.multiple_of(k * rows, rows)
         above = pl.multiple_of(jnp.minimum(k + 1, levels - 1) * rows, rows)
-        begin = pl.multiple_of((k - first) * rows, rows)
         for r in starts:
-            here, out = pl.ds(base + r, strip), pl.ds(begin + r, strip)
+            here = out = pl.ds(base + r, strip)
             plane, padded, below = pl.ds(r, strip), pl.ds(PAD + r, strip), pl.ds(PAD + r - 1, strip)
 
             def north_of(ref, mid):
@@ -256,7 +255,7 @@
         middle = pl.ds(PAD, rows)
         back[middle, :] = 0.0125 * p[middle, :] - dragn[...] * gv[...]
         for r in starts:
-            plane, out = pl.ds(r, strip), pl.ds(begin + r, strip)
+            plane, out = pl.ds(r, strip), pl.ds(base + r, strip)
             wet = depth[plane, :] > kf
             mid = p[pl.ds(PAD + r, strip), :]
             slope = jnp.where(lane < cols - 1, lanes(mid, -1), 0.0) - jnp.where(lane > 0, lanes(mid, 1), 0.0)
@@ -270,18 +269,38 @@
         one_level(k)
 
 
-def low_kernel(levels, half, strip, *refs):
-    inner_kernel(levels, 0, half, strip, *refs[:7], None, None, *refs[7:])
-
-
-def high_kernel(levels, half, strip, *refs):
-    inner_kernel(levels, half, levels, strip, *refs[:9], *refs[10:])
+def levels_before(levels):
+    lon, lat = lax.axis_index("lon"), lax.axis_index("lat")
+    is_top = lat == lax.axis_size("lat") - 1
+    is_last = lon == lax.axis_size("lon") - 1
+    some = jnp.where(jnp.logical_not(is_top) & is_last, 0, levels // 2)
+    some = jnp.where(is_top & (lon == 0), 3 * levels // 8, some)
+    return jnp.where(is_top & (lon == 1), 5 * levels // 8, some)
+
+
+def low_kernel(levels, strip, *refs):
+    inner_kernel(levels, 0, levels_before(levels), strip, *refs[:7], None, None, *refs[7:])
+
+
+def high_kernel(levels, strip, *refs):
+    inputs, (_, *low), outs, rest = refs[:9], refs[9:13], refs[13:16], refs[16:]
+    rows = refs[4].shape[0]
+    split = levels_before(levels)
+
+    @pl.loop(0, split)
+    def hand_on(k):
+        for src, dst in zip(low, outs):
+            for r in range(0, rows, strip):
+                at = pl.ds(pl.multiple_of(k * rows, rows) + r, strip)
+                dst[at, :] = src[at, :]
+
+    inner_kernel(levels, split, levels, strip, *inputs, *outs, *rest)
 
 
 def border_kernel(
-    levels, t_low, u_low, v_low, t_high, u_high, v_high,
+    levels, t_in, u_in, v_in,
     send_a, send_b, recv_a, recv_b, lat_a, lat_b, rim_a, rim_b, drag, drag_ends,
-    t_out, u_out, v_out, tb, ub, vb, tr, ur, vr0, vr1, turned, turned_t, sem,
+    t_out, u_out, v_out, tb, ub, vb, tr, ur, turned, turned_t, sem, end_sem,
 ):
     rows, cols = drag.shape
     lon_even, lat_even = parity("lon"), parity("lat")
@@ -337,45 +356,55 @@
     tail = (8, cols)
     sub8, lane8 = iota(tail, 0), iota((STRIP, cols), 1)
     one, wide = (lane8 < 1) | (lane8 >= cols - 1), (lane8 < 2) | (lane8 >= cols - 2)
-    spots = ((one, cols - 1), (wide, cols - 2), (one, cols - 1 - 4))
-    bufs, outs = (tb, ub, vb), (t_out, u_out, v_out)
-
-    def copy_out(n, k):
-        at = pl.ds(pl.multiple_of(k * rows, rows), rows)
-        return pltpu.make_async_copy(bufs[n].at[at], outs[n].at[at], sem.at[n, k])
-
-    def one_level(k, n, part, inside):
-        base, buf = pl.multiple_of(k * rows, rows), bufs[n]
-        mask, to = spots[n]
+    middle = pl.ds(8, rows - 16)
+
+    def add_columns(k, part, buf, ref, mask, to):
+        base = pl.multiple_of(k * rows, rows)
         by = (to - 8 * k) & (cols - 1)
         for r in range(0, rows, STRIP):
-            moved = pltpu.roll((turned_t if n == 0 else turned)[pl.ds(r, STRIP), :], by, 1)
-            old = part[pl.ds(pl.multiple_of(inside * rows, rows) + r, STRIP), :]
-            buf[pl.ds(base + r, STRIP), :] = old + jnp.where(mask, moved, 0.0)
-
-        def row_of(ref, s):
-            return jnp.broadcast_to(ref[pl.ds(s * levels + k, 1), :], tail)
-
-        for s, (near, far, begin) in enumerate(((0, 1, 0), (7, 6, rows - 8))):
-            add = jnp.where(sub8 == near, row_of((tr, ur, vr0)[n], s), 0.0)
-            if n == 2:
-                add = jnp.where(sub8 == far, row_of(vr1, s), add)
-            at = pl.ds(base + begin, 8)
-            buf[at, :] = buf[at, :] + add
-        copy_out(n, k).start()
-
-    def all_levels(*which):
-        for begin, parts in ((0, (t_low, u_low, v_low)), (levels // 2, (t_high, u_high, v_high))):
-
-            @pl.loop(0, levels // 2, step=CHUNK)
-            def some_of_them(k):
-                for i in range(CHUNK):
-                    for n in which:
-                        one_level(begin + k + i, n, parts[n], k + i)
-
+            moved = jnp.where(mask, pltpu.roll(ref[pl.ds(r, STRIP), :], by, 1), 0.0)
+            buf[k, pl.ds(r, STRIP), :] = part[pl.ds(base + r, STRIP), :] + moved
+
+    def add_rows(k, buf, ref):
+        for s, near, begin in ((0, 0, 0), (1, 7, rows - 8)):
+            line = jnp.broadcast_to(ref[pl.ds(s * levels + k, 1), :], tail)
+            at = pl.ds(begin, 8)
+            buf[k, at, :] = buf[k, at, :] + jnp.where(sub8 == near, line, 0.0)
+
+    def heat_out(k):
+        return pltpu.make_async_copy(tb.at[k], t_out.at[k], sem.at[0, k])
+
+    def east_out(k):
+        return pltpu.make_async_copy(ub.at[k], u_out.at[k], sem.at[1, k])
+
+    def north_out(k):
+        return pltpu.make_async_copy(vb.at[k, middle], v_out.at[k, middle], sem.at[2, k])
+
+    def north_ends(n):
+        at = pl.ds((0, rows - 8)[n], 8)
+        return pltpu.make_async_copy(vb.at[:, at], v_out.at[:, at], end_sem.at[n])
+
+    dp0 = inward
+    step = 1
+    while step < levels:
+        dp0 = dp0 + jnp.where(level_i >= step, sublanes(dp0, step), 0.0)
+        step *= 2
+    slope = jnp.where(lane < cols - 1, lanes(dp0, -1), 0.0) - jnp.where(lane > 0, lanes(dp0, 1), 0.0)
+    ds = f0 * jnp.where(wet01, s1 - s0, 0.0) - 0.0125 * slope
+    ds = jnp.where(wet0, ds, 0.0)
     tr[...] = inward[half:]
-    turn_columns(turned_t, (inward[levels:half], inward[:levels]))
-    all_levels(0)
+    ur[...] = ds[half:]
+    turn_columns(turned_t, (inward[levels:half], inward[:levels], ds[levels:half], ds[:levels]))
+
+    @pl.loop(0, levels, step=CHUNK)
+    def first_out(begin):
+        for i in range(CHUNK):
+            k = begin + i
+            add_columns(k, t_in, tb, turned_t, one, cols - 1)
+            add_rows(k, tb, tr)
+            heat_out(k).start()
+            add_columns(k, v_in, vb, turned_t, one, cols - 1 - 2)
+            north_out(k).start()
 
     before, after = (sw, se, sw, nw), (nw, ne, se, ne)
 
@@ -398,31 +427,35 @@
     rise = 0.125 * ((sublanes(k1, -1) + k1) * (sublanes(t1, -1) - t1))
     rise = jnp.where((level + 1.0 < d1) & (level_i < levels - 1), rise, 0.0)
     change = outer - inward + flux_w - flux_e + rise - sublanes(rise, 1)
-    p1, dp0 = jnp.where(wet1, t1 + change, 0.0), inward
+    p1 = jnp.where(wet1, t1 + change, 0.0)
     step = 1
     while step < levels:
         p1 = p1 + jnp.where(level_i >= step, sublanes(p1, step), 0.0)
-        dp0 = dp0 + jnp.where(level_i >= step, sublanes(dp0, step), 0.0)
         step *= 2
     dn = 0.0125 * (side * p1) + f0 * jnp.where(wet01, n1 - n0, 0.0)
     dn = jnp.where(wet0, dn, 0.0)
     dn2 = jnp.where(level < d0b, 0.0125 * (side * dp0), 0.0)
-    slope = jnp.where(lane < cols - 1, lanes(dp0, -1), 0.0) - jnp.where(lane > 0, lanes(dp0, 1), 0.0)
-    ds = f0 * jnp.where(wet01, s1 - s0, 0.0) - 0.0125 * slope
-    ds = jnp.where(wet0, ds, 0.0)
-    ur[...] = ds[half:]
-    vr0[...] = dn[half:]
-    vr1[...] = dn2[half:]
-
-    turn_columns(
-        turned, (dn2[levels:half], dn[levels:half], dn[:levels], dn2[:levels], ds[levels:half], ds[:levels])
-    )
-    all_levels(1, 2)
+    turn_columns(turned, (dn2[levels:half], dn[levels:half], dn[:levels], dn2[:levels]))
+    for row, x in ((0, dn[half : half + levels]), (1, dn2[half : half + levels]),
+                   (rows - 1, dn[half + levels :]), (rows - 2, dn2[half + levels :])):
+        vb[:, row, :] = vb[:, row, :] + x
+    for n in range(2):
+        north_ends(n).start()
+
+    @pl.loop(0, levels, step=CHUNK)
+    def last_out(begin):
+        for i in range(CHUNK):
+            add_columns(begin + i, u_in, ub, turned, wide, cols - 2)
+            add_rows(begin + i, ub, ur)
+            east_out(begin + i).start()
+
+    for n in range(2):
+        north_ends(n).wait()
 
     @pl.loop(0, levels)
     def finish(k):
-        for n in range(3):
-            copy_out(n, k).wait()
+        for out in (heat_out, north_out, east_out):
+            out(k).wait()
 
 
 def on_device(t, u, v, kd, friction, water, strata):
@@ -473,14 +506,13 @@
         compiler_params=params,
         name="pack",
     )(*fields, water, strata, drag)
-    half = levels // 2
     padded, flat = pltpu.VMEM((rows + 2 * PAD, cols), F32), pltpu.VMEM(plane, F32)
-    part = pltpu.VMEM((half * rows, cols), F32)
+    whole = pltpu.VMEM(stack, F32)
     work = [padded, padded, flat, padded] + [flat] * 4
     cost = pl.CostEstimate(flops=50 * tall * cols, bytes_accessed=1 << 20, transcendentals=0)
     *first, p_mid, up_mid = pl.pallas_call(
-        functools.partial(low_kernel, levels, half, STRIP),
-        out_shape=[part] * 3 + [padded, flat],
+        functools.partial(low_kernel, levels, STRIP),
+        out_shape=[whole] * 3 + [padded, flat],
         in_specs=[vmem] * 7,
         out_specs=[vmem] * 5,
         scratch_shapes=work,
@@ -502,30 +534,30 @@
     recv_a = lax.ppermute(send_a, "lon", lon_pairs)
 
     second = pl.pallas_call(
-        functools.partial(high_kernel, levels, half, STRIP),
-        out_shape=[part] * 3,
-        in_specs=[vmem] * 10,
+        functools.partial(high_kernel, levels, STRIP),
+        out_shape=[whole] * 3,
+        in_specs=[vmem] * 13,
         out_specs=[vmem] * 3,
         scratch_shapes=[padded, flat] + work,
         compiler_params=params,
         cost_estimate=cost,
         name="inner_high",
-    )(*fields, depth, drag, coriolis, p_mid, up_mid, send_a)
+    )(*fields, depth, drag, coriolis, p_mid, up_mid, send_a, *first)
 
     rim_pair = pltpu.VMEM((2 * levels, cols), F32)
     outs = pl.pallas_call(
         functools.partial(border_kernel, levels),
-        out_shape=[jax.ShapeDtypeStruct(stack, F32)] * 3,
-        in_specs=[vmem] * 16,
+        out_shape=[jax.ShapeDtypeStruct((levels, rows, cols), F32)] * 3,
+        in_specs=[vmem] * 13,
         out_specs=[hbm] * 3,
-        scratch_shapes=[pltpu.VMEM(stack, F32)] * 3
-        + [rim_pair] * 4
+        scratch_shapes=[pltpu.VMEM((levels, rows, cols), F32)] * 3
+        + [rim_pair] * 2
         + [pltpu.VMEM(plane, F32)] * 2
-        + [pltpu.SemaphoreType.DMA((3, levels))],
+        + [pltpu.SemaphoreType.DMA((3, levels)), pltpu.SemaphoreType.DMA((2,))],
         compiler_params=params,
         name="border",
-    )(*first, *second, send_a, send_b, recv_a, recv_b, lat_a, lat_b, rim_a, rim_b, drag, drag_ends)
-    return tuple(x.reshape(levels, rows, cols) for x in outs)
+    )(*second, send_a, send_b, recv_a, recv_b, lat_a, lat_b, rim_a, rim_b, drag, drag_ends)
+    return tuple(outs)
 
 
 def solution(mesh):

time: 20 us -> 19.7 us (0.985)
  waiting for transfers between devices: 1.08 us -> 0.01 us
  starting transfers between devices: 6.78 us -> 7.47 us
    ppermute x1, waiting for transfers between devices: 1.07 us -> 0.01 us  [on_device(): recv_b = lax.ppermute(send_b, 'lon', lon_cross)]
    ppermute x1, starting transfers between devices: 2.47 us -> 3.15 us  [on_device(): recv_b = lax.ppermute(send_b, 'lon', lon_cross)]
  transfers between devices with their start and end apart: 4 -> 4, of which waited for: 1 -> 0; matrix products, arithmetic and copies ran while one was open for 0% -> 0% of each run, Pallas kernels for 35% -> 35%
where the time goes in v8:
time: 19.7 us; the launch traced here: 19.6 us
  Pallas kernels  11.3 us (57%)
  starting transfers between devices  7.47 us (38%)
  between operations  0.78 us (4%)
    ppermute x1, starting transfers between devices, on_device(): rim_b = lax.ppermute(lat_b, ('lon', 'lat'), cross)  4.24 us
    pallas_call x1, Pallas kernels, on_device(): pl.pallas_call(functools.partial(high_kernel, levels, STRIP), out_shape=[...  3.44 us
    ppermute x1, starting transfers between devices, on_device(): recv_b = lax.ppermute(send_b, 'lon', lon_cross)  3.15 us
    pallas_call x1, Pallas kernels, on_device(): pl.pallas_call(functools.partial(border_kernel, levels), out_shape=[jax.S...  2.85 us
    pallas_call x1, Pallas kernels, on_device(): pl.pallas_call(functools.partial(low_kernel, levels, STRIP), out_shape=[w...  2.07 us
    pallas_call x1, Pallas kernels, on_device(): pl.pallas_call(functools.partial(pack_kernel, levels), out_shape=[pltpu.V...  1.45 us
    pallas_call x1, Pallas kernels, on_device(): pl.pallas_call(functools.partial(rows_kernel, levels), out_shape=[pltpu.V...  1.41 us
  transfers between devices with their start and end apart: 4, of which 0 were waited for; matrix products, arithmetic and copies ran while one was open for 0% of the time, Pallas kernels for 35%

profile of v8, /device:TPU:2, one launch (start us, length us, event | category | flops | bytes accessed | tf_op | source)
XLA Modules:
  0.0 19.6 jit_solution(2108496210740337799)
XLA Ops:
  0.6 0.0 copy-start
  0.6 0.0 copy-start.1
  0.7 0.0 copy-start.2
  0.7 0.0 copy-start.3
  0.7 0.0 copy-start.4
  0.7 0.0 copy-start.5
  0.7 1.4 %rows.1 = (f32[88,1,128]{2,1,0:T(1,128)S(1)}, f32[88,1,128]{2,1,0:T(1,128)S(1)}, f32[128,128]{1,0:T(8,128)S(1)}, f32[128,128]{1,0:T(8,128)S(1)}) custom-call(f32[16,128,1,128]{3,2,1,0:T(1,128)} %bitcast.12, f32[16,128,1,128]{3,2,1,0:T(1,128)} %bitcast.16, f32[16,128,1,128]{3,2,1,0:T(1,128)} %bitcast.20, f32[16,128,1,128]{3,2,1,0:T(1,128)} %bitcast.24, ...), custom_call_target="tpu_custom_call" | custom-call | tf_op jit(solution)/shard_map/rows/pallas_call | solution.py:473
  2.1 0.1 collective-permute-start.1
  2.2 4.2 %collective-permute-start = (f32[88,128]{1,0:T(8,128)S(1)}, f32[88,128]{1,0:T(8,128)S(1)}, u32[]{:S(2)}, u32[]{:S(2)}) collective-permute-start(f32[88,128]{1,0:T(8,128)S(1)} %bitcast.32), channel_id=1, source_target_pairs={{1,31},{0,2},{3,29},{2,0},{5,27},{4,6},{7,25},{6,4},{9,23},{8,10},... | collective-permute-start | bytes 135176 | tf_op jit(solution)/shard_map/ppermute | solution.py:497
  6.4 0.0 copy-done
  6.4 0.0 copy-done.1
  6.4 0.0 copy-done.4
  6.5 0.0 copy-done.5
  6.5 1.4 %pack.1 = (f32[88,128]{1,0:T(8,128)S(1)}, f32[88,128]{1,0:T(8,128)S(1)}, f32[128,128]{1,0:T(8,128)S(1)}, f32[8,128]{1,0:T(8,128)S(1)}) custom-call(f32[2048,128]{1,0:T(8,128)S(1)} %bitcast.13, f32[2048,128]{1,0:T(8,128)S(1)} %bitcast.17, f32[2048,128]{1,0:T(8,128)S(1)} %bitcast.21, f32[2048,128]{1,0:T(8,128)S(1)} %bitcast.25, s32[128,128]{1,0:T(8,128)S(1)} %copy-done.4, ...), custom_call_target="tpu_custom_call" | custom-call | tf_op jit(solution)/shard_map/pack/pallas_call | solution.py:500
  7.9 2.1 %inner_low.1 = (f32[2048,128]{1,0:T(8,128)S(1)}, f32[2048,128]{1,0:T(8,128)S(1)}, f32[2048,128]{1,0:T(8,128)S(1)}, f32[144,128]{1,0:T(8,128)S(1)}, f32[128,128]{1,0:T(8,128)S(1)}) custom-call(f32[2048,128]{1,0:T(8,128)S(1)} %bitcast.14, f32[2048,128]{1,0:T(8,128)S(1)} %bitcast.18, f32[2048,128]{1,0:T(8,128)S(1)} %bitcast.22, f32[2048,128]{1,0:T(8,128)S(1)} %bitcast.26, ...), custom_call_target="tpu_custom_call" | custom-call | flops 13107200 | bytes 1048576 | tf_op jit(solution)/shard_map/inner_low/pallas_call | solution.py:513
  10.0 0.0 collective-permute-done.1.rim_a
  10.0 0.0 collective-permute-done.rim_b
  10.0 0.1 corners.1
  10.1 3.2 %collective-permute-start.3 = (f32[88,128]{1,0:T(8,128)S(1)}, f32[88,128]{1,0:T(8,128)S(1)}, u32[]{:S(2)}, u32[]{:S(2)}) collective-permute-start(f32[88,128]{1,0:T(8,128)S(1)} %get-tuple-element.37.send_b), channel_id=1, source_target_pairs={{0,30},{2,4},{4,2},{6,8},{8,6},{10,12},{12,10},{14,16},{16,14},{18... | collective-permute-start | bytes 135176 | tf_op jit(solution)/shard_map/ppermute | solution.py:533
  13.3 0.0 collective-permute-start.2
  13.3 3.4 %inner_high.1 = (f32[2048,128]{1,0:T(8,128)S(1)}, f32[2048,128]{1,0:T(8,128)S(1)}, f32[2048,128]{1,0:T(8,128)S(1)}) custom-call(f32[2048,128]{1,0:T(8,128)S(1)} %bitcast.15, f32[2048,128]{1,0:T(8,128)S(1)} %bitcast.19, f32[2048,128]{1,0:T(8,128)S(1)} %bitcast.23, f32[2048,128]{1,0:T(8,128)S(1)} %bitcast.27, f32[128,128]{1,0:T(8,128)S(1)} %get-tuple-element.22.refs_4_, ...), custom_call_target="tpu_custom_call" | custom-call | flops 13107200 | bytes 1048576 | tf_op jit(solution)/shard_map/inner_high/pallas_call | solution.py:536
  16.7 0.0 collective-permute-done.3.recv_b
  16.7 0.0 collective-permute-done.2.recv_a
  16.7 2.8 %border.1 = (f32[16,128,128]{2,1,0:T(8,128)}, f32[16,128,128]{2,1,0:T(8,128)}, f32[16,128,128]{2,1,0:T(8,128)}) custom-call(f32[2048,128]{1,0:T(8,128)S(1)} %get-tuple-element.34.t_in, f32[2048,128]{1,0:T(8,128)S(1)} %get-tuple-element.35.u_in, f32[2048,128]{1,0:T(8,128)S(1)} %get-tuple-element.36.v_in, f32[88,128]{1,0:T(8,128)S(1)} %get-tuple-element.30.refs_9_.send_a, ...), custom_call_target="tpu_custom_call" | custom-call | tf_op jit(solution)/shard_map/border/pallas_call | solution.py:548
  (2 shorter events, 0.0 us)
Async XLA Ops:
  0.6 5.8 %copy-start = (f32[16,128,128]{2,1,0:T(8,128)S(1)}, f32[16,128,128]{2,1,0:T(8,128)}, u32[]{:S(2)}) copy-start(f32[16,128,128]{2,1,0:T(8,128)} %param.7) | copy-start | bytes 3145732
  0.6 5.8 %copy-start.1 = (f32[16,128,128]{2,1,0:T(8,128)S(1)}, f32[16,128,128]{2,1,0:T(8,128)}, u32[]{:S(2)}) copy-start(f32[16,128,128]{2,1,0:T(8,128)} %param.8) | copy-start | bytes 3145732
  0.7 5.8 %copy-start.2 = (f32[16,128,128]{2,1,0:T(8,128)S(1)}, f32[16,128,128]{2,1,0:T(8,128)}, u32[]{:S(2)}) copy-start(f32[16,128,128]{2,1,0:T(8,128)} %param.9) | copy-start | bytes 3145732
  0.7 5.8 %copy-start.3 = (f32[16,128,128]{2,1,0:T(8,128)S(1)}, f32[16,128,128]{2,1,0:T(8,128)}, u32[]{:S(2)}) copy-start(f32[16,128,128]{2,1,0:T(8,128)} %param.10) | copy-start | bytes 3145732
  0.7 5.8 %copy-start.4 = (s32[128,128]{1,0:T(8,128)S(1)}, s32[128,128]{1,0:T(8,128)}, u32[]{:S(2)}) copy-start(s32[128,128]{1,0:T(8,128)} %water.1) | copy-start | bytes 196612
  0.7 5.8 %copy-start.5 = (s32[128,128]{1,0:T(8,128)S(1)}, s32[128,128]{1,0:T(8,128)}, u32[]{:S(2)}) copy-start(s32[128,128]{1,0:T(8,128)} %strata.1) | copy-start | bytes 196612
  2.1 7.9 %collective-permute-start.1 = (f32[88,128]{1,0:T(8,128)S(1)}, f32[88,128]{1,0:T(8,128)S(1)}, u32[]{:S(2)}, u32[]{:S(2)}) collective-permute-start(f32[88,128]{1,0:T(8,128)S(1)} %bitcast.30), channel_id=1, source_target_pairs={{0,1},{1,0},{2,3},{3,2},{4,5},{5,4},{6,7},{7,6},{8,9},{9,8},{10,11... | collective-permute-start | bytes 135176 | tf_op jit(solution)/shard_map/ppermute | solution.py:496
  2.2 7.8 %collective-permute-start = (f32[88,128]{1,0:T(8,128)S(1)}, f32[88,128]{1,0:T(8,128)S(1)}, u32[]{:S(2)}, u32[]{:S(2)}) collective-permute-start(f32[88,128]{1,0:T(8,128)S(1)} %bitcast.32), channel_id=1, source_target_pairs={{1,31},{0,2},{3,29},{2,0},{5,27},{4,6},{7,25},{6,4},{9,23},{8,10},... | collective-permute-start | bytes 135176 | tf_op jit(solution)/shard_map/ppermute | solution.py:497
  10.1 6.6 %collective-permute-start.3 = (f32[88,128]{1,0:T(8,128)S(1)}, f32[88,128]{1,0:T(8,128)S(1)}, u32[]{:S(2)}, u32[]{:S(2)}) collective-permute-start(f32[88,128]{1,0:T(8,128)S(1)} %get-tuple-element.37.send_b), channel_id=1, source_target_pairs={{0,30},{2,4},{4,2},{6,8},{8,6},{10,12},{12,10},{14,16},{16,14},{18... | collective-permute-start | bytes 135176 | tf_op jit(solution)/shard_map/ppermute | solution.py:533
  13.3 3.5 %collective-permute-start.2 = (f32[88,128]{1,0:T(8,128)S(1)}, f32[88,128]{1,0:T(8,128)S(1)}, u32[]{:S(2)}, u32[]{:S(2)}) collective-permute-start(f32[88,128]{1,0:T(8,128)S(1)} %get-tuple-element.30.refs_9_.send_a), channel_id=1, source_target_pairs={{0,2},{2,0},{4,6},{6,4},{8,10},{10,8},{12,14},{14,12},{16,18},{18,... | collective-permute-start | bytes 135176 | tf_op jit(solution)/shard_map/ppermute | solution.py:534

commit v9 on v7

--- a/solution.py
+++ b/solution.py
@@ -176,8 +176,8 @@
 
 def inner_kernel(
     levels, first, last, strip, t, u, v, kd, depth, drag, coriolis, p_in, up_in,
-    t_out, u_out, v_out, p, up,
-    fn, gu, gv, back, de, dw, dn, dragn,
+    t_out, u_out, v_out, p, up, de, dw, dn, dragn,
+    fn, gu, gv, back,
 ):
     rows, cols = depth.shape
     zero = jnp.zeros((PAD, cols), F32)
@@ -188,7 +188,7 @@
     lane = iota(shape, 1)
     row = iota(shape, 0)
     starts = range(0, rows, strip)
-    for r in starts:
+    for r in starts if p_in is None else ():
         here = pl.ds(r, strip)
         d, f = depth[here, :], drag[here, :]
         de[here, :] = jnp.where(lane < cols - 1, jnp.minimum(d, lanes(d, -1)), 0.0)
@@ -208,9 +208,8 @@
         kf = k.astype(F32)
         base = pl.multiple_of(k * rows, rows)
         above = pl.multiple_of(jnp.minimum(k + 1, levels - 1) * rows, rows)
-        begin = pl.multiple_of((k - first) * rows, rows)
         for r in starts:
-            here, out = pl.ds(base + r, strip), pl.ds(begin + r, strip)
+            here = out = pl.ds(base + r, strip)
             plane, padded, below = pl.ds(r, strip), pl.ds(PAD + r, strip), pl.ds(PAD + r - 1, strip)
 
             def north_of(ref, mid):
@@ -256,7 +255,7 @@
         middle = pl.ds(PAD, rows)
         back[middle, :] = 0.0125 * p[middle, :] - dragn[...] * gv[...]
         for r in starts:
-            plane, out = pl.ds(r, strip), pl.ds(begin + r, strip)
+            plane, out = pl.ds(r, strip), pl.ds(base + r, strip)
             wet = depth[plane, :] > kf
             mid = p[pl.ds(PAD + r, strip), :]
             slope = jnp.where(lane < cols - 1, lanes(mid, -1), 0.0) - jnp.where(lane > 0, lanes(mid, 1), 0.0)
@@ -270,16 +269,36 @@
         one_level(k)
 
 
-def low_kernel(levels, half, strip, *refs):
-    inner_kernel(levels, 0, half, strip, *refs[:7], None, None, *refs[7:])
-
-
-def high_kernel(levels, half, strip, *refs):
-    inner_kernel(levels, half, levels, strip, *refs[:9], *refs[10:])
+def levels_before(levels):
+    lon, lat = lax.axis_index("lon"), lax.axis_index("lat")
+    is_top = lat == lax.axis_size("lat") - 1
+    is_last = lon == lax.axis_size("lon") - 1
+    some = jnp.where(jnp.logical_not(is_top) & is_last, 0, levels // 2)
+    some = jnp.where(is_top & (lon == 0), 3 * levels // 8, some)
+    return jnp.where(is_top & (lon == 1), 5 * levels // 8, some)
+
+
+def low_kernel(levels, strip, *refs):
+    inner_kernel(levels, 0, levels_before(levels), strip, *refs[:7], None, None, *refs[7:])
+
+
+def high_kernel(levels, strip, *refs):
+    inputs, planes, (_, *low), outs, rest = refs[:9], refs[9:13], refs[13:17], refs[17:20], refs[20:]
+    rows = refs[4].shape[0]
+    split = levels_before(levels)
+
+    @pl.loop(0, split)
+    def hand_on(k):
+        for src, dst in zip(low, outs):
+            for r in range(0, rows, strip):
+                at = pl.ds(pl.multiple_of(k * rows, rows) + r, strip)
+                dst[at, :] = src[at, :]
+
+    inner_kernel(levels, split, levels, strip, *inputs, *outs, *rest[:2], *planes, *rest[2:])
 
 
 def border_kernel(
-    levels, t_low, u_low, v_low, t_high, u_high, v_high,
+    levels, t_in, u_in, v_in,
     send_a, send_b, recv_a, recv_b, lat_a, lat_b, rim_a, rim_b, drag, drag_ends,
     t_out, u_out, v_out, tb, ub, vb, tr, ur, vr0, vr1, turned, turned_t, sem,
 ):
@@ -341,16 +360,16 @@
     bufs, outs = (tb, ub, vb), (t_out, u_out, v_out)
 
     def copy_out(n, k):
-        at = pl.ds(pl.multiple_of(k * rows, rows), rows)
+        at = pl.ds(k * rows, rows)
         return pltpu.make_async_copy(bufs[n].at[at], outs[n].at[at], sem.at[n, k])
 
     def one_level(k, n, part, inside):
-        base, buf = pl.multiple_of(k * rows, rows), bufs[n]
+        base, buf = k * rows, bufs[n]
         mask, to = spots[n]
         by = (to - 8 * k) & (cols - 1)
         for r in range(0, rows, STRIP):
             moved = pltpu.roll((turned_t if n == 0 else turned)[pl.ds(r, STRIP), :], by, 1)
-            old = part[pl.ds(pl.multiple_of(inside * rows, rows) + r, STRIP), :]
+            old = part[pl.ds(inside * rows + r, STRIP), :]
             buf[pl.ds(base + r, STRIP), :] = old + jnp.where(mask, moved, 0.0)
 
         def row_of(ref, s):
@@ -365,13 +384,9 @@
         copy_out(n, k).start()
 
     def all_levels(*which):
-        for begin, parts in ((0, (t_low, u_low, v_low)), (levels // 2, (t_high, u_high, v_high))):
-
-            @pl.loop(0, levels // 2, step=CHUNK)
-            def some_of_them(k):
-                for i in range(CHUNK):
-                    for n in which:
-                        one_level(begin + k + i, n, parts[n], k + i)
+        for k in range(levels):
+            for n in which:
+                one_level(k, n, (t_in, u_in, v_in)[n], k)
 
     tr[...] = inward[half:]
     turn_columns(turned_t, (inward[levels:half], inward[:levels]))
@@ -419,8 +434,7 @@
     )
     all_levels(1, 2)
 
-    @pl.loop(0, levels)
-    def finish(k):
+    for k in range(levels):
         for n in range(3):
             copy_out(n, k).wait()
 
@@ -473,16 +487,15 @@
         compiler_params=params,
         name="pack",
     )(*fields, water, strata, drag)
-    half = levels // 2
     padded, flat = pltpu.VMEM((rows + 2 * PAD, cols), F32), pltpu.VMEM(plane, F32)
-    part = pltpu.VMEM((half * rows, cols), F32)
-    work = [padded, padded, flat, padded] + [flat] * 4
+    whole = pltpu.VMEM(stack, F32)
+    work = [padded, padded, flat, padded]
     cost = pl.CostEstimate(flops=50 * tall * cols, bytes_accessed=1 << 20, transcendentals=0)
-    *first, p_mid, up_mid = pl.pallas_call(
-        functools.partial(low_kernel, levels, half, STRIP),
-        out_shape=[part] * 3 + [padded, flat],
+    *first, p_mid, up_mid, de, dw, dn, dragn = pl.pallas_call(
+        functools.partial(low_kernel, levels, STRIP),
+        out_shape=[whole] * 3 + [padded] + [flat] * 5,
         in_specs=[vmem] * 7,
-        out_specs=[vmem] * 5,
+        out_specs=[vmem] * 9,
         scratch_shapes=work,
         compiler_params=params,
         cost_estimate=cost,
@@ -502,21 +515,21 @@
     recv_a = lax.ppermute(send_a, "lon", lon_pairs)
 
     second = pl.pallas_call(
-        functools.partial(high_kernel, levels, half, STRIP),
-        out_shape=[part] * 3,
-        in_specs=[vmem] * 10,
+        functools.partial(high_kernel, levels, STRIP),
+        out_shape=[whole] * 3,
+        in_specs=[vmem] * 17,
         out_specs=[vmem] * 3,
         scratch_shapes=[padded, flat] + work,
         compiler_params=params,
         cost_estimate=cost,
         name="inner_high",
-    )(*fields, depth, drag, coriolis, p_mid, up_mid, send_a)
+    )(*fields, depth, drag, coriolis, p_mid, up_mid, de, dw, dn, dragn, send_a, *first)
 
     rim_pair = pltpu.VMEM((2 * levels, cols), F32)
     outs = pl.pallas_call(
         functools.partial(border_kernel, levels),
         out_shape=[jax.ShapeDtypeStruct(stack, F32)] * 3,
-        in_specs=[vmem] * 16,
+        in_specs=[vmem] * 13,
         out_specs=[hbm] * 3,
         scratch_shapes=[pltpu.VMEM(stack, F32)] * 3
         + [rim_pair] * 4
@@ -524,7 +537,7 @@
         + [pltpu.SemaphoreType.DMA((3, levels))],
         compiler_params=params,
         name="border",
-    )(*first, *second, send_a, send_b, recv_a, recv_b, lat_a, lat_b, rim_a, rim_b, drag, drag_ends)
+    )(*second, send_a, send_b, recv_a, recv_b, lat_a, lat_b, rim_a, rim_b, drag, drag_ends)
     return tuple(x.reshape(levels, rows, cols) for x in outs)
 
 

time: 20 us -> 19.6 us (0.980)
  waiting for transfers between devices: 1.08 us -> 0.01 us
  starting transfers between devices: 6.78 us -> 7.43 us
    ppermute x1, waiting for transfers between devices: 1.07 us -> 0.01 us  [on_device(): recv_b = lax.ppermute(send_b, 'lon', lon_cross)]
    ppermute x1, starting transfers between devices: 2.47 us -> 3.11 us  [on_device(): recv_b = lax.ppermute(send_b, 'lon', lon_cross)]
  transfers between devices with their start and end apart: 4 -> 4, of which waited for: 1 -> 0; matrix products, arithmetic and copies ran while one was open for 0% -> 0% of each run, Pallas kernels for 35% -> 35%
where the time goes in v9:
time: 19.6 us; the launch traced here: 19.4 us
  Pallas kernels  11.2 us (57%)
  starting transfers between devices  7.43 us (38%)
  between operations  0.78 us (4%)
    ppermute x1, starting transfers between devices, on_device(): rim_b = lax.ppermute(lat_b, ('lon', 'lat'), cross)  4.24 us
    pallas_call x1, Pallas kernels, on_device(): pl.pallas_call(functools.partial(high_kernel, levels, STRIP), out_shape=[...  3.33 us
    ppermute x1, starting transfers between devices, on_device(): recv_b = lax.ppermute(send_b, 'lon', lon_cross)  3.11 us
    pallas_call x1, Pallas kernels, on_device(): pl.pallas_call(functools.partial(border_kernel, levels), out_shape=[jax.S...  2.78 us
    pallas_call x1, Pallas kernels, on_device(): pl.pallas_call(functools.partial(low_kernel, levels, STRIP), out_shape=[w...  2.11 us
    pallas_call x1, Pallas kernels, on_device(): pl.pallas_call(functools.partial(pack_kernel, levels), out_shape=[pltpu.V...  1.45 us
    pallas_call x1, Pallas kernels, on_device(): pl.pallas_call(functools.partial(rows_kernel, levels), out_shape=[pltpu.V...  1.41 us
  transfers between devices with their start and end apart: 4, of which 0 were waited for; matrix products, arithmetic and copies ran while one was open for 0% of the time, Pallas kernels for 35%

profile of v9, /device:TPU:2, one launch (start us, length us, event | category | flops | bytes accessed | tf_op | source)
XLA Modules:
  0.0 19.4 jit_solution(6385969286713699811)
XLA Ops:
  0.6 0.0 copy-start
  0.6 0.0 copy-start.1
  0.7 0.0 copy-start.2
  0.7 0.0 copy-start.3
  0.7 0.0 copy-start.4
  0.7 0.0 copy-start.5
  0.7 1.4 %rows.1 = (f32[88,1,128]{2,1,0:T(1,128)S(1)}, f32[88,1,128]{2,1,0:T(1,128)S(1)}, f32[128,128]{1,0:T(8,128)S(1)}, f32[128,128]{1,0:T(8,128)S(1)}) custom-call(f32[16,128,1,128]{3,2,1,0:T(1,128)} %bitcast.15, f32[16,128,1,128]{3,2,1,0:T(1,128)} %bitcast.19, f32[16,128,1,128]{3,2,1,0:T(1,128)} %bitcast.23, f32[16,128,1,128]{3,2,1,0:T(1,128)} %bitcast.27, ...), custom_call_target="tpu_custom_call" | custom-call | tf_op jit(solution)/shard_map/rows/pallas_call | solution.py:454
  2.1 0.1 collective-permute-start.1
  2.2 4.2 %collective-permute-start = (f32[88,128]{1,0:T(8,128)S(1)}, f32[88,128]{1,0:T(8,128)S(1)}, u32[]{:S(2)}, u32[]{:S(2)}) collective-permute-start(f32[88,128]{1,0:T(8,128)S(1)} %bitcast.35), channel_id=1, source_target_pairs={{1,31},{0,2},{3,29},{2,0},{5,27},{4,6},{7,25},{6,4},{9,23},{8,10},... | collective-permute-start | bytes 135176 | tf_op jit(solution)/shard_map/ppermute | solution.py:478
  6.4 0.0 copy-done
  6.4 0.0 copy-done.3
  6.4 0.0 copy-done.4
  6.5 0.0 copy-done.5
  6.5 1.4 %pack.1 = (f32[88,128]{1,0:T(8,128)S(1)}, f32[88,128]{1,0:T(8,128)S(1)}, f32[128,128]{1,0:T(8,128)S(1)}, f32[8,128]{1,0:T(8,128)S(1)}) custom-call(f32[2048,128]{1,0:T(8,128)S(1)} %bitcast.16, f32[2048,128]{1,0:T(8,128)S(1)} %bitcast.20, f32[2048,128]{1,0:T(8,128)S(1)} %bitcast.24, f32[2048,128]{1,0:T(8,128)S(1)} %bitcast.28, s32[128,128]{1,0:T(8,128)S(1)} %copy-done.4, ...), custom_call_target="tpu_custom_call" | custom-call | tf_op jit(solution)/shard_map/pack/pallas_call | solution.py:481
  7.9 2.1 %inner_low.1 = (f32[2048,128]{1,0:T(8,128)S(1)}, f32[2048,128]{1,0:T(8,128)S(1)}, f32[2048,128]{1,0:T(8,128)S(1)}, f32[144,128]{1,0:T(8,128)S(1)}, f32[128,128]{...) custom-call(f32[2048,128]{1,0:T(8,128)S(1)} %bitcast.17, ...), custom_call_target="tpu_custom_call" | custom-call | flops 13107200 | bytes 1048576 | tf_op jit(solution)/shard_map/inner_low/pallas_call | solution.py:494
  10.0 0.0 collective-permute-done.1.rim_a
  10.0 0.0 collective-permute-done.rim_b
  10.1 0.1 corners.1
  10.2 3.1 %collective-permute-start.3 = (f32[88,128]{1,0:T(8,128)S(1)}, f32[88,128]{1,0:T(8,128)S(1)}, u32[]{:S(2)}, u32[]{:S(2)}) collective-permute-start(f32[88,128]{1,0:T(8,128)S(1)} %get-tuple-element.48.send_b), channel_id=1, source_target_pairs={{0,30},{2,4},{4,2},{6,8},{8,6},{10,12},{12,10},{14,16},{16,14},{18... | collective-permute-start | bytes 135176 | tf_op jit(solution)/shard_map/ppermute | solution.py:514
  13.3 0.0 collective-permute-start.2
  13.3 3.3 %inner_high.1 = (f32[2048,128]{1,0:T(8,128)S(1)}, f32[2048,128]{1,0:T(8,128)S(1)}, f32[2048,128]{1,0:T(8,128)S(1)}) custom-call(f32[2048,128]{1,0:T(8,128)S(1)} %bitcast.18, f32[2048,128]{1,0:T(8,128)S(1)} %bitcast.22, f32[2048,128]{1,0:T(8,128)S(1)} %bitcast.26, f32[2048,128]{1,0:T(8,128)S(1)} %bitcast.30, f32[128,128]{1,0:T(8,128)S(1)} %get-tuple-element.29.refs_4_, ...), custom_call_target="tpu_custom_call" | custom-call | flops 13107200 | bytes 1048576 | tf_op jit(solution)/shard_map/inner_high/pallas_call | solution.py:517
  16.6 0.0 collective-permute-done.3.recv_b
  16.6 0.0 collective-permute-done.2.recv_a
  16.6 2.8 %border.1 = (f32[2048,128]{1,0:T(8,128)}, f32[2048,128]{1,0:T(8,128)}, f32[2048,128]{1,0:T(8,128)}) custom-call(f32[2048,128]{1,0:T(8,128)S(1)} %get-tuple-element.45.t_in, f32[2048,128]{1,0:T(8,128)S(1)} %get-tuple-element.46.u_in, f32[2048,128]{1,0:T(8,128)S(1)} %get-tuple-element.47.v_in, f32[88,128]{1,0:T(8,128)S(1)} %get-tuple-element.41.refs_13_.send_a, ...), custom_call_target="tpu_custom_call" | custom-call | tf_op jit(solution)/shard_map/border/pallas_call | solution.py:529
  (2 shorter events, 0.0 us)
Async XLA Ops:
  0.6 5.8 %copy-start = (f32[16,128,128]{2,1,0:T(8,128)S(1)}, f32[16,128,128]{2,1,0:T(8,128)}, u32[]{:S(2)}) copy-start(f32[16,128,128]{2,1,0:T(8,128)} %param.7) | copy-start | bytes 3145732
  0.6 5.8 %copy-start.1 = (f32[16,128,128]{2,1,0:T(8,128)S(1)}, f32[16,128,128]{2,1,0:T(8,128)}, u32[]{:S(2)}) copy-start(f32[16,128,128]{2,1,0:T(8,128)} %param.8) | copy-start | bytes 3145732
  0.7 5.8 %copy-start.2 = (f32[16,128,128]{2,1,0:T(8,128)S(1)}, f32[16,128,128]{2,1,0:T(8,128)}, u32[]{:S(2)}) copy-start(f32[16,128,128]{2,1,0:T(8,128)} %param.9) | copy-start | bytes 3145732
  0.7 5.8 %copy-start.3 = (f32[16,128,128]{2,1,0:T(8,128)S(1)}, f32[16,128,128]{2,1,0:T(8,128)}, u32[]{:S(2)}) copy-start(f32[16,128,128]{2,1,0:T(8,128)} %param.10) | copy-start | bytes 3145732
  0.7 5.8 %copy-start.4 = (s32[128,128]{1,0:T(8,128)S(1)}, s32[128,128]{1,0:T(8,128)}, u32[]{:S(2)}) copy-start(s32[128,128]{1,0:T(8,128)} %water.1) | copy-start | bytes 196612
  0.7 5.8 %copy-start.5 = (s32[128,128]{1,0:T(8,128)S(1)}, s32[128,128]{1,0:T(8,128)}, u32[]{:S(2)}) copy-start(s32[128,128]{1,0:T(8,128)} %strata.1) | copy-start | bytes 196612
  2.1 7.9 %collective-permute-start.1 = (f32[88,128]{1,0:T(8,128)S(1)}, f32[88,128]{1,0:T(8,128)S(1)}, u32[]{:S(2)}, u32[]{:S(2)}) collective-permute-start(f32[88,128]{1,0:T(8,128)S(1)} %bitcast.33), channel_id=1, source_target_pairs={{0,1},{1,0},{2,3},{3,2},{4,5},{5,4},{6,7},{7,6},{8,9},{9,8},{10,11... | collective-permute-start | bytes 135176 | tf_op jit(solution)/shard_map/ppermute | solution.py:477
  2.2 7.9 %collective-permute-start = (f32[88,128]{1,0:T(8,128)S(1)}, f32[88,128]{1,0:T(8,128)S(1)}, u32[]{:S(2)}, u32[]{:S(2)}) collective-permute-start(f32[88,128]{1,0:T(8,128)S(1)} %bitcast.35), channel_id=1, source_target_pairs={{1,31},{0,2},{3,29},{2,0},{5,27},{4,6},{7,25},{6,4},{9,23},{8,10},... | collective-permute-start | bytes 135176 | tf_op jit(solution)/shard_map/ppermute | solution.py:478
  10.2 6.5 %collective-permute-start.3 = (f32[88,128]{1,0:T(8,128)S(1)}, f32[88,128]{1,0:T(8,128)S(1)}, u32[]{:S(2)}, u32[]{:S(2)}) collective-permute-start(f32[88,128]{1,0:T(8,128)S(1)} %get-tuple-element.48.send_b), channel_id=1, source_target_pairs={{0,30},{2,4},{4,2},{6,8},{8,6},{10,12},{12,10},{14,16},{16,14},{18... | collective-permute-start | bytes 135176 | tf_op jit(solution)/shard_map/ppermute | solution.py:514
  13.3 3.3 %collective-permute-start.2 = (f32[88,128]{1,0:T(8,128)S(1)}, f32[88,128]{1,0:T(8,128)S(1)}, u32[]{:S(2)}, u32[]{:S(2)}) collective-permute-start(f32[88,128]{1,0:T(8,128)S(1)} %get-tuple-element.41.refs_13_.send_a), channel_id=1, source_target_pairs={{0,2},{2,0},{4,6},{6,4},{8,10},{10,8},{12,14},{14,12},{16,18},{18,... | collective-permute-start | bytes 135176 | tf_op jit(solution)/shard_map/ppermute | solution.py:515

commit v10 on v9

--- a/solution.py
+++ b/solution.py
@@ -55,10 +55,9 @@
         north = lat_even if side == 0 else jnp.logical_not(lat_even)
         near = jnp.where(north, rows - 1, 0)
         far = jnp.where(north, rows - 2, 1)
-        for n, row in enumerate((near, far)):
-            for m, (src, dst) in enumerate(((water, water_rows), (strata, strata_rows))):
-                at = dst.at[pl.ds(2 * side + n, 1)]
-                planes.append(pltpu.make_async_copy(src.at[pl.ds(row, 1)], at, plane_sem.at[m, side, n]))
+        pair = pl.ds(jnp.where(north, rows - 2, 0), 2)
+        for m, (src, dst) in enumerate(((water, water_rows), (strata, strata_rows))):
+            planes.append(pltpu.make_async_copy(src.at[pair], dst.at[pl.ds(2 * side, 2)], plane_sem.at[m, side]))
         for q, src in enumerate((t, kd, v, u)):
             at = message.at[pl.ds(q * levels, levels)]
             copies.append(pltpu.make_async_copy(src.at[:, near], at, sem.at[side, q]))
@@ -75,9 +74,12 @@
         copy.wait()
     for side, message in enumerate((lat_a, lat_b)):
         message[pl.ds(TAIL + 2, RIM - TAIL - 2)] = jnp.zeros((RIM - TAIL - 2, 1, cols), F32)
-        for n in range(2):
-            at = pl.ds(2 * side + n, 1)
-            message[pl.ds(TAIL + n, 1)] = (water_rows[at] * strata_rows[at]).astype(F32)
+        north = lat_even if side == 0 else jnp.logical_not(lat_even)
+        first, second = (
+            (water_rows[pl.ds(2 * side + n, 1)] * strata_rows[pl.ds(2 * side + n, 1)]).astype(F32) for n in range(2)
+        )
+        message[pl.ds(TAIL, 1)] = jnp.where(north, second, first)
+        message[pl.ds(TAIL + 1, 1)] = jnp.where(north, first, second)
     whole.wait()
     drag[...] = DT * drag[...]
     for copy in copies:
@@ -316,10 +318,6 @@
     south, north = sides(lat_even, rim_a, rim_b)
     south = jnp.where(lax.axis_index("lat") == 0, 0.0, south)
 
-    low, high = TAIL + 2, TAIL + 3
-    ends_w, ends_e = square(west).T, square(east).T
-    sw, nw = (ends_w[:, n : n + 1] for n in (low, high))
-    se, ne = (ends_e[:, n : n + 1] for n in (low, high))
     line = iota((RIM, 1), 0)
     turn = jnp.where((line >= 2 * levels) & (line < 4 * levels), -1.0, 1.0)
     mirrored = turn * jnp.take_along_axis(north, cols - 1 - iota((RIM, cols), 1), axis=1)
@@ -360,16 +358,16 @@
     bufs, outs = (tb, ub, vb), (t_out, u_out, v_out)
 
     def copy_out(n, k):
-        at = pl.ds(k * rows, rows)
+        at = pl.ds(pl.multiple_of(k * rows, rows), rows)
         return pltpu.make_async_copy(bufs[n].at[at], outs[n].at[at], sem.at[n, k])
 
     def one_level(k, n, part, inside):
-        base, buf = k * rows, bufs[n]
+        base, buf = pl.multiple_of(k * rows, rows), bufs[n]
         mask, to = spots[n]
         by = (to - 8 * k) & (cols - 1)
         for r in range(0, rows, STRIP):
             moved = pltpu.roll((turned_t if n == 0 else turned)[pl.ds(r, STRIP), :], by, 1)
-            old = part[pl.ds(inside * rows + r, STRIP), :]
+            old = part[pl.ds(pl.multiple_of(inside * rows, rows) + r, STRIP), :]
             buf[pl.ds(base + r, STRIP), :] = old + jnp.where(mask, moved, 0.0)
 
         def row_of(ref, s):
@@ -384,14 +382,20 @@
         copy_out(n, k).start()
 
     def all_levels(*which):
-        for k in range(levels):
-            for n in which:
-                one_level(k, n, (t_in, u_in, v_in)[n], k)
+        @pl.loop(0, levels, step=CHUNK)
+        def some_of_them(k):
+            for i in range(CHUNK):
+                for n in which:
+                    one_level(k + i, n, (t_in, u_in, v_in)[n], k + i)
 
     tr[...] = inward[half:]
     turn_columns(turned_t, (inward[levels:half], inward[:levels]))
     all_levels(0)
 
+    low, high = TAIL + 2, TAIL + 3
+    ends_w, ends_e = square(west).T, square(east).T
+    sw, nw = (ends_w[:, n : n + 1] for n in (low, high))
+    se, ne = (ends_e[:, n : n + 1] for n in (low, high))
     before, after = (sw, se, sw, nw), (nw, ne, se, ne)
 
     def beyond(x, at):
@@ -434,7 +438,8 @@
     )
     all_levels(1, 2)
 
-    for k in range(levels):
+    @pl.loop(0, levels)
+    def finish(k):
         for n in range(3):
             copy_out(n, k).wait()
 
@@ -458,7 +463,7 @@
         out_specs=[vmem] * 4,
         scratch_shapes=[pltpu.VMEM((2, 3, levels, 1, cols), F32)]
         + [pltpu.VMEM((4, 1, cols), jnp.int32)] * 2
-        + [pltpu.SemaphoreType.DMA((2, 7)), pltpu.SemaphoreType.DMA((2, 2, 2)), pltpu.SemaphoreType.DMA],
+        + [pltpu.SemaphoreType.DMA((2, 7)), pltpu.SemaphoreType.DMA((2, 2)), pltpu.SemaphoreType.DMA],
         compiler_params=params,
         name="rows",
     )(

time: 19.6 us -> 19.5 us (level)
  transfers between devices with their start and end apart: 4 -> 4, of which waited for: 0 -> 0; matrix products, arithmetic and copies ran while one was open for 0% -> 0% of each run, Pallas kernels for 35% -> 36%
where the time goes in v10:
time: 19.5 us; the launch traced here: 19.3 us
  Pallas kernels  11.1 us (57%)
  starting transfers between devices  7.43 us (38%)
  between operations  0.78 us (4%)
    ppermute x1, starting transfers between devices, on_device(): rim_b = lax.ppermute(lat_b, ('lon', 'lat'), cross)  4.24 us
    pallas_call x1, Pallas kernels, on_device(): pl.pallas_call(functools.partial(high_kernel, levels, STRIP), out_shape=[...  3.33 us
    ppermute x1, starting transfers between devices, on_device(): recv_b = lax.ppermute(send_b, 'lon', lon_cross)  3.11 us
    pallas_call x1, Pallas kernels, on_device(): pl.pallas_call(functools.partial(border_kernel, levels), out_shape=[jax.S...  2.76 us
    pallas_call x1, Pallas kernels, on_device(): pl.pallas_call(functools.partial(low_kernel, levels, STRIP), out_shape=[w...  2.11 us
    pallas_call x1, Pallas kernels, on_device(): pl.pallas_call(functools.partial(pack_kernel, levels), out_shape=[pltpu.V...  1.45 us
    pallas_call x1, Pallas kernels, on_device(): pl.pallas_call(functools.partial(rows_kernel, levels), out_shape=[pltpu.V...  1.36 us
  transfers between devices with their start and end apart: 4, of which 0 were waited for; matrix products, arithmetic and copies ran while one was open for 0% of the time, Pallas kernels for 36%

profile of v10, /device:TPU:2, one launch (start us, length us, event | category | flops | bytes accessed | tf_op | source)
XLA Modules:
  0.0 19.3 jit_solution(8840346978377919136)
XLA Ops:
  0.6 0.0 copy-start
  0.6 0.0 copy-start.1
  0.7 0.0 copy-start.2
  0.7 0.0 copy-start.3
  0.7 0.0 copy-start.4
  0.7 0.0 copy-start.5
  0.7 1.4 %rows.1 = (f32[88,1,128]{2,1,0:T(1,128)S(1)}, f32[88,1,128]{2,1,0:T(1,128)S(1)}, f32[128,128]{1,0:T(8,128)S(1)}, f32[128,128]{1,0:T(8,128)S(1)}) custom-call(f32[16,128,1,128]{3,2,1,0:T(1,128)} %bitcast.15, f32[16,128,1,128]{3,2,1,0:T(1,128)} %bitcast.19, f32[16,128,1,128]{3,2,1,0:T(1,128)} %bitcast.23, f32[16,128,1,128]{3,2,1,0:T(1,128)} %bitcast.27, ...), custom_call_target="tpu_custom_call" | custom-call | tf_op jit(solution)/shard_map/rows/pallas_call | solution.py:459
  2.1 0.1 collective-permute-start.1
  2.1 4.2 %collective-permute-start = (f32[88,128]{1,0:T(8,128)S(1)}, f32[88,128]{1,0:T(8,128)S(1)}, u32[]{:S(2)}, u32[]{:S(2)}) collective-permute-start(f32[88,128]{1,0:T(8,128)S(1)} %bitcast.35), channel_id=1, source_target_pairs={{1,31},{0,2},{3,29},{2,0},{5,27},{4,6},{7,25},{6,4},{9,23},{8,10},... | collective-permute-start | bytes 135176 | tf_op jit(solution)/shard_map/ppermute | solution.py:483
  6.4 0.0 copy-done
  6.4 0.0 copy-done.1
  6.4 0.0 copy-done.2
  6.4 0.0 copy-done.3
  6.4 1.4 %pack.1 = (f32[88,128]{1,0:T(8,128)S(1)}, f32[88,128]{1,0:T(8,128)S(1)}, f32[128,128]{1,0:T(8,128)S(1)}, f32[8,128]{1,0:T(8,128)S(1)}) custom-call(f32[2048,128]{1,0:T(8,128)S(1)} %bitcast.16, f32[2048,128]{1,0:T(8,128)S(1)} %bitcast.20, f32[2048,128]{1,0:T(8,128)S(1)} %bitcast.24, f32[2048,128]{1,0:T(8,128)S(1)} %bitcast.28, s32[128,128]{1,0:T(8,128)S(1)} %copy-done.4, ...), custom_call_target="tpu_custom_call" | custom-call | tf_op jit(solution)/shard_map/pack/pallas_call | solution.py:486
  7.9 2.1 %inner_low.1 = (f32[2048,128]{1,0:T(8,128)S(1)}, f32[2048,128]{1,0:T(8,128)S(1)}, f32[2048,128]{1,0:T(8,128)S(1)}, f32[144,128]{1,0:T(8,128)S(1)}, f32[128,128]{...) custom-call(f32[2048,128]{1,0:T(8,128)S(1)} %bitcast.17, ...), custom_call_target="tpu_custom_call" | custom-call | flops 13107200 | bytes 1048576 | tf_op jit(solution)/shard_map/inner_low/pallas_call | solution.py:499
  10.0 0.0 collective-permute-done.1.rim_a
  10.0 0.0 collective-permute-done.rim_b
  10.0 0.1 corners.1
  10.1 3.1 %collective-permute-start.3 = (f32[88,128]{1,0:T(8,128)S(1)}, f32[88,128]{1,0:T(8,128)S(1)}, u32[]{:S(2)}, u32[]{:S(2)}) collective-permute-start(f32[88,128]{1,0:T(8,128)S(1)} %get-tuple-element.48.send_b), channel_id=1, source_target_pairs={{0,30},{2,4},{4,2},{6,8},{8,6},{10,12},{12,10},{14,16},{16,14},{18... | collective-permute-start | bytes 135176 | tf_op jit(solution)/shard_map/ppermute | solution.py:519
  13.2 0.0 collective-permute-start.2
  13.2 3.3 %inner_high.1 = (f32[2048,128]{1,0:T(8,128)S(1)}, f32[2048,128]{1,0:T(8,128)S(1)}, f32[2048,128]{1,0:T(8,128)S(1)}) custom-call(f32[2048,128]{1,0:T(8,128)S(1)} %bitcast.18, f32[2048,128]{1,0:T(8,128)S(1)} %bitcast.22, f32[2048,128]{1,0:T(8,128)S(1)} %bitcast.26, f32[2048,128]{1,0:T(8,128)S(1)} %bitcast.30, f32[128,128]{1,0:T(8,128)S(1)} %get-tuple-element.29.refs_4_, ...), custom_call_target="tpu_custom_call" | custom-call | flops 13107200 | bytes 1048576 | tf_op jit(solution)/shard_map/inner_high/pallas_call | solution.py:522
  16.6 0.0 collective-permute-done.3.recv_b
  16.6 0.0 collective-permute-done.2.recv_a
  16.6 2.8 %border.1 = (f32[2048,128]{1,0:T(8,128)}, f32[2048,128]{1,0:T(8,128)}, f32[2048,128]{1,0:T(8,128)}) custom-call(f32[2048,128]{1,0:T(8,128)S(1)} %get-tuple-element.45.t_in, f32[2048,128]{1,0:T(8,128)S(1)} %get-tuple-element.46.u_in, f32[2048,128]{1,0:T(8,128)S(1)} %get-tuple-element.47.v_in, f32[88,128]{1,0:T(8,128)S(1)} %get-tuple-element.41.refs_13_.send_a, ...), custom_call_target="tpu_custom_call" | custom-call | tf_op jit(solution)/shard_map/border/pallas_call | solution.py:534
  (2 shorter events, 0.0 us)
Async XLA Ops:
  0.6 5.7 %copy-start = (f32[16,128,128]{2,1,0:T(8,128)S(1)}, f32[16,128,128]{2,1,0:T(8,128)}, u32[]{:S(2)}) copy-start(f32[16,128,128]{2,1,0:T(8,128)} %param.7) | copy-start | bytes 3145732
  0.6 5.7 %copy-start.1 = (f32[16,128,128]{2,1,0:T(8,128)S(1)}, f32[16,128,128]{2,1,0:T(8,128)}, u32[]{:S(2)}) copy-start(f32[16,128,128]{2,1,0:T(8,128)} %param.8) | copy-start | bytes 3145732
  0.7 5.7 %copy-start.2 = (f32[16,128,128]{2,1,0:T(8,128)S(1)}, f32[16,128,128]{2,1,0:T(8,128)}, u32[]{:S(2)}) copy-start(f32[16,128,128]{2,1,0:T(8,128)} %param.9) | copy-start | bytes 3145732
  0.7 5.7 %copy-start.3 = (f32[16,128,128]{2,1,0:T(8,128)S(1)}, f32[16,128,128]{2,1,0:T(8,128)}, u32[]{:S(2)}) copy-start(f32[16,128,128]{2,1,0:T(8,128)} %param.10) | copy-start | bytes 3145732
  0.7 5.7 %copy-start.4 = (s32[128,128]{1,0:T(8,128)S(1)}, s32[128,128]{1,0:T(8,128)}, u32[]{:S(2)}) copy-start(s32[128,128]{1,0:T(8,128)} %water.1) | copy-start | bytes 196612
  0.7 5.7 %copy-start.5 = (s32[128,128]{1,0:T(8,128)S(1)}, s32[128,128]{1,0:T(8,128)}, u32[]{:S(2)}) copy-start(s32[128,128]{1,0:T(8,128)} %strata.1) | copy-start | bytes 196612
  2.1 7.9 %collective-permute-start.1 = (f32[88,128]{1,0:T(8,128)S(1)}, f32[88,128]{1,0:T(8,128)S(1)}, u32[]{:S(2)}, u32[]{:S(2)}) collective-permute-start(f32[88,128]{1,0:T(8,128)S(1)} %bitcast.33), channel_id=1, source_target_pairs={{0,1},{1,0},{2,3},{3,2},{4,5},{5,4},{6,7},{7,6},{8,9},{9,8},{10,11... | collective-permute-start | bytes 135176 | tf_op jit(solution)/shard_map/ppermute | solution.py:482
  2.1 7.9 %collective-permute-start = (f32[88,128]{1,0:T(8,128)S(1)}, f32[88,128]{1,0:T(8,128)S(1)}, u32[]{:S(2)}, u32[]{:S(2)}) collective-permute-start(f32[88,128]{1,0:T(8,128)S(1)} %bitcast.35), channel_id=1, source_target_pairs={{1,31},{0,2},{3,29},{2,0},{5,27},{4,6},{7,25},{6,4},{9,23},{8,10},... | collective-permute-start | bytes 135176 | tf_op jit(solution)/shard_map/ppermute | solution.py:483
  10.1 6.5 %collective-permute-start.3 = (f32[88,128]{1,0:T(8,128)S(1)}, f32[88,128]{1,0:T(8,128)S(1)}, u32[]{:S(2)}, u32[]{:S(2)}) collective-permute-start(f32[88,128]{1,0:T(8,128)S(1)} %get-tuple-element.48.send_b), channel_id=1, source_target_pairs={{0,30},{2,4},{4,2},{6,8},{8,6},{10,12},{12,10},{14,16},{16,14},{18... | collective-permute-start | bytes 135176 | tf_op jit(solution)/shard_map/ppermute | solution.py:519
  13.2 3.3 %collective-permute-start.2 = (f32[88,128]{1,0:T(8,128)S(1)}, f32[88,128]{1,0:T(8,128)S(1)}, u32[]{:S(2)}, u32[]{:S(2)}) collective-permute-start(f32[88,128]{1,0:T(8,128)S(1)} %get-tuple-element.41.refs_13_.send_a), channel_id=1, source_target_pairs={{0,2},{2,0},{4,6},{6,4},{8,10},{10,8},{12,14},{14,12},{16,18},{18,... | collective-permute-start | bytes 135176 | tf_op jit(solution)/shard_map/ppermute | solution.py:520

commit v11 on v10

--- a/solution.py
+++ b/solution.py
@@ -497,7 +497,7 @@
     work = [padded, padded, flat, padded]
     cost = pl.CostEstimate(flops=50 * tall * cols, bytes_accessed=1 << 20, transcendentals=0)
     *first, p_mid, up_mid, de, dw, dn, dragn = pl.pallas_call(
-        functools.partial(low_kernel, levels, STRIP),
+        functools.partial(low_kernel, levels, STRIP // 2),
         out_shape=[whole] * 3 + [padded] + [flat] * 5,
         in_specs=[vmem] * 7,
         out_specs=[vmem] * 9,
@@ -520,7 +520,7 @@
     recv_a = lax.ppermute(send_a, "lon", lon_pairs)
 
     second = pl.pallas_call(
-        functools.partial(high_kernel, levels, STRIP),
+        functools.partial(high_kernel, levels, STRIP // 2),
         out_shape=[whole] * 3,
         in_specs=[vmem] * 17,
         out_specs=[vmem] * 3,

time: 19.5 us -> 19.5 us (level)
  transfers between devices with their start and end apart: 4 -> 4, of which waited for: 0 -> 0; matrix products, arithmetic and copies ran while one was open for 0% -> 0% of each run, Pallas kernels for 36% -> 35%
where the time goes in v11:
time: 19.5 us; the launch traced here: 19.3 us
  Pallas kernels  11 us (56%)
  starting transfers between devices  7.49 us (38%)
  between operations  0.78 us (4%)
    ppermute x1, starting transfers between devices, on_device(): rim_b = lax.ppermute(lat_b, ('lon', 'lat'), cross)  4.24 us
    pallas_call x1, Pallas kernels, on_device(): pl.pallas_call(functools.partial(high_kernel, levels, STRIP // 2), out_sh...  3.3 us
    ppermute x1, starting transfers between devices, on_device(): recv_b = lax.ppermute(send_b, 'lon', lon_cross)  3.18 us
    pallas_call x1, Pallas kernels, on_device(): pl.pallas_call(functools.partial(border_kernel, levels), out_shape=[jax.S...  2.76 us
    pallas_call x1, Pallas kernels, on_device(): pl.pallas_call(functools.partial(low_kernel, levels, STRIP // 2), out_sha...  2.04 us
    pallas_call x1, Pallas kernels, on_device(): pl.pallas_call(functools.partial(pack_kernel, levels), out_shape=[pltpu.V...  1.45 us
    pallas_call x1, Pallas kernels, on_device(): pl.pallas_call(functools.partial(rows_kernel, levels), out_shape=[pltpu.V...  1.36 us
  transfers between devices with their start and end apart: 4, of which 0 were waited for; matrix products, arithmetic and copies ran while one was open for 0% of the time, Pallas kernels for 35%

profile of v11, /device:TPU:2, one launch (start us, length us, event | category | flops | bytes accessed | tf_op | source)
XLA Modules:
  0.0 19.3 jit_solution(890474330957324118)
XLA Ops:
  0.6 0.0 copy-start
  0.6 0.0 copy-start.1
  0.7 0.0 copy-start.2
  0.7 0.0 copy-start.3
  0.7 0.0 copy-start.4
  0.7 0.0 copy-start.5
  0.7 1.4 %rows.1 = (f32[88,1,128]{2,1,0:T(1,128)S(1)}, f32[88,1,128]{2,1,0:T(1,128)S(1)}, f32[128,128]{1,0:T(8,128)S(1)}, f32[128,128]{1,0:T(8,128)S(1)}) custom-call(f32[16,128,1,128]{3,2,1,0:T(1,128)} %bitcast.15, f32[16,128,1,128]{3,2,1,0:T(1,128)} %bitcast.19, f32[16,128,1,128]{3,2,1,0:T(1,128)} %bitcast.23, f32[16,128,1,128]{3,2,1,0:T(1,128)} %bitcast.27, ...), custom_call_target="tpu_custom_call" | custom-call | tf_op jit(solution)/shard_map/rows/pallas_call | solution.py:459
  2.1 0.1 collective-permute-start.1
  2.1 4.2 %collective-permute-start = (f32[88,128]{1,0:T(8,128)S(1)}, f32[88,128]{1,0:T(8,128)S(1)}, u32[]{:S(2)}, u32[]{:S(2)}) collective-permute-start(f32[88,128]{1,0:T(8,128)S(1)} %bitcast.35), channel_id=1, source_target_pairs={{1,31},{0,2},{3,29},{2,0},{5,27},{4,6},{7,25},{6,4},{9,23},{8,10},... | collective-permute-start | bytes 135176 | tf_op jit(solution)/shard_map/ppermute | solution.py:483
  6.4 0.0 copy-done
  6.4 0.0 copy-done.1
  6.4 0.0 copy-done.2
  6.4 0.0 copy-done.3
  6.4 1.4 %pack.1 = (f32[88,128]{1,0:T(8,128)S(1)}, f32[88,128]{1,0:T(8,128)S(1)}, f32[128,128]{1,0:T(8,128)S(1)}, f32[8,128]{1,0:T(8,128)S(1)}) custom-call(f32[2048,128]{1,0:T(8,128)S(1)} %bitcast.16, f32[2048,128]{1,0:T(8,128)S(1)} %bitcast.20, f32[2048,128]{1,0:T(8,128)S(1)} %bitcast.24, f32[2048,128]{1,0:T(8,128)S(1)} %bitcast.28, s32[128,128]{1,0:T(8,128)S(1)} %copy-done.4, ...), custom_call_target="tpu_custom_call" | custom-call | tf_op jit(solution)/shard_map/pack/pallas_call | solution.py:486
  7.9 2.0 %inner_low.1 = (f32[2048,128]{1,0:T(8,128)S(1)}, f32[2048,128]{1,0:T(8,128)S(1)}, f32[2048,128]{1,0:T(8,128)S(1)}, f32[144,128]{1,0:T(8,128)S(1)}, f32[128,128]{...) custom-call(f32[2048,128]{1,0:T(8,128)S(1)} %bitcast.17, ...), custom_call_target="tpu_custom_call" | custom-call | flops 13107200 | bytes 1048576 | tf_op jit(solution)/shard_map/inner_low/pallas_call | solution.py:499
  9.9 0.0 collective-permute-done.1.rim_a
  9.9 0.0 collective-permute-done.rim_b
  9.9 0.1 corners.1
  10.0 3.2 %collective-permute-start.3 = (f32[88,128]{1,0:T(8,128)S(1)}, f32[88,128]{1,0:T(8,128)S(1)}, u32[]{:S(2)}, u32[]{:S(2)}) collective-permute-start(f32[88,128]{1,0:T(8,128)S(1)} %get-tuple-element.48.send_b), channel_id=1, source_target_pairs={{0,30},{2,4},{4,2},{6,8},{8,6},{10,12},{12,10},{14,16},{16,14},{18... | collective-permute-start | bytes 135176 | tf_op jit(solution)/shard_map/ppermute | solution.py:519
  13.2 0.0 collective-permute-start.2
  13.2 3.3 %inner_high.1 = (f32[2048,128]{1,0:T(8,128)S(1)}, f32[2048,128]{1,0:T(8,128)S(1)}, f32[2048,128]{1,0:T(8,128)S(1)}) custom-call(f32[2048,128]{1,0:T(8,128)S(1)} %bitcast.18, f32[2048,128]{1,0:T(8,128)S(1)} %bitcast.22, f32[2048,128]{1,0:T(8,128)S(1)} %bitcast.26, f32[2048,128]{1,0:T(8,128)S(1)} %bitcast.30, f32[128,128]{1,0:T(8,128)S(1)} %get-tuple-element.29.refs_4_, ...), custom_call_target="tpu_custom_call" | custom-call | flops 13107200 | bytes 1048576 | tf_op jit(solution)/shard_map/inner_high/pallas_call | solution.py:522
  16.5 0.0 collective-permute-done.3.recv_b
  16.6 0.0 collective-permute-done.2.recv_a
  16.6 2.8 %border.1 = (f32[2048,128]{1,0:T(8,128)}, f32[2048,128]{1,0:T(8,128)}, f32[2048,128]{1,0:T(8,128)}) custom-call(f32[2048,128]{1,0:T(8,128)S(1)} %get-tuple-element.45.t_in, f32[2048,128]{1,0:T(8,128)S(1)} %get-tuple-element.46.u_in, f32[2048,128]{1,0:T(8,128)S(1)} %get-tuple-element.47.v_in, f32[88,128]{1,0:T(8,128)S(1)} %get-tuple-element.41.refs_13_.send_a, ...), custom_call_target="tpu_custom_call" | custom-call | tf_op jit(solution)/shard_map/border/pallas_call | solution.py:534
  (2 shorter events, 0.0 us)
Async XLA Ops:
  0.6 5.7 %copy-start = (f32[16,128,128]{2,1,0:T(8,128)S(1)}, f32[16,128,128]{2,1,0:T(8,128)}, u32[]{:S(2)}) copy-start(f32[16,128,128]{2,1,0:T(8,128)} %param.7) | copy-start | bytes 3145732
  0.6 5.7 %copy-start.1 = (f32[16,128,128]{2,1,0:T(8,128)S(1)}, f32[16,128,128]{2,1,0:T(8,128)}, u32[]{:S(2)}) copy-start(f32[16,128,128]{2,1,0:T(8,128)} %param.8) | copy-start | bytes 3145732
  0.7 5.7 %copy-start.2 = (f32[16,128,128]{2,1,0:T(8,128)S(1)}, f32[16,128,128]{2,1,0:T(8,128)}, u32[]{:S(2)}) copy-start(f32[16,128,128]{2,1,0:T(8,128)} %param.9) | copy-start | bytes 3145732
  0.7 5.7 %copy-start.3 = (f32[16,128,128]{2,1,0:T(8,128)S(1)}, f32[16,128,128]{2,1,0:T(8,128)}, u32[]{:S(2)}) copy-start(f32[16,128,128]{2,1,0:T(8,128)} %param.10) | copy-start | bytes 3145732
  0.7 5.7 %copy-start.4 = (s32[128,128]{1,0:T(8,128)S(1)}, s32[128,128]{1,0:T(8,128)}, u32[]{:S(2)}) copy-start(s32[128,128]{1,0:T(8,128)} %water.1) | copy-start | bytes 196612
  0.7 5.7 %copy-start.5 = (s32[128,128]{1,0:T(8,128)S(1)}, s32[128,128]{1,0:T(8,128)}, u32[]{:S(2)}) copy-start(s32[128,128]{1,0:T(8,128)} %strata.1) | copy-start | bytes 196612
  2.1 7.9 %collective-permute-start.1 = (f32[88,128]{1,0:T(8,128)S(1)}, f32[88,128]{1,0:T(8,128)S(1)}, u32[]{:S(2)}, u32[]{:S(2)}) collective-permute-start(f32[88,128]{1,0:T(8,128)S(1)} %bitcast.33), channel_id=1, source_target_pairs={{0,1},{1,0},{2,3},{3,2},{4,5},{5,4},{6,7},{7,6},{8,9},{9,8},{10,11... | collective-permute-start | bytes 135176 | tf_op jit(solution)/shard_map/ppermute | solution.py:482
  2.1 7.8 %collective-permute-start = (f32[88,128]{1,0:T(8,128)S(1)}, f32[88,128]{1,0:T(8,128)S(1)}, u32[]{:S(2)}, u32[]{:S(2)}) collective-permute-start(f32[88,128]{1,0:T(8,128)S(1)} %bitcast.35), channel_id=1, source_target_pairs={{1,31},{0,2},{3,29},{2,0},{5,27},{4,6},{7,25},{6,4},{9,23},{8,10},... | collective-permute-start | bytes 135176 | tf_op jit(solution)/shard_map/ppermute | solution.py:483
  10.0 6.5 %collective-permute-start.3 = (f32[88,128]{1,0:T(8,128)S(1)}, f32[88,128]{1,0:T(8,128)S(1)}, u32[]{:S(2)}, u32[]{:S(2)}) collective-permute-start(f32[88,128]{1,0:T(8,128)S(1)} %get-tuple-element.48.send_b), channel_id=1, source_target_pairs={{0,30},{2,4},{4,2},{6,8},{8,6},{10,12},{12,10},{14,16},{16,14},{18... | collective-permute-start | bytes 135176 | tf_op jit(solution)/shard_map/ppermute | solution.py:519
  13.2 3.3 %collective-permute-start.2 = (f32[88,128]{1,0:T(8,128)S(1)}, f32[88,128]{1,0:T(8,128)S(1)}, u32[]{:S(2)}, u32[]{:S(2)}) collective-permute-start(f32[88,128]{1,0:T(8,128)S(1)} %get-tuple-element.41.refs_13_.send_a), channel_id=1, source_target_pairs={{0,2},{2,0},{4,6},{6,4},{8,10},{10,8},{12,14},{14,12},{16,18},{18,... | collective-permute-start | bytes 135176 | tf_op jit(solution)/shard_map/ppermute | solution.py:520

commit v12 on v10

--- a/solution.py
+++ b/solution.py
@@ -110,15 +110,15 @@
         gathered[0, at, :] = jnp.zeros((STRIP, cols), F32)
         gathered[1, at, :] = jnp.zeros((STRIP, cols), F32)
 
-    @pl.loop(0, levels // CHUNK)
+    @pl.loop(0, levels // (2 * CHUNK))
     def one_piece(part):
-        begin = pl.multiple_of(part * CHUNK * rows, rows)
+        begin = pl.multiple_of(part * 2 * CHUNK * rows, rows)
         for f, full in enumerate((t, kd, u, v)):
             for r in range(0, rows, STRIP):
                 acc = gathered[f // 2, pl.ds(r, STRIP), :]
-                for n in range(CHUNK):
+                for n in range(2 * CHUNK):
                     x = jnp.where(edge, full[pl.ds(begin + n * rows + r, STRIP), :], 0.0)
-                    to = 8 * (part * CHUNK + n) + 4 * (f % 2) + 2
+                    to = 8 * (part * 2 * CHUNK + n) + 4 * (f % 2) + 2
                     acc = acc + pltpu.roll(x, to & (cols - 1), 1)
                 gathered[f // 2, pl.ds(r, STRIP), :] = acc
 

time: 19.5 us -> 19.5 us (level)
  transfers between devices with their start and end apart: 4 -> 4, of which waited for: 0 -> 0; matrix products, arithmetic and copies ran while one was open for 0% -> 0% of each run, Pallas kernels for 36% -> 35%
where the time goes in v12:
time: 19.5 us; the launch traced here: 19.3 us
  Pallas kernels  11 us (56%)
  starting transfers between devices  7.54 us (39%)
  between operations  0.78 us (4%)
    ppermute x1, starting transfers between devices, on_device(): rim_b = lax.ppermute(lat_b, ('lon', 'lat'), cross)  4.24 us
    pallas_call x1, Pallas kernels, on_device(): pl.pallas_call(functools.partial(high_kernel, levels, STRIP), out_shape=[...  3.33 us
    ppermute x1, starting transfers between devices, on_device(): recv_b = lax.ppermute(send_b, 'lon', lon_cross)  3.23 us
    pallas_call x1, Pallas kernels, on_device(): pl.pallas_call(functools.partial(border_kernel, levels), out_shape=[jax.S...  2.76 us
    pallas_call x1, Pallas kernels, on_device(): pl.pallas_call(functools.partial(low_kernel, levels, STRIP), out_shape=[w...  2.11 us
    pallas_call x1, Pallas kernels, on_device(): pl.pallas_call(functools.partial(rows_kernel, levels), out_shape=[pltpu.V...  1.36 us
    pallas_call x1, Pallas kernels, on_device(): pl.pallas_call(functools.partial(pack_kernel, levels), out_shape=[pltpu.V...  1.33 us
  transfers between devices with their start and end apart: 4, of which 0 were waited for; matrix products, arithmetic and copies ran while one was open for 0% of the time, Pallas kernels for 35%

profile of v12, /device:TPU:2, one launch (start us, length us, event | category | flops | bytes accessed | tf_op | source)
XLA Modules:
  0.0 19.3 jit_solution(4506684843822990959)
XLA Ops:
  0.6 0.0 copy-start
  0.6 0.0 copy-start.1
  0.7 0.0 copy-start.2
  0.7 0.0 copy-start.3
  0.7 0.0 copy-start.4
  0.7 0.0 copy-start.5
  0.7 1.4 %rows.1 = (f32[88,1,128]{2,1,0:T(1,128)S(1)}, f32[88,1,128]{2,1,0:T(1,128)S(1)}, f32[128,128]{1,0:T(8,128)S(1)}, f32[128,128]{1,0:T(8,128)S(1)}) custom-call(f32[16,128,1,128]{3,2,1,0:T(1,128)} %bitcast.15, f32[16,128,1,128]{3,2,1,0:T(1,128)} %bitcast.19, f32[16,128,1,128]{3,2,1,0:T(1,128)} %bitcast.23, f32[16,128,1,128]{3,2,1,0:T(1,128)} %bitcast.27, ...), custom_call_target="tpu_custom_call" | custom-call | tf_op jit(solution)/shard_map/rows/pallas_call | solution.py:459
  2.1 0.1 collective-permute-start.1
  2.1 4.2 %collective-permute-start = (f32[88,128]{1,0:T(8,128)S(1)}, f32[88,128]{1,0:T(8,128)S(1)}, u32[]{:S(2)}, u32[]{:S(2)}) collective-permute-start(f32[88,128]{1,0:T(8,128)S(1)} %bitcast.35), channel_id=1, source_target_pairs={{1,31},{0,2},{3,29},{2,0},{5,27},{4,6},{7,25},{6,4},{9,23},{8,10},... | collective-permute-start | bytes 135176 | tf_op jit(solution)/shard_map/ppermute | solution.py:483
  6.4 0.0 copy-done
  6.4 0.0 copy-done.1
  6.4 0.0 copy-done.2
  6.4 0.0 copy-done.3
  6.4 1.3 %pack.1 = (f32[88,128]{1,0:T(8,128)S(1)}, f32[88,128]{1,0:T(8,128)S(1)}, f32[128,128]{1,0:T(8,128)S(1)}, f32[8,128]{1,0:T(8,128)S(1)}) custom-call(f32[2048,128]{1,0:T(8,128)S(1)} %bitcast.16, f32[2048,128]{1,0:T(8,128)S(1)} %bitcast.20, f32[2048,128]{1,0:T(8,128)S(1)} %bitcast.24, f32[2048,128]{1,0:T(8,128)S(1)} %bitcast.28, s32[128,128]{1,0:T(8,128)S(1)} %copy-done.4, ...), custom_call_target="tpu_custom_call" | custom-call | tf_op jit(solution)/shard_map/pack/pallas_call | solution.py:486
  7.7 2.1 %inner_low.1 = (f32[2048,128]{1,0:T(8,128)S(1)}, f32[2048,128]{1,0:T(8,128)S(1)}, f32[2048,128]{1,0:T(8,128)S(1)}, f32[144,128]{1,0:T(8,128)S(1)}, f32[128,128]{...) custom-call(f32[2048,128]{1,0:T(8,128)S(1)} %bitcast.17, ...), custom_call_target="tpu_custom_call" | custom-call | flops 13107200 | bytes 1048576 | tf_op jit(solution)/shard_map/inner_low/pallas_call | solution.py:499
  9.9 0.0 collective-permute-done.1.rim_a
  9.9 0.0 collective-permute-done.rim_b
  9.9 0.1 corners.1
  10.0 3.2 %collective-permute-start.3 = (f32[88,128]{1,0:T(8,128)S(1)}, f32[88,128]{1,0:T(8,128)S(1)}, u32[]{:S(2)}, u32[]{:S(2)}) collective-permute-start(f32[88,128]{1,0:T(8,128)S(1)} %get-tuple-element.48.send_b), channel_id=1, source_target_pairs={{0,30},{2,4},{4,2},{6,8},{8,6},{10,12},{12,10},{14,16},{16,14},{18... | collective-permute-start | bytes 135176 | tf_op jit(solution)/shard_map/ppermute | solution.py:519
  13.2 0.0 collective-permute-start.2
  13.2 3.3 %inner_high.1 = (f32[2048,128]{1,0:T(8,128)S(1)}, f32[2048,128]{1,0:T(8,128)S(1)}, f32[2048,128]{1,0:T(8,128)S(1)}) custom-call(f32[2048,128]{1,0:T(8,128)S(1)} %bitcast.18, f32[2048,128]{1,0:T(8,128)S(1)} %bitcast.22, f32[2048,128]{1,0:T(8,128)S(1)} %bitcast.26, f32[2048,128]{1,0:T(8,128)S(1)} %bitcast.30, f32[128,128]{1,0:T(8,128)S(1)} %get-tuple-element.29.refs_4_, ...), custom_call_target="tpu_custom_call" | custom-call | flops 13107200 | bytes 1048576 | tf_op jit(solution)/shard_map/inner_high/pallas_call | solution.py:522
  16.6 0.0 collective-permute-done.3.recv_b
  16.6 0.0 collective-permute-done.2.recv_a
  16.6 2.8 %border.1 = (f32[2048,128]{1,0:T(8,128)}, f32[2048,128]{1,0:T(8,128)}, f32[2048,128]{1,0:T(8,128)}) custom-call(f32[2048,128]{1,0:T(8,128)S(1)} %get-tuple-element.45.t_in, f32[2048,128]{1,0:T(8,128)S(1)} %get-tuple-element.46.u_in, f32[2048,128]{1,0:T(8,128)S(1)} %get-tuple-element.47.v_in, f32[88,128]{1,0:T(8,128)S(1)} %get-tuple-element.41.refs_13_.send_a, ...), custom_call_target="tpu_custom_call" | custom-call | tf_op jit(solution)/shard_map/border/pallas_call | solution.py:534
  (2 shorter events, 0.0 us)
Async XLA Ops:
  0.6 5.7 %copy-start = (f32[16,128,128]{2,1,0:T(8,128)S(1)}, f32[16,128,128]{2,1,0:T(8,128)}, u32[]{:S(2)}) copy-start(f32[16,128,128]{2,1,0:T(8,128)} %param.7) | copy-start | bytes 3145732
  0.6 5.7 %copy-start.1 = (f32[16,128,128]{2,1,0:T(8,128)S(1)}, f32[16,128,128]{2,1,0:T(8,128)}, u32[]{:S(2)}) copy-start(f32[16,128,128]{2,1,0:T(8,128)} %param.8) | copy-start | bytes 3145732
  0.7 5.7 %copy-start.2 = (f32[16,128,128]{2,1,0:T(8,128)S(1)}, f32[16,128,128]{2,1,0:T(8,128)}, u32[]{:S(2)}) copy-start(f32[16,128,128]{2,1,0:T(8,128)} %param.9) | copy-start | bytes 3145732
  0.7 5.7 %copy-start.3 = (f32[16,128,128]{2,1,0:T(8,128)S(1)}, f32[16,128,128]{2,1,0:T(8,128)}, u32[]{:S(2)}) copy-start(f32[16,128,128]{2,1,0:T(8,128)} %param.10) | copy-start | bytes 3145732
  0.7 5.7 %copy-start.4 = (s32[128,128]{1,0:T(8,128)S(1)}, s32[128,128]{1,0:T(8,128)}, u32[]{:S(2)}) copy-start(s32[128,128]{1,0:T(8,128)} %water.1) | copy-start | bytes 196612
  0.7 5.7 %copy-start.5 = (s32[128,128]{1,0:T(8,128)S(1)}, s32[128,128]{1,0:T(8,128)}, u32[]{:S(2)}) copy-start(s32[128,128]{1,0:T(8,128)} %strata.1) | copy-start | bytes 196612
  2.1 7.8 %collective-permute-start.1 = (f32[88,128]{1,0:T(8,128)S(1)}, f32[88,128]{1,0:T(8,128)S(1)}, u32[]{:S(2)}, u32[]{:S(2)}) collective-permute-start(f32[88,128]{1,0:T(8,128)S(1)} %bitcast.33), channel_id=1, source_target_pairs={{0,1},{1,0},{2,3},{3,2},{4,5},{5,4},{6,7},{7,6},{8,9},{9,8},{10,11... | collective-permute-start | bytes 135176 | tf_op jit(solution)/shard_map/ppermute | solution.py:482
  2.1 7.7 %collective-permute-start = (f32[88,128]{1,0:T(8,128)S(1)}, f32[88,128]{1,0:T(8,128)S(1)}, u32[]{:S(2)}, u32[]{:S(2)}) collective-permute-start(f32[88,128]{1,0:T(8,128)S(1)} %bitcast.35), channel_id=1, source_target_pairs={{1,31},{0,2},{3,29},{2,0},{5,27},{4,6},{7,25},{6,4},{9,23},{8,10},... | collective-permute-start | bytes 135176 | tf_op jit(solution)/shard_map/ppermute | solution.py:483
  10.0 6.6 %collective-permute-start.3 = (f32[88,128]{1,0:T(8,128)S(1)}, f32[88,128]{1,0:T(8,128)S(1)}, u32[]{:S(2)}, u32[]{:S(2)}) collective-permute-start(f32[88,128]{1,0:T(8,128)S(1)} %get-tuple-element.48.send_b), channel_id=1, source_target_pairs={{0,30},{2,4},{4,2},{6,8},{8,6},{10,12},{12,10},{14,16},{16,14},{18... | collective-permute-start | bytes 135176 | tf_op jit(solution)/shard_map/ppermute | solution.py:519
  13.2 3.3 %collective-permute-start.2 = (f32[88,128]{1,0:T(8,128)S(1)}, f32[88,128]{1,0:T(8,128)S(1)}, u32[]{:S(2)}, u32[]{:S(2)}) collective-permute-start(f32[88,128]{1,0:T(8,128)S(1)} %get-tuple-element.41.refs_13_.send_a), channel_id=1, source_target_pairs={{0,2},{2,0},{4,6},{6,4},{8,10},{10,8},{12,14},{14,12},{16,18},{18,... | collective-permute-start | bytes 135176 | tf_op jit(solution)/shard_map/ppermute | solution.py:520
